TPU v7x, 128 devices: a whole 4x4x4 slice. The times are simulated.
128 devices in a mesh: dp: 32 (over y, z, core), mp: 4 (over x).
Axes of the slice: x: 4, y: 4, z: 4, core: 2. Of those that a mesh axis runs over, the one named last changes fastest.
Arguments:
- patches: bfloat16 [32, 1024, 768], P('dp'), may hold values from -6 to 6
- image_ids: int32 [32, 1024], P('dp'), may hold values from 0 to 7, as said below
- keep: int32 [32, 1024], P('dp'), may hold values from 0 to 1, as said below
- labels: int32 [32, 8], P('dp'), may hold values from 0 to 999
- owners: int32 [96], replicated, may hold values from 0 to 95, as said below
- soap_weight: float32 [384, 36864], P(('dp', 'mp'))
- soap_first: float32 [384, 36864], P(('dp', 'mp')), may hold values from -3.8146973e-06 to 3.8146973e-06
- soap_second: float32 [384, 36864], P(('dp', 'mp')), may hold values from 3.4163574e-13 to 1.353651e-12
- stat_left: float32 [384, 36864], P(('dp', 'mp')), as said below
- stat_right: float32 [384, 36864], P(('dp', 'mp')), as said below
- basis_left: float32 [384, 36864], P(('dp', 'mp')), as said below
- basis_right: float32 [384, 36864], P(('dp', 'mp')), as said below
- embed_weight: float32 [768, 768], P(None, 'mp'), may hold values from -0.21875 to 0.21875
- embed_first: float32 [768, 768], P(None, 'mp'), may hold values from -3.8146973e-06 to 3.8146973e-06
- embed_second: float32 [768, 768], P(None, 'mp'), may hold values from 3.4163574e-13 to 1.353651e-12
- head_weight: float32 [768, 1000], P('mp'), may hold values from -0.625 to 0.625
- head_first: float32 [768, 1000], P('mp'), may hold values from -3.8146973e-06 to 3.8146973e-06
- head_second: float32 [768, 1000], P('mp'), may hold values from 3.4163574e-13 to 1.353651e-12
- vectors: float32 [5096], replicated
- vector_first: float32 [5096], replicated, may hold values from -3.8146973e-05 to 3.8146973e-05
- vector_second: float32 [5096], replicated, may hold values from 3.416357e-11 to 1.353651e-10
Outputs:
- loss_sum: float32 [], replicated
- image_count: float32 [], replicated
- grad_norm: float32 [], replicated
- soap_weight_new: float32 [384, 36864], P(('dp', 'mp'))
- soap_first_new: float32 [384, 36864], P(('dp', 'mp'))
- soap_second_new: float32 [384, 36864], P(('dp', 'mp'))
- stat_left_new: float32 [384, 36864], P(('dp', 'mp'))
- stat_right_new: float32 [384, 36864], P(('dp', 'mp'))
- basis_left_new: float32 [384, 36864], P(('dp', 'mp'))
- basis_right_new: float32 [384, 36864], P(('dp', 'mp'))
- soap_weight_low: bfloat16 [384, 36864], P(('dp', 'mp'))
- embed_new: float32 [768, 768], P(None, 'mp')
- embed_first_new: float32 [768, 768], P(None, 'mp')
- embed_second_new: float32 [768, 768], P(None, 'mp')
- head_new: float32 [768, 1000], P('mp')
- head_first_new: float32 [768, 1000], P('mp')
- head_second_new: float32 [768, 1000], P('mp')
- vectors_new: float32 [5096], replicated
- vector_first_new: float32 [5096], replicated
- vector_second_new: float32 [5096], replicated
Inputs may be any that keep to these rules, and one draw needn't show every extreme that they name: `image_ids`: images are contiguous runs of positions numbered 0, 1, 2 ... in order, every position belongs to one; a sequence holds up to 8 images and the last sequence holds exactly 8. `keep`: the first position of every image is kept. `owners`: A permutation of the block numbers. `stat_left`: each block is symmetric positive definite. `stat_right`: each block is symmetric positive definite. `basis_left`: each block is an orthogonal matrix. `basis_right`: each block is an orthogonal matrix.
All inputs are finite; a program needn't handle non-finite values.
Results may differ from a plain program's by a relative error of at most 0.014.
The roundings to bfloat16 on the way count: a program that leaves them out, or rounds other values in their place, can miss the bound.
Values may be sent and summed in bfloat16 or wider, within the bound.
No kernel may reach another device: no remote copies, remote signals or barrier semaphores. Data moves between devices by JAX's collectives and lax.ppermute only.
A program may use at most 256 MiB of HBM per device.

v0:
```python
from functools import partial

import jax
import jax.numpy as jnp
from jax import lax
from jax.sharding import PartitionSpec as P

D = 768
FF = 3072
HD = 64
CLASSES = 1000
LAYERS = 2
IMGS = 8
STEP = 10


first_decay = 0.9
second_decay = 0.95
weight_decay = 0.05
matrix_rate = 0.03
vector_rate = 0.3
clip_limit = 0.01
adam_epsilon = 1e-08
norm_epsilon = 1e-06
masked_score = -1e30
highest = lax.Precision.HIGHEST


def layer_norm(values, gain_row):
    centered = values - jnp.mean(values, -1, keepdims=True)
    return (
        centered
        * lax.rsqrt(jnp.mean(centered * centered, -1, keepdims=True) + norm_epsilon)
        * gain_row
    )


def matmul(left, right):
    return jnp.dot(left, right, preferred_element_type=jnp.float32)


def to_blocks(w_qkv, w_out, w_up, w_down):
    layers, breadth, triple, tile_size = w_qkv.shape
    row_tiles = breadth // tile_size
    hid_tiles = w_up.shape[2] // tile_size
    qkv_tiles = (
        w_qkv.reshape(layers, row_tiles, tile_size, triple, tile_size)
        .transpose(0, 1, 3, 2, 4)
        .reshape(layers, row_tiles * triple, tile_size, tile_size)
    )
    out_tiles = w_out.reshape(layers, tile_size, row_tiles, tile_size).transpose(0, 2, 1, 3)
    up_tiles = (
        w_up.reshape(layers, row_tiles, tile_size, hid_tiles, tile_size)
        .transpose(0, 1, 3, 2, 4)
        .reshape(layers, row_tiles * hid_tiles, tile_size, tile_size)
    )
    down_tiles = (
        w_down.reshape(layers, hid_tiles, tile_size, row_tiles, tile_size)
        .transpose(0, 1, 3, 2, 4)
        .reshape(layers, hid_tiles * row_tiles, tile_size, tile_size)
    )
    joined = jnp.concatenate([qkv_tiles, out_tiles, up_tiles, down_tiles], axis=1)
    return joined.reshape(layers * joined.shape[1], tile_size, tile_size)


def from_blocks(stack, row_tiles, hid_tiles):
    tile_size = stack.shape[-1]
    per_layer = stack.reshape(LAYERS, -1, tile_size, tile_size)
    cut_one = 3 * row_tiles
    cut_two = cut_one + row_tiles
    cut_three = cut_two + row_tiles * hid_tiles
    w_qkv = (
        per_layer[:, :cut_one]
        .reshape(LAYERS, row_tiles, 3, tile_size, tile_size)
        .transpose(0, 1, 3, 2, 4)
        .reshape(LAYERS, row_tiles * tile_size, 3, tile_size)
    )
    w_out = (
        per_layer[:, cut_one:cut_two]
        .transpose(0, 2, 1, 3)
        .reshape(LAYERS, tile_size, row_tiles * tile_size)
    )
    w_up = (
        per_layer[:, cut_two:cut_three]
        .reshape(LAYERS, row_tiles, hid_tiles, tile_size, tile_size)
        .transpose(0, 1, 3, 2, 4)
        .reshape(LAYERS, row_tiles * tile_size, hid_tiles * tile_size)
    )
    w_down = (
        per_layer[:, cut_three:]
        .reshape(LAYERS, hid_tiles, row_tiles, tile_size, tile_size)
        .transpose(0, 1, 3, 2, 4)
        .reshape(LAYERS, hid_tiles * tile_size, row_tiles * tile_size)
    )
    return (w_qkv, w_out, w_up, w_down)


def rotate(matrix, left_basis, right_basis):
    return jnp.einsum("nji,njk,nkl->nil", left_basis, matrix, right_basis, precision=highest)


def unrotate(matrix, left_basis, right_basis):
    return jnp.einsum("nij,njk,nlk->nil", left_basis, matrix, right_basis, precision=highest)


def power_step(statistic, basis_now):
    turned = jnp.einsum("nij,njk->nik", statistic, basis_now, precision=highest)
    gram_mat = jnp.einsum("nji,njk->nik", turned, turned, precision=highest)
    factor = jnp.linalg.cholesky(gram_mat)
    solved = jax.vmap(
        lambda lower_tri, right_side: jax.scipy.linalg.solve_triangular(
            lower_tri, right_side, lower=True
        )
    )(factor, jnp.swapaxes(turned, 1, 2))
    return jnp.swapaxes(solved, 1, 2)


def soap_update(master, gradient, first, second, stat_l, stat_r, left_basis, right_basis):
    bias_one = 1.0 - first_decay**STEP
    bias_two = 1.0 - second_decay**STEP
    first_new = first_decay * first + (1.0 - first_decay) * gradient
    turned = rotate(gradient, left_basis, right_basis)
    second_new = second_decay * second + (1.0 - second_decay) * turned * turned
    scaled = (
        rotate(first_new, left_basis, right_basis)
        / bias_one
        / (jnp.sqrt(second_new / bias_two) + adam_epsilon)
    )
    master_new = master * (1.0 - matrix_rate * weight_decay) - matrix_rate * unrotate(
        scaled, left_basis, right_basis
    )
    stat_l_new = second_decay * stat_l + (1.0 - second_decay) * jnp.einsum(
        "nij,nkj->nik", gradient, gradient, precision=highest
    )
    stat_r_new = second_decay * stat_r + (1.0 - second_decay) * jnp.einsum(
        "nji,njk->nik", gradient, gradient, precision=highest
    )
    return (
        master_new,
        first_new,
        second_new,
        stat_l_new,
        stat_r_new,
        power_step(stat_l_new, left_basis),
        power_step(stat_r_new, right_basis),
        master_new.astype(jnp.bfloat16),
    )


def adamw(master, gradient, first, second, rate, decay):
    first_new = first_decay * first + (1.0 - first_decay) * gradient
    second_new = second_decay * second + (1.0 - second_decay) * gradient * gradient
    step_dir = (
        first_new
        / (1.0 - first_decay**STEP)
        / (jnp.sqrt(second_new / (1.0 - second_decay**STEP)) + adam_epsilon)
    )
    return (master * (1.0 - rate * decay) - rate * step_dir, first_new, second_new)


def branch_sum(partial_sum):
    return lax.psum(partial_sum, "mp")


def by_sequence(array, seq_count, seq_len):
    return array.reshape(seq_count, seq_len, -1, HD)


def masked_scores(queries, keys_low, allowed):
    scores = jnp.einsum(
        "qhd,khd->hqk", queries, keys_low, preferred_element_type=jnp.float32
    ) * HD ** (-0.5)
    return jnp.where(allowed[None], scores, masked_score)


def attend_forward(bundle):
    queries, keys_low, values, allowed = bundle
    scores = masked_scores(queries, keys_low, allowed)
    row_max = jnp.max(scores, -1, keepdims=True)
    weights = jnp.exp(scores - row_max)
    row_sum = jnp.sum(weights, -1, keepdims=True)
    probs_low = (weights / row_sum).astype(jnp.bfloat16)
    output = jnp.einsum(
        "hqk,khd->qhd", probs_low, values, preferred_element_type=jnp.float32
    ).astype(jnp.bfloat16)
    return (output, (row_max + jnp.log(row_sum))[..., 0])


def attend_backward(bundle):
    queries, keys_low, values, log_total, grad_out, allowed = bundle
    weights = jnp.exp(masked_scores(queries, keys_low, allowed) - log_total[..., None])
    grad_values = jnp.einsum(
        "hqk,qhd->khd", weights.astype(jnp.bfloat16), grad_out, preferred_element_type=jnp.float32
    )
    grad_weights = jnp.einsum("qhd,khd->hqk", grad_out, values, preferred_element_type=jnp.float32)
    inner = jnp.sum(weights * grad_weights, -1, keepdims=True)
    grad_scores = (weights * (grad_weights - inner)).astype(jnp.bfloat16)
    grad_queries = jnp.einsum(
        "hqk,khd->qhd", grad_scores, keys_low, preferred_element_type=jnp.float32
    ) * HD ** (-0.5)
    grad_keys = jnp.einsum(
        "hqk,qhd->khd", grad_scores, queries, preferred_element_type=jnp.float32
    ) * HD ** (-0.5)
    return (grad_queries, grad_keys, grad_values)


def layer_forward(resid, weights, gain_vecs, allowed):
    w_qkv, w_out, w_up, w_down = weights
    gain_one, gain_two, gain_query, gain_key = gain_vecs
    seq_count, seq_len = (allowed.shape[0], allowed.shape[1])
    normed = layer_norm(resid, gain_one).astype(jnp.bfloat16)
    row_count = normed.shape[0]
    projected = jnp.einsum("rd,dcs->rcs", normed, w_qkv, preferred_element_type=jnp.float32)
    head_count = projected.shape[2] // HD
    query_pre = projected[:, 0].reshape(row_count, head_count, HD)
    key_pre = projected[:, 1].reshape(row_count, head_count, HD)
    queries = layer_norm(query_pre, gain_query).astype(jnp.bfloat16)
    keys_low = layer_norm(key_pre, gain_key).astype(jnp.bfloat16)
    values = projected[:, 2].reshape(row_count, head_count, HD).astype(jnp.bfloat16)
    attended, log_total = lax.map(
        attend_forward,
        (
            by_sequence(queries, seq_count, seq_len),
            by_sequence(keys_low, seq_count, seq_len),
            by_sequence(values, seq_count, seq_len),
            allowed,
        ),
    )
    attended = attended.reshape(row_count, head_count * HD)
    resid_mid = resid + branch_sum(matmul(attended, w_out))
    normed_two = layer_norm(resid_mid, gain_two).astype(jnp.bfloat16)
    expanded = matmul(normed_two, w_up)
    activated = jax.nn.gelu(expanded, approximate=False).astype(jnp.bfloat16)
    resid_out = resid_mid + branch_sum(matmul(activated, w_down))
    return (
        resid_out,
        (
            resid,
            normed,
            query_pre,
            key_pre,
            queries,
            keys_low,
            values,
            log_total,
            attended,
            resid_mid,
            normed_two,
            expanded,
            activated,
        ),
    )


def layer_backward(grad_out, saved, weights, gain_vecs, allowed):
    (
        resid,
        normed,
        query_pre,
        key_pre,
        queries,
        keys_low,
        values,
        log_total,
        attended,
        resid_mid,
        normed_two,
        expanded,
        activated,
    ) = saved
    w_qkv, w_out, w_up, w_down = weights
    gain_one, gain_two, gain_query, gain_key = gain_vecs
    row_count = normed.shape[0]
    seq_count, seq_len = (allowed.shape[0], allowed.shape[1])
    head_count = queries.shape[1]
    grad_low = grad_out.astype(jnp.bfloat16)
    grad_down = matmul(activated.T, grad_low)
    gelu_value, gelu_back = jax.vjp(partial(jax.nn.gelu, approximate=False), expanded)
    grad_expanded = gelu_back(matmul(grad_low, w_down.T))[0].astype(jnp.bfloat16)
    grad_up = matmul(normed_two.T, grad_expanded)
    grad_normed_two = branch_sum(matmul(grad_expanded, w_up.T))
    second_value, second_back = jax.vjp(layer_norm, resid_mid, gain_two)
    grad_mid_part, grad_gain_two = second_back(grad_normed_two)
    grad_mid = grad_out + grad_mid_part
    grad_mid_low = grad_mid.astype(jnp.bfloat16)
    grad_w_out = matmul(attended.T, grad_mid_low)
    grad_attended = matmul(grad_mid_low, w_out.T).astype(jnp.bfloat16)
    grad_query, grad_key, grad_value = lax.map(
        attend_backward,
        (
            by_sequence(queries, seq_count, seq_len),
            by_sequence(keys_low, seq_count, seq_len),
            by_sequence(values, seq_count, seq_len),
            log_total,
            by_sequence(grad_attended, seq_count, seq_len),
            allowed,
        ),
    )
    query_value, query_back = jax.vjp(layer_norm, query_pre, gain_query)
    grad_query_pre, grad_gain_query = query_back(grad_query.reshape(row_count, head_count, HD))
    key_value, key_back = jax.vjp(layer_norm, key_pre, gain_key)
    grad_key_pre, grad_gain_key = key_back(grad_key.reshape(row_count, head_count, HD))
    grad_proj = jnp.stack(
        [
            grad_query_pre.reshape(row_count, -1),
            grad_key_pre.reshape(row_count, -1),
            grad_value.reshape(row_count, -1),
        ],
        axis=1,
    ).astype(jnp.bfloat16)
    grad_w_qkv = jnp.einsum("rd,rcs->dcs", normed, grad_proj, preferred_element_type=jnp.float32)
    grad_normed = branch_sum(
        jnp.einsum("rcs,dcs->rd", grad_proj, w_qkv, preferred_element_type=jnp.float32)
    )
    first_value, first_back = jax.vjp(layer_norm, resid, gain_one)
    grad_in_part, grad_gain_one = first_back(grad_normed)
    return (
        grad_mid + grad_in_part,
        (grad_w_qkv, grad_w_out, grad_up, grad_down),
        (grad_gain_one, grad_gain_two, jnp.stack([grad_gain_query, grad_gain_key])),
    )


def shards(
    patches,
    image_ids,
    keep,
    labels,
    owners,
    soap_weight,
    soap_first,
    soap_second,
    stat_left,
    stat_right,
    basis_left,
    basis_right,
    embed_weight,
    embed_first,
    embed_second,
    head_weight,
    head_first,
    head_second,
    vectors,
    vector_first,
    vector_second,
):
    seq_count, seq_len, patch_dim = patches.shape
    slot_count = soap_weight.shape[0]
    tile_size = D // lax.axis_size("mp")
    row_tiles = D // tile_size
    hid_tiles = FF // D

    def tiled(flat_rows):
        return flat_rows.reshape(flat_rows.shape[0], tile_size, tile_size)

    mp_index = lax.axis_index("mp")
    stacked = lax.all_gather(soap_weight.astype(jnp.bfloat16), "dp", axis=0, tiled=True)
    w_qkv, w_out, w_up, w_down = from_blocks(tiled(stacked)[owners], row_tiles, hid_tiles)
    embed_low = embed_weight.astype(jnp.bfloat16)
    head_low = head_weight.astype(jnp.bfloat16)
    split_one = (2 * LAYERS + 1) * D
    gain_rows = vectors[:split_one].reshape(2 * LAYERS + 1, D)
    head_gains = vectors[split_one : split_one + 2 * LAYERS * HD].reshape(LAYERS, 2, HD)
    class_bias = vectors[vectors.shape[0] - CLASSES :]
    allowed = (image_ids[:, :, None] == image_ids[:, None, :]) & (keep[:, None, :] == 1)
    member = (
        (image_ids[:, :, None] == jnp.arange(IMGS)[None, None, :]) & (keep[:, :, None] == 1)
    ).astype(jnp.float32)
    counts = jnp.sum(member, axis=1)
    present = (counts > 0).astype(jnp.float32).reshape(-1)
    local_count = jnp.sum(present)
    tokens = patches.reshape(seq_count * seq_len, patch_dim)
    resid = lax.all_gather(
        matmul(tokens, embed_low).astype(jnp.bfloat16), "mp", axis=1, tiled=True
    ).astype(jnp.float32)
    saved_all = []
    for depth in range(LAYERS):
        gain_vecs = (
            gain_rows[2 * depth],
            gain_rows[2 * depth + 1],
            head_gains[depth, 0],
            head_gains[depth, 1],
        )
        resid, saved = layer_forward(
            resid, (w_qkv[depth], w_out[depth], w_up[depth], w_down[depth]), gain_vecs, allowed
        )
        saved_all.append(saved)
    final_value, final_back = jax.vjp(layer_norm, resid, gain_rows[2 * LAYERS])
    divisor = jnp.maximum(counts, 1.0).reshape(-1)
    seq_eye = jnp.eye(seq_count, dtype=jnp.float32)
    pool_table = (member[:, :, None, :] * seq_eye[:, None, :, None]).reshape(
        seq_count * seq_len, seq_count * IMGS
    )

    def pool(final_rows):
        return jnp.dot(pool_table.T, final_rows, precision=highest) / divisor[:, None]

    pooled, pool_back = jax.vjp(pool, final_value)
    pooled_low = pooled.astype(jnp.bfloat16)
    col_count = head_weight.shape[0]
    pooled_mine = lax.dynamic_slice_in_dim(pooled_low, mp_index * col_count, col_count, 1)
    logits = lax.psum(matmul(pooled_mine, head_low), "mp") + class_bias
    row_max = jnp.max(logits, -1, keepdims=True)
    exps = jnp.exp(logits - row_max)
    row_sum = jnp.sum(exps, -1, keepdims=True)
    log_norm = row_max[:, 0] + jnp.log(row_sum[:, 0])
    onehot = (jnp.arange(CLASSES)[None, :] == labels.reshape(-1)[:, None]).astype(jnp.float32)
    picked = jnp.sum(onehot * logits, -1)
    local_loss = jnp.sum((log_norm - picked) * present)
    image_total, loss_total = lax.psum((local_count, local_loss), "dp")
    grad_logits = (exps / row_sum - onehot) * present[:, None] / image_total
    grad_bias = jnp.sum(grad_logits, 0)
    grad_logit_low = grad_logits.astype(jnp.bfloat16)
    grad_head = matmul(pooled_mine.T, grad_logit_low)
    grad_pooled = lax.all_gather(matmul(grad_logit_low, head_low.T), "mp", axis=1, tiled=True)
    grad_final = pool_back(grad_pooled)[0]
    grad_resid, grad_gain_final = final_back(grad_final)
    layer_grads = []
    gain_grads = []
    for depth in reversed(range(LAYERS)):
        gain_vecs = (
            gain_rows[2 * depth],
            gain_rows[2 * depth + 1],
            head_gains[depth, 0],
            head_gains[depth, 1],
        )
        grad_resid, matrices, gains_back = layer_backward(
            grad_resid,
            saved_all[depth],
            (w_qkv[depth], w_out[depth], w_up[depth], w_down[depth]),
            gain_vecs,
            allowed,
        )
        layer_grads.insert(0, matrices)
        gain_grads.insert(0, gains_back)
    embed_cols = embed_weight.shape[1]
    grad_input_low = grad_resid.astype(jnp.bfloat16)
    grad_embed = matmul(
        tokens.T, lax.dynamic_slice_in_dim(grad_input_low, mp_index * embed_cols, embed_cols, 1)
    )
    stacked_grads = [jnp.stack([entry[kind] for entry in layer_grads]) for kind in range(4)]
    slotted = to_blocks(*stacked_grads)[jnp.argsort(owners)]
    slotted = slotted.reshape(slotted.shape[0], tile_size * tile_size)
    norm_list = []
    for entry in gain_grads:
        norm_list.extend([entry[0], entry[1]])
    norm_list.append(grad_gain_final)
    norm_grads = jnp.stack(norm_list).reshape(-1)
    head_gain_grads = jnp.stack([entry[2] for entry in gain_grads]).reshape(-1)
    norm_part = norm_grads / lax.axis_size("mp")
    norm_grads, head_gain_grads = lax.psum((norm_part, head_gain_grads), "mp")
    grad_vector = jnp.concatenate([norm_grads, head_gain_grads, grad_bias])
    summed, grad_embed, grad_head, grad_vector = lax.psum(
        (slotted, grad_embed, grad_head, grad_vector), "dp"
    )
    mine = lax.dynamic_slice_in_dim(summed, lax.axis_index("dp") * slot_count, slot_count, 0)
    local_squares = jnp.sum(mine * mine) + (
        jnp.sum(grad_embed * grad_embed) + jnp.sum(grad_head * grad_head)
    ) / lax.axis_size("dp")
    squares = lax.psum(local_squares, ("dp", "mp"))
    grad_norm = jnp.sqrt(squares + jnp.sum(grad_vector * grad_vector))
    factor = clip_limit / jnp.maximum(grad_norm, clip_limit)
    soap_new = soap_update(
        tiled(soap_weight),
        tiled(mine) * factor,
        tiled(soap_first),
        tiled(soap_second),
        tiled(stat_left),
        tiled(stat_right),
        tiled(basis_left),
        tiled(basis_right),
    )
    soap_new = tuple((entry.reshape(slot_count, tile_size * tile_size) for entry in soap_new))
    embed_new = adamw(
        embed_weight, grad_embed * factor, embed_first, embed_second, matrix_rate, weight_decay
    )
    head_new = adamw(
        head_weight, grad_head * factor, head_first, head_second, matrix_rate, weight_decay
    )
    vector_new = adamw(vectors, grad_vector * factor, vector_first, vector_second, vector_rate, 0.0)
    return (
        loss_total,
        image_total,
        grad_norm,
        soap_new[0],
        soap_new[1],
        soap_new[2],
        soap_new[3],
        soap_new[4],
        soap_new[5],
        soap_new[6],
        soap_new[7],
        embed_new[0],
        embed_new[1],
        embed_new[2],
        head_new[0],
        head_new[1],
        head_new[2],
        vector_new[0],
        vector_new[1],
        vector_new[2],
    )


def solution(mesh):
    return jax.shard_map(
        shards,
        mesh=mesh,
        in_specs=(
            P("dp", None, None),
            P("dp", None),
            P("dp", None),
            P("dp", None),
            P(),
            P(("dp", "mp"), None),
            P(("dp", "mp"), None),
            P(("dp", "mp"), None),
            P(("dp", "mp"), None),
            P(("dp", "mp"), None),
            P(("dp", "mp"), None),
            P(("dp", "mp"), None),
            P(None, "mp"),
            P(None, "mp"),
            P(None, "mp"),
            P("mp", None),
            P("mp", None),
            P("mp", None),
            P(),
            P(),
            P(),
        ),
        out_specs=(
            P(),
            P(),
            P(),
            P(("dp", "mp"), None),
            P(("dp", "mp"), None),
            P(("dp", "mp"), None),
            P(("dp", "mp"), None),
            P(("dp", "mp"), None),
            P(("dp", "mp"), None),
            P(("dp", "mp"), None),
            P(("dp", "mp"), None),
            P(None, "mp"),
            P(None, "mp"),
            P(None, "mp"),
            P("mp", None),
            P("mp", None),
            P("mp", None),
            P(),
            P(),
            P(),
        ),
        check_vma=False,
    )
```

profile of v0, /device:TPU:1, one launch (start us, length us, event | category | flops | bytes accessed | tf_op | source)
XLA Modules:
  0.0 1613.8 jit_solution(10627482282690080061)
XLA Ops:
  15.5 25.4 %all-gather.5.cloned.1.call-done = bf16[1024,768]{0,1:T(8,128)(2,1)} async-done(((bf16[1024,192]{0,1:T(8,128)(2,1)}), bf16[1024,768]{0,1:T(8,128)(2,1)}) %all-gather.5.cloned.1.call-update) | async-done | bytes 1572880 | tf_op jit(solution)/shard_map/all_gather | solution.py:373
  44.6 55.3 %all-gather.7.cloned.1.call-done = bf16[32,3,36864]{2,1,0:T(4,128)(2,1)} async-done(((bf16[1,3,36864]{2,1,0:T(4,128)(2,1)}), bf16[32,3,36864]{2,1,0:T(4,128)(2,1)}) %all-gather.7.cloned.1.call-update) | async-done | bytes 7077904 | tf_op jit(solution)/shard_map/all_gather | solution.py:357
  99.9 16.8 %reshape.742 = bf16[96,192,192]{2,1,0:T(8,128)(2,1)} reshape(bf16[32,3,36864]{2,1,0:T(4,128)(2,1)} %all-gather.7.cloned.1.call-done) | data formatting | bytes 14155776 | tf_op jit(solution)/shard_map/reshape | solution.py:354
  116.6 11.1 gather_fusion
  185.9 51.1 %all-reduce.16.cloned.1.call-done = f32[1024,768]{0,1:T(8,128)} async-done(((f32[1024,768]{0,1:T(8,128)}), f32[1024,768]{0,1:T(8,128)}) %all-reduce.16.cloned.1.call-update) | async-done | bytes 3145744 | tf_op jit(solution)/shard_map/psum | solution.py:162
  241.8 9.7 multiply_convert_fusion.5
  262.1 69.3 %all-reduce.18.cloned.1.call-done = f32[1024,768]{0,1:T(8,128)} async-done(((f32[1024,768]{0,1:T(8,128)}), f32[1024,768]{0,1:T(8,128)}) %all-reduce.18.cloned.1.call-update) | async-done | bytes 3145744 | tf_op jit(solution)/shard_map/psum | solution.py:162
  361.9 69.1 %all-reduce.20.cloned.1.call-done = f32[1024,768]{0,1:T(8,128)} async-done(((f32[1024,768]{0,1:T(8,128)}), f32[1024,768]{0,1:T(8,128)}) %all-reduce.20.cloned.1.call-update) | async-done | bytes 3145744 | tf_op jit(solution)/shard_map/psum | solution.py:162
  437.0 9.7 multiply_convert_fusion.2
  452.6 63.7 %psum.132 = f32[]{:T(128)} all-reduce(f32[]{:T(128)} %get-tuple-element.255), channel_id=1, replica_groups=mesh['dp'=32,'mp'=4] {'dp'}, use_global_device_ids=true, to_apply=%region_34.35 | all-reduce | flops 1 | bytes 8 | tf_op jit(solution)/shard_map/psum | solution.py:410
  517.1 9.9 all-reduce.22.cloned.1.call-done
  534.5 11.4 psum.130
  547.2 9.0 all-gather.1
  576.2 79.0 %all-reduce.24.cloned.1.call-done = f32[1024,768]{0,1:T(8,128)} async-done(((f32[1024,768]{0,1:T(8,128)}), f32[1024,768]{0,1:T(8,128)}) %all-reduce.24.cloned.1.call-update) | async-done | bytes 3145744 | tf_op jit(solution)/shard_map/psum | solution.py:162
  691.2 74.5 %all-reduce.26.cloned.1.call-done = f32[1024,768]{0,1:T(8,128)} async-done(((f32[1024,768]{0,1:T(8,128)}), f32[1024,768]{0,1:T(8,128)}) %all-reduce.26.cloned.1.call-update) | async-done | bytes 3145744 | tf_op jit(solution)/shard_map/psum | solution.py:162
  839.7 19.1 %all-reduce.28.cloned.1.call-done = f32[1024,768]{0,1:T(8,128)} async-done(((f32[1024,768]{0,1:T(8,128)}), f32[1024,768]{0,1:T(8,128)}) %all-reduce.28.cloned.1.call-update) | async-done | bytes 3145744 | tf_op jit(solution)/shard_map/psum | solution.py:162
  866.5 6.8 fusion.164
  883.4 6.9 multiply_convert_fusion
  950.6 9.6 pad_maximum_fusion
  960.3 18.4 %gather_fusion.1 = f32[96,192,192]{2,1,0:T(8,128)} fusion(f32[96,192,192]{2,1,0:T(8,128)} %bitcast.326, s32[1024]{0:T(1024)} %pad_clamp_fusion), kind=kCustom, calls=%fused_computation.1 | custom fusion | bytes 28311936 | tf_op jit(solution)/shard_map/gather | solution.py:442
  978.7 18.2 %reshape.754 = f32[96,36864]{1,0:T(8,128)} reshape(f32[96,192,192]{2,1,0:T(8,128)} %gather_fusion.1) | data formatting | bytes 28311552 | tf_op jit(solution)/shard_map/reshape | solution.py:443
  1011.2 12.5 all-reduce.5
  1023.7 124.2 %all-reduce.3 = (f32[]{:T(128)}, f32[5096]{0:T(1024)S(1)}) all-reduce(f32[]{:T(128)} %fusion.138, f32[5096]{0:T(1024)S(1)} %pad_maximum_fusion.10), channel_id=1, replica_groups=mesh['dp'=32,'mp'=4] {'dp'}, use_global_device_ids=true, to_apply=%region_32.33 | all-reduce | flops 5097 | bytes 40776 | tf_op jit(solution)/shard_map/psum | solution.py:410
  1158.9 65.7 %psum.140 = f32[]{:T(128)} all-reduce(f32[]{:T(128)S(6)} %add.323), channel_id=1, replica_groups=mesh['dp'=32,'mp'=4] {'dp','mp'}, use_global_device_ids=true, to_apply=%region_66.67 | all-reduce | flops 1 | bytes 8 | tf_op jit(solution)/shard_map/psum | solution.py:460
  1252.9 36.1 %custom-call.21 = f32[3,128,128]{2,1,0:T(8,128)S(1)} custom-call(f32[3,128,128]{2,1,0:T(8,128)} %cholesky.218), custom_call_target="Cholesky" | custom-call | tf_op jit(solution)/shard_map/jit(cholesky)/cholesky | solution.py:109
  1293.0 35.8 %custom-call.17 = f32[3,128,128]{2,1,0:T(8,128)} custom-call(f32[3,128,128]{2,1,0:T(8,128)S(1)} %cholesky.215), custom_call_target="Cholesky" | custom-call | tf_op jit(solution)/shard_map/jit(cholesky)/cholesky | solution.py:109
  1331.8 30.3 %custom-call.22 = f32[3,1,128,128]{2,3,1,0:T(8,128)S(1)} custom-call(f32[3,1,128,128]{3,2,1,0:T(8,128)} %get-tuple-element.235), custom_call_target="InvertDiagBlocksLowerTriangular" | custom-call | tf_op jit(solution)/shard_map/jit(cholesky)/cholesky | solution.py:109
  1365.1 18.2 %custom-call.23 = f32[3,64,64]{2,1,0:T(8,128)} custom-call(f32[3,64,64]{2,1,0:T(8,128)S(1)} %convolution_subtract_fusion.2), custom_call_target="Cholesky" | custom-call | tf_op jit(solution)/shard_map/jit(cholesky)/cholesky | solution.py:109
  1383.3 30.5 %custom-call.18 = f32[3,1,128,128]{2,3,1,0:T(8,128)S(1)} custom-call(f32[3,1,128,128]{3,2,1,0:T(8,128)} %get-tuple-element.236), custom_call_target="InvertDiagBlocksLowerTriangular" | custom-call | tf_op jit(solution)/shard_map/jit(cholesky)/cholesky | solution.py:109
  1416.2 17.6 %custom-call.19 = f32[3,64,64]{2,1,0:T(8,128)S(1)} custom-call(f32[3,64,64]{2,1,0:T(8,128)S(1)} %convolution_subtract_fusion.3), custom_call_target="Cholesky" | custom-call | tf_op jit(solution)/shard_map/jit(cholesky)/cholesky | solution.py:109
  1442.5 60.4 %custom-call.24 = f32[3,2,128,128]{2,3,1,0:T(8,128)} custom-call(f32[3,2,128,128]{3,2,1,0:T(8,128)} %pad_maximum_fusion.7), custom_call_target="InvertDiagBlocksLowerTriangular" | custom-call | tf_op jit(solution)/shard_map/vmap(jit(_solve_triangular))/triangular_solve | solution.py:111
  1504.6 60.6 %custom-call.20 = f32[3,2,128,128]{2,3,1,0:T(8,128)} custom-call(f32[3,2,128,128]{3,2,1,0:T(8,128)} %pad_maximum_fusion.6), custom_call_target="InvertDiagBlocksLowerTriangular" | custom-call | tf_op jit(solution)/shard_map/vmap(jit(_solve_triangular))/triangular_solve | solution.py:111
  (785 shorter events, 455.8 us)
Async XLA Ops:
  7.3 33.7 %all-gather.5.cloned.1.call-start = ((), (), s32[]{:S(2)}) async-start(), calls=%async_computation | async-start | bytes 1966080 | tf_op jit(solution)/shard_map/all_gather | solution.py:373
  11.1 88.8 %all-gather.7.cloned.1.call-start = ((), (), s32[]{:S(2)}) async-start(), calls=%async_computation.9 | async-start | bytes 9732096 | tf_op jit(solution)/shard_map/all_gather | solution.py:357
  12.3 224.8 %all-reduce.16.cloned.1.call-start = ((), (), s32[]{:S(2)}) async-start(), calls=%async_computation.1 | async-start | bytes 6291456 | tf_op jit(solution)/shard_map/psum | solution.py:162
  12.5 104.2 %copy-start.178 = (f32[2,2,64]{2,1,0:T(2,128)}, f32[2,2,64]{2,1,0:T(2,128)S(1)}, u32[]{:S(2)}) copy-start(f32[2,2,64]{2,1,0:T(2,128)S(1)} %reshape.745) | copy-start | bytes 3076
  13.1 135.0 %copy-start.190 = (f32[64]{0:T(128)}, f32[64]{0:T(128)S(1)}, u32[]{:S(2)}) copy-start(f32[64]{0:T(128)S(1)} %get-tuple-element.252) | copy-start | bytes 772
  13.1 135.0 %copy-start.199 = (f32[64]{0:T(128)}, f32[64]{0:T(128)S(1)}, u32[]{:S(2)}) copy-start(f32[64]{0:T(128)S(1)} %get-tuple-element.253) | copy-start | bytes 772
  13.7 126.4 %copy-start.154 = (f32[768]{0:T(1024)}, f32[768]{0:T(1024)S(1)}, u32[]{:S(2)}) copy-start(f32[768]{0:T(1024)S(1)} %get-tuple-element.245) | copy-start | bytes 9220
  13.7 226.4 %copy-start.143 = (f32[768]{0:T(1024)}, f32[768]{0:T(1024)S(1)}, u32[]{:S(2)}) copy-start(f32[768]{0:T(1024)S(1)} %get-tuple-element.244) | copy-start | bytes 9220
  13.7 322.2 %copy-start.167 = (f32[768]{0:T(1024)}, f32[768]{0:T(1024)S(1)}, u32[]{:S(2)}) copy-start(f32[768]{0:T(1024)S(1)} %get-tuple-element.243) | copy-start | bytes 9220
  13.7 421.6 %copy-start.149 = (f32[768]{0:T(1024)}, f32[768]{0:T(1024)S(1)}, u32[]{:S(2)}) copy-start(f32[768]{0:T(1024)S(1)} %get-tuple-element.242) | copy-start | bytes 9220
  42.7 97.5 %copy-start.137 = (f32[1024]{0:T(1024)}, f32[1024]{0:T(1024)S(1)}, u32[]{:S(2)}) copy-start(f32[1024]{0:T(1024)S(1)} %broadcast_multiply_fusion.14) | copy-start | bytes 12292
  44.5 95.6 %copy-start.156 = (f32[1024]{0:T(1024)}, f32[1024]{0:T(1024)S(1)}, u32[]{:S(2)}) copy-start(f32[1024]{0:T(1024)S(1)} %fusion.132) | copy-start | bytes 12292
  162.1 169.3 %all-reduce.18.cloned.1.call-start = ((), (), s32[]{:S(2)}) async-start(), calls=%async_computation.2 | async-start | bytes 6291456 | tf_op jit(solution)/shard_map/psum | solution.py:162
  255.8 175.2 %all-reduce.20.cloned.1.call-start = ((), (), s32[]{:S(2)}) async-start(), calls=%async_computation.3 | async-start | bytes 6291456 | tf_op jit(solution)/shard_map/psum | solution.py:162
  355.3 171.6 %all-reduce.22.cloned.1.call-start = ((), (), s32[]{:S(2)}) async-start(), calls=%async_computation.4 | async-start | bytes 6291456 | tf_op jit(solution)/shard_map/psum | solution.py:162
  434.9 226.8 %copy-start.132 = (f32[1024]{0:T(1024)}, f32[1024]{0:T(1024)S(1)}, u32[]{:S(2)}) copy-start(f32[1024]{0:T(1024)S(1)} %broadcast_multiply_fusion.11) | copy-start | bytes 12292
  435.3 226.4 %copy-start.171 = (f32[1024]{0:T(1024)}, f32[1024]{0:T(1024)S(1)}, u32[]{:S(2)}) copy-start(f32[1024]{0:T(1024)S(1)} %fusion.135) | copy-start | bytes 12292
  451.2 204.0 %all-reduce.24.cloned.1.call-start = ((), (), s32[]{:S(2)}) async-start(), calls=%async_computation.5 | async-start | bytes 6291456 | tf_op jit(solution)/shard_map/psum | solution.py:162
  452.6 103.7 %copy-start.203 = (f32[8]{0:T(128)}, f32[8]{0:T(128)S(1)}, u32[]{:S(2)}) copy-start(f32[8]{0:T(128)S(1)} %get-tuple-element.254) | copy-start | bytes 100
  545.9 279.7 %copy-start.88 = (f32[8,1000]{1,0:T(8,128)}, f32[8,1000]{1,0:T(8,128)S(1)}, u32[]{:S(2)}) copy-start(f32[8,1000]{1,0:T(8,128)S(1)} %psum.130) | copy-start | bytes 96004
  562.9 98.8 %copy-start.188 = (f32[1024]{0:T(1024)}, f32[1024]{0:T(1024)S(1)}, u32[]{:S(2)}) copy-start(f32[1024]{0:T(1024)S(1)} %negate_multiply_fusion.10) | copy-start | bytes 12292
  572.9 82.3 %copy-start.150 = (f32[768]{0:T(1024)S(1)}, f32[768]{0:T(1024)}, u32[]{:S(2)}) copy-start(f32[768]{0:T(1024)} %copy-done.149) | copy-start | bytes 9220
  572.9 192.8 %all-reduce.26.cloned.1.call-start = ((), (), s32[]{:S(2)}) async-start(), calls=%async_computation.6 | async-start | bytes 6291456 | tf_op jit(solution)/shard_map/psum | solution.py:162
  690.0 75.7 %copy-start.148 = (f32[1024]{0:T(1024)S(1)}, f32[1024]{0:T(1024)}, u32[]{:S(2)}) copy-start(f32[1024]{0:T(1024)} %copy-done.147) | copy-start | bytes 12292
  690.0 75.7 %copy-start.168 = (f32[768]{0:T(1024)S(1)}, f32[768]{0:T(1024)}, u32[]{:S(2)}) copy-start(f32[768]{0:T(1024)} %copy-done.167) | copy-start | bytes 9220
  690.0 75.7 %copy-start.170 = (f32[1024]{0:T(1024)S(1)}, f32[1024]{0:T(1024)}, u32[]{:S(2)}) copy-start(f32[1024]{0:T(1024)} %copy-done.169) | copy-start | bytes 12292
  690.0 168.8 %all-reduce.28.cloned.1.call-start = ((), (), s32[]{:S(2)}) async-start(), calls=%async_computation.7 | async-start | bytes 6291456 | tf_op jit(solution)/shard_map/psum | solution.py:162
  691.2 79.0 %copy-start.166 = (f32[1024]{0:T(1024)S(1)}, f32[1024]{0:T(1024)}, u32[]{:S(2)}) copy-start(f32[1024]{0:T(1024)} %copy-done.165) | copy-start | bytes 12292
  783.2 213.7 %all-reduce.30.cloned.1.call-start = ((), (), s32[]{:S(2)}) async-start(), calls=%async_computation.8 | async-start | bytes 6291456 | tf_op jit(solution)/shard_map/psum | solution.py:162
  900.2 249.8 %all-reduce.32.cloned.1.call-start = ((), (), s32[]{:S(2)}) async-start(), calls=%async_computation.10 | async-start | bytes 31064064 | tf_op jit(solution)/shard_map/psum | solution.py:453
  1148.0 81.3 %copy-start.134 = (f32[5096]{0:T(1024)}, f32[5096]{0:T(1024)S(1)}, u32[]{:S(2)}) copy-start(f32[5096]{0:T(1024)S(1)} %get-tuple-element.177) | copy-start | bytes 61156
  1437.0 128.3 %copy-start.56 = (f32[3,192,192]{1,2,0:T(8,128)S(1)}, f32[3,192,192]{1,2,0:T(8,128)}, u32[]{:S(2)}) copy-start(f32[3,192,192]{1,2,0:T(8,128)} %copy.346) | copy-start | bytes 1327108
  (217 other events, 1438.2 us)
Sparse Core Ops, SparseCore 0:
  11.2 29.6 all-gather.4
  43.8 56.0 all-gather.6
  162.3 74.7 all-reduce.15
  255.9 75.5 all-reduce.17
  355.4 75.5 all-reduce.19
  451.3 75.5 all-reduce.21
  573.0 82.1 all-reduce.23
  690.1 75.5 all-reduce.25
  783.3 75.5 all-reduce.27
  900.3 75.5 all-reduce.29
  1003.3 146.6 all-reduce.31
where the time goes:
time: 1620 us; the launch traced here: 1610 us
  waiting for transfers between devices  455 us (28%)
  other arithmetic  424 us (26%)
  blocking collectives  287 us (18%)
  local copies, waits for them, and re-layouts  258 us (16%)
  matrix products  167 us (10%)
  between operations  21.7 us (1%)
    psum x8, waiting for transfers between devices, branch_sum(): return lax.psum(partial_sum, 'mp')  372 us
    psum x2, blocking collectives, shards(): image_total, loss_total = lax.psum((local_count, local_loss), 'dp')  188 us
    another operation x16, other arithmetic, power_step(): factor = jnp.linalg.cholesky(gram_mat)  174 us
    another operation x9, other arithmetic, power_step(): jax.scipy.linalg.solve_triangular(lower_tri, right_side, lower=True)  127 us
    dot_general x23, matrix products, matmul(): return jnp.dot(left, right, preferred_element_type=jnp.float32)  71.4 us
    psum x1, blocking collectives, shards(): squares = lax.psum(local_squares, ('dp', 'mp'))  65.7 us
    all_gather x1, waiting for transfers between devices, shards(): lax.all_gather(soap_weight.astype(jnp.bfloat16), 'dp', axis=0, tiled=True)  55.3 us
    unnamed x479, local copies, waits for them, and re-layouts  52.4 us
  transfers between devices with their start and end apart: 11, of which 10 were waited for; matrix products, arithmetic and copies ran while one was open for 13% of the time, Pallas kernels for 0%

commit v1 on v0

v1 whole, which is shorter than its diff:
```python
import jax
import jax.numpy as jnp
from jax import lax
from jax.experimental import pallas as pl
from jax.experimental.pallas import tpu as pltpu
from jax.sharding import PartitionSpec as P

D = 768
HD = 64
HEADS = 3
CLASSES = 1000
LAYERS = 2
IMGS = 8
STEP = 10
TILE = 192
TOKENS = 1024
OWN = 256
PACK = 288
SMALL = 96
ROWS = 3 * PACK + SMALL
EMBED_ROWS = 36
HEAD_ROWS = 48

first_decay = 0.9
second_decay = 0.95
weight_decay = 0.05
matrix_rate = 0.03
vector_rate = 0.3
clip_limit = 0.01
adam_epsilon = 1e-08
norm_epsilon = 1e-06
masked_score = -1e30
highest = lax.Precision.HIGHEST
f32 = jnp.float32
bf16 = jnp.bfloat16
MIB = 2**20
VM = pl.BlockSpec(memory_space=pltpu.VMEM)
SM = pl.BlockSpec(memory_space=pltpu.SMEM)
ANY = pl.BlockSpec(memory_space=pl.ANY)


def params(mib):
    return pltpu.CompilerParams(vmem_limit_bytes=mib * MIB)


def cost(flops, moved, exps=0):
    return pl.CostEstimate(flops=flops, bytes_accessed=moved, transcendentals=exps)


def shape(dims, kind=f32):
    return jax.ShapeDtypeStruct(dims, kind)


def mm(a, b, ca=1, cb=0):
    return lax.dot_general(a, b, (((ca,), (cb,)), ((), ())), preferred_element_type=f32)


def mm_full(a, b, ca, cb):
    return lax.dot_general(
        a, b, (((ca,), (cb,)), ((), ())), precision=highest, preferred_element_type=f32
    )


def mm_split(a, b, ca, cb):
    a_high, b_high = (a.astype(bf16), b.astype(bf16))
    a_low = (a - a_high.astype(f32)).astype(bf16)
    b_low = (b - b_high.astype(f32)).astype(bf16)
    return mm(a_high, b_high, ca, cb) + (mm(a_high, b_low, ca, cb) + mm(a_low, b_high, ca, cb))


def normalize(values):
    centered = values - jnp.mean(values, -1, keepdims=True)
    inverse = lax.rsqrt(jnp.mean(centered * centered, -1, keepdims=True) + norm_epsilon)
    return centered * inverse, inverse


def norm_back(grad, gain, normed, inverse):
    scaled = grad * gain
    return inverse * (
        scaled
        - jnp.mean(scaled, -1, keepdims=True)
        - normed * jnp.mean(scaled * normed, -1, keepdims=True)
    )


def gauss_parts(value):
    size = jnp.abs(value) * 0.7071067811865476
    bell = jnp.exp(-size * size)
    t = 1.0 / (1.0 + 0.3275911 * size)
    poly = t * (
        0.254829592
        + t * (-0.284496736 + t * (1.421413741 + t * (-1.453152027 + t * 1.061405429)))
    )
    tail = 0.5 * poly * bell
    return jnp.where(value >= 0, 1.0 - tail, tail), bell


def gelu(value):
    return value * gauss_parts(value)[0]


def pack_tile(tile):
    half = TILE // 2
    right = tile[..., 128:]
    return jnp.concatenate(
        [
            tile[..., :128],
            jnp.concatenate([right[..., :half, :], right[..., half:, :]], axis=-1),
        ],
        axis=-2,
    )


def unpack_tile(packed):
    half = TILE // 2
    right = packed[..., TILE:, :]
    return jnp.concatenate(
        [
            packed[..., :TILE, :],
            jnp.concatenate([right[..., :64], right[..., 64:]], axis=-2),
        ],
        axis=-1,
    )


def assemble(table, slots, blocks):
    rows = len(blocks)
    flat = [block for line in blocks for block in line]

    def kernel(table_ref, *refs):
        out_ref = refs[-1]
        for i in range(rows):
            for t in range(4):
                out_ref[0, TILE * i : TILE * i + TILE, TILE * t : TILE * t + TILE] = unpack_tile(
                    refs[4 * i + t][0]
                )

    def spec(block):
        return pl.BlockSpec((1, PACK, 128), lambda r, table_ref: (table_ref[r * 96 + block], 0, 0))

    return pl.pallas_call(
        kernel,
        grid_spec=pltpu.PrefetchScalarGridSpec(
            num_scalar_prefetch=1,
            grid=(4,),
            in_specs=[spec(block) for block in flat],
            out_specs=pl.BlockSpec((1, rows * TILE, D), lambda r, table_ref: (r, 0, 0)),
        ),
        out_shape=shape((4, rows * TILE, D), bf16),
        compiler_params=params(32),
        cost_estimate=cost(0, 16 * rows * TILE * TILE * 4),
        name="assemble",
    )(table, *([slots] * len(flat)))


def layer_weights(table, slots, depth):
    base = 48 * depth
    qkv = assemble(table, slots, [[base + 3 * r + c for r in range(4)] for c in range(3)])
    out = assemble(table, slots, [[base + 12 + t for t in range(4)]])
    up = assemble(table, slots, [[base + 16 + 4 * r + t for r in range(4)] for t in range(4)])
    down = assemble(table, slots, [[base + 32 + 4 * t + r for r in range(4)] for t in range(4)])
    return qkv, out.reshape(D, D), up, down


def column_norm(values):
    centered = values - jnp.mean(values, 0, keepdims=True)
    inverse = lax.rsqrt(jnp.mean(centered * centered, 0, keepdims=True) + norm_epsilon)
    return centered * inverse, inverse


def attend_fwd(w_ref, a0, a1, a2, a3, gain_ref, qid_ref, kid_ref, pre_ref, v_ref, lse_ref, o_ref, q_s, k_s):
    for c in range(3):
        for r, a_ref in enumerate((a0, a1, a2, a3)):
            cols = slice(OWN * r, OWN * r + OWN)
            part = mm(w_ref[0, TILE * c : TILE * c + TILE, :], a_ref[...], 1, 1)
            if c == 2:
                v_ref[:, cols] = part.astype(bf16)
                continue
            pre_ref[TILE * c : TILE * c + TILE, cols] = part
            for h in range(HEADS):
                rows = slice(HD * h, HD * h + HD)
                low = (column_norm(part[rows, :])[0] * gain_ref[:, c : c + 1]).astype(bf16)
                if c == 0:
                    q_s[r, rows, :] = low * bf16(0.125)
                else:
                    k_s[h, cols, :] = low.T

    def step(i, carry):
        h, t = (i // 4, i % 4)
        rows = pl.ds(pl.multiple_of(h * HD, HD), HD)
        cols = pl.ds(pl.multiple_of(t * OWN, OWN), OWN)
        scores = mm(k_s[h], q_s[t, rows, :])
        scores = jnp.where(kid_ref[...] == qid_ref[:, cols], scores, masked_score)
        top = jnp.max(scores, 0, keepdims=True)
        weights = jnp.exp(scores - top)
        total = jnp.sum(weights, 0, keepdims=True)
        lse_ref[h, :, cols] = top + jnp.log(total)
        probs = (weights * (1.0 / total)).astype(bf16)
        o_ref[t, rows, :] = mm(v_ref[rows, :], probs).astype(bf16)
        return carry

    lax.fori_loop(0, 4 * HEADS, step, 0)


def run_attend_fwd(w, acts, gains, qid, kid):
    return pl.pallas_call(
        attend_fwd,
        grid=(1,),
        in_specs=[pl.BlockSpec((1, 3 * TILE, D), lambda i: (0, 0, 0))] + [VM] * 7,
        out_specs=[VM] * 4,
        out_shape=[
            shape((2 * TILE, TOKENS)),
            shape((TILE, TOKENS), bf16),
            shape((HEADS, 1, TOKENS)),
            shape((4, TILE, OWN), bf16),
        ],
        scratch_shapes=[pltpu.VMEM((4, TILE, OWN), bf16), pltpu.VMEM((HEADS, TOKENS, HD), bf16)],
        compiler_params=params(48),
        cost_estimate=cost(10**10, 6 * 10**6, 3 * 2**20),
        name="attend_fwd",
    )(w, *acts, gains, qid, kid)


def attend_bwd(
    pre_ref, v_ref, lse_ref, g0, g1, g2, g3, gain_ref, qid_ref, kid_ref,
    dp_ref, dgain_ref, q_s, qn_s, k_s, kt_s, vn_s, do_s, dq_s, dk_s, dv_s,
):
    for r, ref in enumerate((g0, g1, g2, g3)):
        do_s[r] = ref[...]
    for h in range(HEADS):
        rows = slice(HD * h, HD * h + HD)
        low = (column_norm(pre_ref[rows, :])[0] * gain_ref[:, 0:1]).astype(bf16)
        q_s[rows, :] = low * bf16(0.125)
        qn_s[h] = q_s[rows, :].T
        low = (column_norm(pre_ref[TILE + HD * h : TILE + HD * h + HD, :])[0] * gain_ref[:, 1:2]).astype(bf16)
        kt_s[rows, :] = low
        k_s[h] = low.T
        vn_s[h] = v_ref[rows, :].T
    dk_s[...] = jnp.zeros_like(dk_s)
    dv_s[...] = jnp.zeros_like(dv_s)

    def step(i, carry):
        h, t = (i // 4, i % 4)
        rows = pl.ds(pl.multiple_of(h * HD, HD), HD)
        cols = pl.ds(pl.multiple_of(t * OWN, OWN), OWN)
        scores = mm(k_s[h], q_s[rows, cols])
        scores = jnp.where(kid_ref[...] == qid_ref[:, cols], scores, masked_score)
        weights = jnp.exp(scores - lse_ref[h, :, cols])
        grad_out = do_s[t, rows, :]
        grad_weights = mm(vn_s[h], grad_out)
        dv_s[h] += mm(weights.astype(bf16), grad_out.T)
        inner = jnp.sum(weights * grad_weights, 0, keepdims=True)
        grad_scores = (weights * (grad_weights - inner)).astype(bf16)
        dq_s[rows, cols] = mm(kt_s[rows, :], grad_scores) * 0.125
        dk_s[h] += mm(grad_scores, qn_s[h, cols, :])
        return carry

    lax.fori_loop(0, 4 * HEADS, step, 0)
    for c in range(2):
        total = jnp.zeros((HD, 1), f32)
        for h in range(HEADS):
            grad = dq_s[HD * h : HD * h + HD, :] if c == 0 else dk_s[h].T
            base = TILE * c + HD * h
            normed, inverse = column_norm(pre_ref[base : base + HD, :])
            total = total + jnp.sum(grad * normed, 1, keepdims=True)
            scaled = grad * gain_ref[:, c : c + 1]
            back = inverse * (
                scaled
                - jnp.mean(scaled, 0, keepdims=True)
                - normed * jnp.mean(scaled * normed, 0, keepdims=True)
            )
            for r in range(4):
                dp_ref[r, base : base + HD, :] = back[:, OWN * r : OWN * r + OWN].astype(bf16)
        dgain_ref[:, c : c + 1] = total
    for h in range(HEADS):
        back = dv_s[h].T.astype(bf16)
        for r in range(4):
            dp_ref[r, 2 * TILE + HD * h : 2 * TILE + HD * h + HD, :] = back[:, OWN * r : OWN * r + OWN]


def run_attend_bwd(pre, v, lse, grads, gains, qid, kid):
    return pl.pallas_call(
        attend_bwd,
        in_specs=[VM] * 10,
        out_specs=[VM] * 2,
        out_shape=[shape((4, 3 * TILE, OWN), bf16), shape((HD, 2))],
        scratch_shapes=[
            pltpu.VMEM((TILE, TOKENS), bf16),
            pltpu.VMEM((HEADS, TOKENS, HD), bf16),
            pltpu.VMEM((HEADS, TOKENS, HD), bf16),
            pltpu.VMEM((TILE, TOKENS), bf16),
            pltpu.VMEM((HEADS, TOKENS, HD), bf16),
            pltpu.VMEM((4, TILE, OWN), bf16),
            pltpu.VMEM((TILE, TOKENS), f32),
            pltpu.VMEM((HEADS, TOKENS, HD), f32),
            pltpu.VMEM((HEADS, TOKENS, HD), f32),
        ],
        compiler_params=params(48),
        cost_estimate=cost(2 * 10**10, 6 * 10**6, 3 * 2**20),
        name="attend_bwd",
    )(pre, v, lse, *grads, gains, qid, kid)


def mix_fwd(x_ref, o0, o1, o2, o3, w_out, gain_ref, next_ref, up_ref, down_ref,
            mid_ref, u_ref, ct_ref, x_out, a_out, c_s):
    r = pl.program_id(0)

    @pl.when(r == 0)
    def _():
        mid = x_ref[...]
        for k, ref in enumerate((o0, o1, o2, o3)):
            mid = mid + mm(ref[...], w_out[TILE * k : TILE * k + TILE, :], 0, 0)
        mid_ref[...] = mid
        low = (normalize(mid)[0] * gain_ref[...]).astype(bf16)
        c_s[...] = low
        ct_ref[...] = low.T
        x_out[...] = mid

    u = mm(c_s[...], up_ref[0], 1, 1)
    u_ref[0] = u
    x_out[...] += mm(gelu(u).astype(bf16), down_ref[0])

    @pl.when(r == 3)
    def _():
        a_out[...] = (normalize(x_out[...])[0] * next_ref[...]).astype(bf16)


def whole(*dims):
    return pl.BlockSpec(dims, lambda r: (0,) * len(dims))


def part(*dims):
    return pl.BlockSpec((1, *dims), lambda r: (r,) + (0,) * len(dims))


def run_mix_fwd(x, outs, w_out, gain, gain_next, up, down):
    return pl.pallas_call(
        mix_fwd,
        grid=(4,),
        in_specs=[whole(OWN, D)] + [whole(TILE, OWN)] * 4 + [whole(D, D), whole(1, D), whole(1, D), part(D, D), part(D, D)],
        out_specs=[whole(OWN, D), part(OWN, D), whole(D, OWN), whole(OWN, D), whole(OWN, D)],
        out_shape=[shape((OWN, D)), shape((4, OWN, D)), shape((D, OWN), bf16), shape((OWN, D)), shape((OWN, D), bf16)],
        scratch_shapes=[pltpu.VMEM((OWN, D), bf16)],
        compiler_params=params(48),
        cost_estimate=cost(6 * 10**9, 17 * 10**6, 10**6),
        name="mix_fwd",
    )(x, *outs, w_out, gain, gain_next, up, down)


def mix_bwd(g_ref, low_ref, mid_ref, u_ref, gain_ref, w_out, up_ref, down_ref,
            du_ref, mid_grad, mid_low, dgain_ref, do_ref, acc):
    r = pl.program_id(0)

    @pl.when(r == 0)
    def _():
        acc[...] = jnp.zeros_like(acc)

    df = mm(low_ref[...], down_ref[0], 1, 1)
    u = u_ref[0]
    cdf, bell = gauss_parts(u)
    du = (df * (cdf + u * bell * 0.3989422804014327)).astype(bf16)
    du_ref[0] = du
    acc[...] += mm(du, up_ref[0])

    @pl.when(r == 3)
    def _():
        normed, inverse = normalize(mid_ref[...])
        grad = acc[...]
        dgain_ref[...] = jnp.sum(grad * normed, 0, keepdims=True)
        total = g_ref[...] + norm_back(grad, gain_ref[...], normed, inverse)
        mid_grad[...] = total
        low = total.astype(bf16)
        mid_low[...] = low
        for k in range(4):
            do_ref[k] = mm(w_out[TILE * k : TILE * k + TILE, :], low, 1, 1).astype(bf16)


def run_mix_bwd(grad, grad_low, mid, u, gain, w_out, up, down):
    return pl.pallas_call(
        mix_bwd,
        grid=(4,),
        in_specs=[whole(OWN, D), whole(OWN, D), whole(OWN, D), part(OWN, D), whole(1, D), whole(D, D), part(D, D), part(D, D)],
        out_specs=[part(OWN, D), whole(OWN, D), whole(OWN, D), whole(1, D), whole(4, TILE, OWN)],
        out_shape=[shape((4, OWN, D), bf16), shape((OWN, D)), shape((OWN, D), bf16), shape((1, D)), shape((4, TILE, OWN), bf16)],
        scratch_shapes=[pltpu.VMEM((OWN, D), f32)],
        compiler_params=params(48),
        cost_estimate=cost(6 * 10**9, 17 * 10**6, 10**6),
        name="mix_bwd",
    )(grad, grad_low, mid, u, gain, w_out, up, down)


def input_bwd(mid_grad, d0, d1, d2, d3, w_ref, x_ref, gain_ref, grad_ref, low_ref, dgain_ref):
    grad = mm(d0[...], w_ref[0], 0, 0)
    for k, ref in ((1, d1), (2, d2), (3, d3)):
        grad = grad + mm(ref[...], w_ref[k], 0, 0)
    normed, inverse = normalize(x_ref[...])
    dgain_ref[...] = jnp.sum(grad * normed, 0, keepdims=True)
    total = mid_grad[...] + norm_back(grad, gain_ref[...], normed, inverse)
    grad_ref[...] = total
    low_ref[...] = total.astype(bf16)


def run_input_bwd(mid_grad, grads, w, x, gain):
    return pl.pallas_call(
        input_bwd,
        in_specs=[VM] * 8,
        out_specs=[VM] * 3,
        out_shape=[shape((OWN, D)), shape((OWN, D), bf16), shape((1, D))],
        compiler_params=params(48),
        cost_estimate=cost(10**9, 6 * 10**6),
        name="input_bwd",
    )(mid_grad, *grads, w, x, gain)


def send_tiles(places, stage, sems, keep, send, tiles, base):
    for i, (block, tile) in enumerate(tiles):
        at = base + i
        stage[at] = pack_tile(tile.astype(bf16))
        place = places[block]
        rows = pl.ds(pl.multiple_of((place % 3) * PACK, 16), PACK)

        @pl.when(place < 48)
        def _():
            pltpu.make_async_copy(stage.at[at], keep.at[place // 3, rows], sems.at[at]).start()

        @pl.when(place >= 48)
        def _():
            pltpu.make_async_copy(stage.at[at], send.at[place // 3 - 16, rows], sems.at[at]).start()


def wait_tiles(stage, sems, keep, count):
    for at in range(count):
        pltpu.make_async_copy(stage.at[at], keep.at[0, pl.ds(0, PACK)], sems.at[at]).wait()


def cut(line, count=4):
    return [line[:, TILE * t : TILE * t + TILE] for t in range(count)]


def mlp_grads(depth, places, *refs):
    ct, du, low, mid_low = (refs[0:4], refs[4:8], refs[8:12], refs[12:16])
    o_ref, up_ref = refs[16:18]
    keep, send, stage, f_s, sems = refs[-5:]
    base = 48 * depth
    for r in range(4):
        f_s[r] = gelu(mm(up_ref[0], ct[r][...])).astype(bf16)

    def rows_of(pieces, others, i):
        rows = slice(TILE * i, TILE * i + TILE)
        total = mm(pieces[0][rows, :], others[0][...])
        for r in range(1, 4):
            total = total + mm(pieces[r][rows, :], others[r][...])
        return total

    line = rows_of([o_ref.at[r] for r in range(4)], mid_low, 0)
    send_tiles(places, stage, sems, keep, send, [(base + 12 + t, x) for t, x in enumerate(cut(line))], 0)
    for i in range(4):
        line = rows_of(ct, du, i)
        tiles = [(base + 16 + 4 * i + t, x) for t, x in enumerate(cut(line))]
        send_tiles(places, stage, sems, keep, send, tiles, 4 + 4 * i)
    for i in range(4):
        line = rows_of([f_s.at[r] for r in range(4)], low, i)
        tiles = [(base + 32 + 4 * i + t, x) for t, x in enumerate(cut(line))]
        send_tiles(places, stage, sems, keep, send, tiles, 20 + 4 * i)
    wait_tiles(stage, sems, keep, 36)


def qkv_grads(depth, places, *refs):
    dp_ref, acts = (refs[0], refs[1:5])
    keep, send, stage, sems = refs[-4:]
    base = 48 * depth
    for c in range(3):
        rows = slice(TILE * c, TILE * c + TILE)
        line = mm(dp_ref[0, rows, :], acts[0][...])
        for r in range(1, 4):
            line = line + mm(dp_ref[r, rows, :], acts[r][...])
        tiles = [(base + 3 * t + c, x) for t, x in enumerate(cut(line))]
        send_tiles(places, stage, sems, keep, send, tiles, 4 * c)
    wait_tiles(stage, sems, keep, 12)


def grads_call(kernel, name, places, args, specs, buffers, scratch, flops):
    out = [shape((16, ROWS, 128), bf16)] * 2
    given = list(buffers) if buffers is not None else []
    first = 1 + len(args)
    return pl.pallas_call(
        kernel,
        grid=(1,),
        in_specs=[SM] + specs + [ANY] * len(given),
        out_specs=[ANY] * 2,
        out_shape=out,
        input_output_aliases={first + i: i for i in range(len(given))},
        scratch_shapes=scratch,
        compiler_params=params(56),
        cost_estimate=cost(flops, 10**7),
        name=name,
    )(places, *args, *given)


def run_mlp_grads(depth, places, ct, du, low, mid_low, o, up, buffers):
    specs = [VM] * 17 + [pl.BlockSpec((1, D, D), lambda i: (0, 0, 0))]
    return grads_call(
        lambda *refs: mlp_grads(depth, *refs), "mlp_grads", places,
        [*ct, *du, *low, *mid_low, o, up], specs, buffers,
        [pltpu.VMEM((36, PACK, 128), bf16), pltpu.VMEM((4, D, OWN), bf16), pltpu.SemaphoreType.DMA((36,))],
        4 * 10**9,
    )


def run_qkv_grads(depth, places, dp, acts, buffers):
    return grads_call(
        lambda *refs: qkv_grads(depth, *refs), "qkv_grads", places, [dp, *acts], [VM] * 5, buffers,
        [pltpu.VMEM((12, PACK, 128), bf16), pltpu.SemaphoreType.DMA((12,))], 10**9,
    )


def soap_early(first, stat_l, stat_r, left, right, turned_ref, l_ref, r_ref):
    turned_ref[0] = mm_split(mm_split(left[0], first[0], 0, 0), right[0], 1, 0)
    l_ref[0] = mm_full(stat_l[0], left[0], 1, 0)
    r_ref[0] = mm_full(stat_r[0], right[0], 1, 0)


def soap_mid(flip_ref, packed, left, right, grad_ref, turned_ref, yl_ref, yr_ref, gl_ref, gr_ref):
    tile = unpack_tile(packed[0])
    turned_tile = tile.T
    flip = flip_ref[pl.program_id(0)] == 1
    grad = jnp.where(flip, turned_tile, tile)
    grad_t = jnp.where(flip, tile, turned_tile)
    grad_ref[0] = grad
    right_part = mm_full(grad, right[0], 1, 0)
    turned_ref[0] = mm_split(left[0], right_part, 0, 0)
    yr_ref[0] = mm_full(grad_t, right_part, 1, 0)
    yl_ref[0] = mm_full(grad, mm_full(grad_t, left[0], 1, 0), 1, 0)
    gl_ref[0] = mm_full(grad, grad_t, 1, 0)
    gr_ref[0] = mm_full(grad_t, grad, 1, 0)


def factor_inverses(grams):
    size = 64
    row = lax.broadcasted_iota(jnp.int32, (8, 128), 0)
    lane = lax.broadcasted_iota(jnp.int32, (8, 128), 1)
    states = []
    for gram in grams:
        wide = jnp.concatenate([gram, jnp.zeros((size, size), f32)], axis=1)
        states.append(
            [jnp.where(lane == row + (size + 8 * t), 1.0, wide[8 * t : 8 * t + 8, :]) for t in range(8)]
        )
    for k in range(size):
        home, at = divmod(k, 8)
        for tiles in states:
            pivot = tiles[home][at : at + 1, k : k + 1]
            line = tiles[home][at : at + 1, :] * (1.0 / pivot)
            for t in range(home, 8):
                update = tiles[t][:, k : k + 1] * line
                if t == home:
                    update = jnp.where(row > at, update, 0.0)
                tiles[t] = tiles[t] - update
    inverses = []
    for tiles in states:
        done = []
        for t in range(8):
            diagonal = jnp.sum(jnp.where(lane == row + 8 * t, tiles[t], 0.0), axis=1, keepdims=True)
            done.append(tiles[t] * lax.rsqrt(diagonal))
        inverses.append(jnp.concatenate(done, axis=0)[:, size:])
    return inverses


def soap_late(
    f_ref, grad, first, second, stat_l, stat_r, left, right, weight, turned, turned_first, xl, xr, yl, yr, gl, gr,
    weight_ref, first_ref, second_ref, sl_ref, sr_ref, left_ref, right_ref, low_ref, panels,
):
    factor = f_ref[0, 0]
    bias_one = 1.0 - first_decay**STEP
    bias_two = 1.0 - second_decay**STEP
    for n in range(3):
        first_ref[n] = first_decay * first[n] + (1.0 - first_decay) * (grad[n] * factor)
        rotated = turned[n] * factor
        second_new = second_decay * second[n] + (1.0 - second_decay) * rotated * rotated
        second_ref[n] = second_new
        scaled = (
            (first_decay * turned_first[n] + (1.0 - first_decay) * rotated)
            / bias_one
            / (jnp.sqrt(second_new / bias_two) + adam_epsilon)
        )
        back = mm_split(mm_split(left[n], scaled, 1, 0), right[n], 1, 1)
        weight_new = weight[n] * (1.0 - matrix_rate * weight_decay) - matrix_rate * back
        weight_ref[n] = weight_new
        low_ref[n] = weight_new.astype(bf16)
        sl_ref[n] = second_decay * stat_l[n] + (1.0 - second_decay) * (factor * (factor * gl[n]))
        sr_ref[n] = second_decay * stat_r[n] + (1.0 - second_decay) * (factor * (factor * gr[n]))
        for side, (old, new) in enumerate(((xl, yl), (xr, yr))):
            product = second_decay * old[n] + (1.0 - second_decay) * (factor * (factor * new[n]))
            for j in range(3):
                panels[2 * n + side, j] = product[:, 64 * j : 64 * j + 64]
    outs = (left_ref, right_ref)
    for j in range(3):
        inverses = factor_inverses([mm_full(panels[i, j], panels[i, j], 0, 0) for i in range(6)])
        for i in range(6):
            basis = mm_full(panels[i, j], inverses[i], 1, 1)
            outs[i % 2][i // 2, :, 64 * j : 64 * j + 64] = basis
            for k in range(j + 1, 3):
                panel = panels[i, k]
                panels[i, k] = panel - mm_full(basis, mm_full(basis, panel, 0, 0), 1, 0)


def tile_spec():
    return pl.BlockSpec((1, TILE, TILE), lambda i: (i, 0, 0))


def tiles_of_three(count):
    return [shape((3, TILE, TILE))] * count


def run_soap_early(first, stat_l, stat_r, left, right):
    return pl.pallas_call(
        soap_early, grid=(3,), in_specs=[tile_spec()] * 5, out_specs=[tile_spec()] * 3,
        out_shape=tiles_of_three(3), compiler_params=params(32), cost_estimate=cost(10**9, 4 * 10**6), name="soap_early",
    )(first, stat_l, stat_r, left, right)


def run_soap_mid(flips, packed, left, right):
    return pl.pallas_call(
        soap_mid, grid=(3,),
        in_specs=[SM, pl.BlockSpec((1, PACK, 128), lambda i: (i, 0, 0)), tile_spec(), tile_spec()],
        out_specs=[tile_spec()] * 6, out_shape=tiles_of_three(6),
        compiler_params=params(32), cost_estimate=cost(10**9, 4 * 10**6), name="soap_mid",
    )(flips, packed, left, right)


def run_soap_late(*args):
    return pl.pallas_call(
        soap_late, in_specs=[SM] + [VM] * 16, out_specs=[VM] * 8,
        out_shape=tiles_of_three(7) + [shape((3, TILE, TILE), bf16)],
        scratch_shapes=[pltpu.VMEM((6, 3, TILE, 64), f32)],
        compiler_params=params(56), cost_estimate=cost(10**9, 10**7), name="soap_late",
    )(*args)


def adamw(master, gradient, first, second, rate, decay):
    first_new = first_decay * first + (1.0 - first_decay) * gradient
    second_new = second_decay * second + (1.0 - second_decay) * gradient * gradient
    step_dir = (
        first_new
        / (1.0 - first_decay**STEP)
        / (jnp.sqrt(second_new / (1.0 - second_decay**STEP)) + adam_epsilon)
    )
    return (master * (1.0 - rate * decay) - rate * step_dir, first_new, second_new)


def swap(array, axis, r, size):
    return lax.ppermute(array, axis, [(i, i ^ r) for i in range(size)])


def swap_mp(array, r):
    return swap(array, "mp", r, 4)


def swap_dp(array, r):
    return swap(array, "dp", r, 32)


def gather_mp(array):
    return [array] + [swap_mp(array, r) for r in (1, 2, 3)]


def trade_mp(pieces):
    return [pieces[0]] + [swap_mp(pieces[r], r) for r in (1, 2, 3)]


def sum_four(pieces):
    return (pieces[0] + pieces[1]) + (pieces[2] + pieces[3])


def total_mp(array):
    return sum_four(gather_mp(array))


def total_dp(array):
    array = array + swap_dp(array, 1)
    array = sum_four([array] + [swap_dp(array, 2 * r) for r in (1, 2, 3)])
    return sum_four([array] + [swap_dp(array, 8 * r) for r in (1, 2, 3)])


def by_partner(array, index):
    return jnp.take(array, jnp.arange(array.shape[0]) ^ index, axis=0)


def shards(
    patches, image_ids, keep, labels, owners,
    soap_weight, soap_first, soap_second, stat_left, stat_right, basis_left, basis_right,
    embed_weight, embed_first, embed_second, head_weight, head_first, head_second,
    vectors, vector_first, vector_second,
):
    mp_index = lax.axis_index("mp")
    dp_index = lax.axis_index("dp")

    def tiled(flat_rows):
        return flat_rows.reshape(3, TILE, TILE)

    device, within = (owners // 3, owners % 3)
    partners = jnp.arange(4) ^ mp_index
    table = (device * 12 + within)[None, :] + 3 * partners[:, None]
    table = table.reshape(-1).astype(jnp.int32)
    relative = device ^ dp_index
    places = (((relative & 1) * 16 + (relative >> 1)) * 3 + within).astype(jnp.int32)
    my_slots = dp_index * 3 + jnp.arange(3)
    my_blocks = jnp.sum(
        jnp.where(owners[None, :] == my_slots[:, None], jnp.arange(96)[None, :], 0), axis=1
    )
    kind = my_blocks % 48
    grad_flips = (kind < 12).astype(jnp.int32)
    weight_flips = (kind < 12) | ((kind >= 16) & (kind < 32))

    master = tiled(soap_weight)
    low = master.astype(bf16)
    low = jnp.where(weight_flips[:, None, None], jnp.swapaxes(low, 1, 2), low)
    slots = lax.all_gather(pack_tile(low), ("dp", "mp"), axis=0, tiled=True)

    embed_parts = jnp.stack(gather_mp(embed_weight.astype(bf16)))
    embed_low = by_partner(embed_parts, mp_index).transpose(1, 0, 2).reshape(D, D)
    head_mine = head_weight.astype(bf16)
    head_low = by_partner(jnp.stack(gather_mp(head_mine)), mp_index).reshape(D, CLASSES)

    split_one = (2 * LAYERS + 1) * D
    gain_rows = vectors[:split_one].reshape(2 * LAYERS + 1, 1, D)
    head_gains = vectors[split_one : split_one + 2 * LAYERS * HD].reshape(LAYERS, 2, HD)
    class_bias = vectors[vectors.shape[0] - CLASSES :]

    tokens = by_partner(patches.reshape(4, OWN, D), mp_index)
    ids = by_partner(image_ids.reshape(4, OWN), mp_index)
    kept = by_partner(keep.reshape(4, OWN), mp_index) == 1
    query_ids = ids.reshape(1, TOKENS)
    key_ids = jnp.where(kept, ids, -1).reshape(TOKENS, 1)
    member_all = (image_ids[0, :, None] == jnp.arange(IMGS)[None, :]) & (keep[0, :, None] == 1)
    counts = jnp.sum(member_all.astype(f32), axis=0)
    present = (counts > 0).astype(f32)
    divisor = jnp.maximum(counts, 1.0)
    member = ((ids[0][:, None] == jnp.arange(IMGS)[None, :]) & kept[0][:, None]).astype(f32)
    image_total = total_dp(jnp.full((8, 128), jnp.sum(present), f32))[0, 0]

    first_tiles, second_tiles = (tiled(soap_first), tiled(soap_second))
    left_stat, right_stat = (tiled(stat_left), tiled(stat_right))
    left, right = (tiled(basis_left), tiled(basis_right))
    turned_first, left_old, right_old = run_soap_early(first_tiles, left_stat, right_stat, left, right)

    resid = jnp.dot(tokens[0], embed_low, preferred_element_type=f32).astype(bf16).astype(f32)
    act = (normalize(resid)[0] * gain_rows[0]).astype(bf16)

    weights = [layer_weights(table, slots, depth) for depth in range(LAYERS)]
    saved = []
    for depth in range(LAYERS):
        qkv, out, up, down = weights[depth]
        gains = head_gains[depth].T
        acts = gather_mp(act)
        pre, v, lse, o = run_attend_fwd(qkv, acts, gains, query_ids, key_ids)
        outs = trade_mp([o[r] for r in range(4)])
        mid, u, ct, resid_next, act = run_mix_fwd(
            resid, outs, out, gain_rows[2 * depth + 1], gain_rows[2 * depth + 2], up, down
        )
        saved.append((resid, acts, pre, v, lse, o, mid, u, gather_mp(ct)))
        resid = resid_next

    final, final_inverse = normalize(resid)
    gain_last = gain_rows[2 * LAYERS]
    pooled = total_mp(jnp.dot(member.T, final * gain_last, precision=highest)) / divisor[:, None]
    pooled_low = pooled.astype(bf16)
    logits = jnp.dot(pooled_low, head_low, preferred_element_type=f32) + class_bias
    row_max = jnp.max(logits, -1, keepdims=True)
    exps = jnp.exp(logits - row_max)
    row_sum = jnp.sum(exps, -1, keepdims=True)
    log_norm = row_max[:, 0] + jnp.log(row_sum[:, 0])
    onehot = (jnp.arange(CLASSES)[None, :] == labels.reshape(-1)[:, None]).astype(f32)
    local_loss = jnp.sum((log_norm - jnp.sum(onehot * logits, -1)) * present)
    loss_total = total_dp(jnp.full((8, 128), local_loss, f32))[0, 0]
    grad_logits = (exps / row_sum - onehot) * present[:, None] / image_total
    grad_bias = jnp.sum(grad_logits, 0)
    grad_logit_low = grad_logits.astype(bf16)
    pooled_mine = lax.dynamic_slice_in_dim(pooled_low, mp_index * TILE, TILE, 1)
    grad_head = jnp.dot(pooled_mine.T, grad_logit_low, preferred_element_type=f32)
    grad_pooled = jnp.dot(grad_logit_low, head_low.T, preferred_element_type=f32)
    grad_final = jnp.dot(member, grad_pooled / divisor[:, None], precision=highest)
    gain_grads = [jnp.sum(grad_final * final, 0)]
    grad = norm_back(grad_final, gain_last, final, final_inverse)
    grad_low = grad.astype(bf16)

    buffers = None
    head_gain_grads = []
    for depth in reversed(range(LAYERS)):
        qkv, out, up, down = weights[depth]
        resid, acts, pre, v, lse, o, mid, u, ct = saved[depth]
        gains = head_gains[depth].T
        lows = gather_mp(grad_low)
        du, mid_grad, mid_low, gain_two, do = run_mix_bwd(
            grad, grad_low, mid, u, gain_rows[2 * depth + 1], out, up, down
        )
        dos = trade_mp([do[r] for r in range(4)])
        dus = trade_mp([du[r] for r in range(4)])
        mid_lows = gather_mp(mid_low)
        dp, gain_heads = run_attend_bwd(pre, v, lse, dos, gains, query_ids, key_ids)
        dps = trade_mp([dp[r] for r in range(4)])
        grad, grad_low, gain_one = run_input_bwd(mid_grad, dps, qkv, resid, gain_rows[2 * depth])
        buffers = run_mlp_grads(depth, places, ct, dus, lows, mid_lows, o, up, buffers)
        buffers = run_qkv_grads(depth, places, dp, acts, buffers)
        gain_grads = [gain_one[0], gain_two[0]] + gain_grads
        head_gain_grads.insert(0, gain_heads.T)

    pieces = [
        lax.dynamic_slice_in_dim(grad_low, (mp_index ^ r) * TILE, TILE, 1) for r in range(4)
    ]
    columns = jnp.concatenate(trade_mp(pieces), axis=0)
    grad_embed = jnp.dot(tokens.reshape(TOKENS, D).T, columns, preferred_element_type=f32)
    embed_rows = pack_rows(grad_embed)
    head_rows = jnp.pad(grad_head, ((0, 0), (0, 24))).reshape(32, HEAD_ROWS, 128)
    vector_part = jnp.concatenate([jnp.concatenate(gain_grads), jnp.stack(head_gain_grads).reshape(-1)])
    vector_sum = jnp.concatenate([total_mp(vector_part), grad_bias, jnp.zeros((24,), f32)])
    vector_rows = jnp.pad(vector_sum.reshape(32, 160), ((0, 0), (0, 1536 - 160))).reshape(32, 12, 128)
    small = jnp.concatenate([embed_rows, head_rows, vector_rows], axis=1).astype(bf16)
    small = by_partner(small, dp_index).reshape(16, 2, SMALL, 128)
    keep_buffer = buffers[0].at[:, 3 * PACK :].set(small[:, 0])
    send_buffer = buffers[1].at[:, 3 * PACK :].set(small[:, 1])

    both = keep_buffer.astype(f32) + swap_dp(send_buffer, 1).astype(f32)
    both = both.reshape(4, 4, ROWS, 128)
    both = sum_four([both[0]] + [swap_dp(both[r].astype(bf16), 8 * r).astype(f32) for r in (1, 2, 3)])
    mine = sum_four([both[0]] + [swap_dp(both[r].astype(bf16), 2 * r).astype(f32) for r in (1, 2, 3)])
    mine_slots = mine[: 3 * PACK]
    share = mine[3 * PACK :]
    cut_at = EMBED_ROWS + HEAD_ROWS
    local_squares = (
        jnp.sum(mine_slots * mine_slots)
        + jnp.sum(share[:cut_at] * share[:cut_at])
        + jnp.sum(share[cut_at:] * share[cut_at:]) * 0.25
    )
    squares = total_dp(total_mp(jnp.full((8, 128), local_squares, f32)))[0, 0]
    grad_norm = jnp.sqrt(squares)
    factor = clip_limit / jnp.maximum(grad_norm, clip_limit)

    grad_tiles, turned, left_new, right_new, gram_left, gram_right = run_soap_mid(
        grad_flips, mine_slots.reshape(3, PACK, 128), left, right
    )
    soap_new = run_soap_late(
        factor.reshape(1, 1), grad_tiles, first_tiles, second_tiles, left_stat, right_stat, left, right, master,
        turned, turned_first, left_old, right_old, left_new, right_new, gram_left, gram_right,
    )
    soap_new = [entry.reshape(3, TILE * TILE) for entry in soap_new]

    shares = jnp.stack([share] + [swap_dp(share, 2 * r) for r in (1, 2, 3)])
    shares = jnp.stack([shares] + [swap_dp(shares, 8 * r) for r in (1, 2, 3)])
    shares = jnp.stack([shares, swap_dp(shares, 1)], axis=2).reshape(32, SMALL, 128)
    shares = by_partner(shares, dp_index)
    grad_embed = unpack_rows(shares[:, :EMBED_ROWS])
    grad_head = shares[:, EMBED_ROWS:cut_at].reshape(TILE, 1024)[:, :CLASSES]
    grad_vector = shares[:, cut_at:].reshape(32, 1536)[:, :160].reshape(-1)[: vectors.shape[0]]
    embed_new = adamw(
        embed_weight, grad_embed * factor, embed_first, embed_second, matrix_rate, weight_decay
    )
    head_new = adamw(
        head_weight, grad_head * factor, head_first, head_second, matrix_rate, weight_decay
    )
    vector_new = adamw(vectors, grad_vector * factor, vector_first, vector_second, vector_rate, 0.0)
    return (loss_total, image_total, grad_norm, *soap_new, *embed_new, *head_new, *vector_new)


def pack_rows(array):
    rows = array.reshape(32, 24, TILE)
    right = rows[:, :, 128:]
    right = jnp.concatenate([right[:, :12], right[:, 12:]], axis=2)
    return jnp.concatenate([rows[:, :, :128], right], axis=1)


def unpack_rows(packed):
    right = packed[:, 24:]
    right = jnp.concatenate([right[:, :, :64], right[:, :, 64:]], axis=1)
    return jnp.concatenate([packed[:, :24], right], axis=2).reshape(D, TILE)


def solution(mesh):
    by_slot = P(("dp", "mp"), None)
    columns = P(None, "mp")
    rows = P("mp", None)
    return jax.shard_map(
        shards,
        mesh=mesh,
        in_specs=(P("dp", None, None), P("dp", None), P("dp", None), P("dp", None), P())
        + (by_slot,) * 7
        + (columns,) * 3
        + (rows,) * 3
        + (P(),) * 3,
        out_specs=(P(),) * 3 + (by_slot,) * 8 + (columns,) * 3 + (rows,) * 3 + (P(),) * 3,
        check_vma=False,
    )
```

time: 1620 us -> 761 us (0.47)
  other arithmetic: 424 us -> 49.9 us
  blocking collectives: 287 us -> 0 us
  waiting for transfers between devices: 455 us -> 189 us
  Pallas kernels: 0 us -> 237 us
  local copies, waits for them, and re-layouts: 258 us -> 95.7 us
  matrix products: 167 us -> 8.32 us
  starting transfers between devices: 1.38 us -> 149 us
    psum x9 -> x0, waiting for transfers between devices: 374 us -> none  [the longest x8 372 us: branch_sum(): return lax.psum(partial_sum, 'mp')]
    another operation x37 -> x10, other arithmetic: 309 us -> 9.17 us  [the longest x16 174 us: power_step(): factor = jnp.linalg.cholesky(gram_mat)]
    psum x5 -> x0, blocking collectives: 278 us -> none  [the longest x2 188 us: shards(): image_total, loss_total = lax.psum((local_count, local_loss), 'dp')]
    pallas_call x0 -> x25, Pallas kernels: none -> 237 us  [the longest x1 43.5 us: run_soap_late(): pl.pallas_call(soap_late, in_specs=[SM] + [VM] * 16, out_specs=[VM] * 8,...]
    ppermute x0 -> x101, starting transfers between devices: none -> 149 us  [swap(): return lax.ppermute(array, axis, [(i, i ^ r) for i in range(size)])]
    dot_general x51 -> x7, matrix products: 144 us -> 8.32 us  [the longest x1 1.71 us: shards(): jnp.dot(pooled_mine.T, grad_logit_low, preferred_element_type=f32)]
    ppermute x0 -> x101, waiting for transfers between devices: none -> 112 us  [swap(): return lax.ppermute(array, axis, [(i, i ^ r) for i in range(size)])]
    another operation x22 -> x3, local copies, waits for them, and re-layouts: 55.7 us -> 0.15 us  [the longest x1 0.14 us: shards(): jnp.stack([shares, swap_dp(shares, 1)], axis=2).reshape(32, SMALL, 128)]
  transfers between devices with their start and end apart: 11 -> 102, of which waited for: 10 -> 30; matrix products, arithmetic and copies ran while one was open for 13% -> 12% of each run, Pallas kernels for 0% -> 29%
where the time goes in v1:
time: 761 us; the launch traced here: 749 us
  Pallas kernels  237 us (31%)
  waiting for transfers between devices  189 us (25%)
  starting transfers between devices  149 us (20%)
  local copies, waits for them, and re-layouts  95.7 us (13%)
  other arithmetic  49.9 us (7%)
  between operations  20.8 us (3%)
  matrix products  8.32 us (1%)
    ppermute x101, starting transfers between devices, swap(): return lax.ppermute(array, axis, [(i, i ^ r) for i in range(size)])  149 us
    ppermute x101, waiting for transfers between devices, swap(): return lax.ppermute(array, axis, [(i, i ^ r) for i in range(size)])  112 us
    all_gather x1, waiting for transfers between devices, shards(): slots = lax.all_gather(pack_tile(low), ('dp', 'mp'), axis=0, tiled=True)  77.2 us
    pallas_call x1, Pallas kernels, run_soap_late(): pl.pallas_call(soap_late, in_specs=[SM] + [VM] * 16, out_specs=[VM] * 8,...  43.5 us
    unnamed x370, local copies, waits for them, and re-layouts  41 us
    pallas_call x8, Pallas kernels, assemble(): pl.pallas_call(kernel, grid_spec=pltpu.PrefetchScalarGridSpec(num_scalar_...  40.2 us
    pallas_call x2, Pallas kernels, run_attend_bwd(): pl.pallas_call(attend_bwd, in_specs=[VM] * 10, out_specs=[VM] * 2, out_sh...  38.3 us
    pallas_call x4, Pallas kernels, grads_call(): pl.pallas_call(kernel, grid=(1,), in_specs=[SM] + specs + [ANY] * len(giv...  29.2 us
  transfers between devices with their start and end apart: 102, of which 30 were waited for; matrix products, arithmetic and copies ran while one was open for 12% of the time, Pallas kernels for 29%

profile of v1, /device:TPU:1, one launch (start us, length us, event | category | flops | bytes accessed | tf_op | source)
XLA Modules:
  0.0 748.8 jit_solution(12926644159128278660)
XLA Ops:
  49.6 77.2 %all-gather.2.cloned.1.call-done.refs_0_.refs_1_.refs_2_.refs_3_.refs_4_.refs_5_.refs_6_.refs_7_.refs_8_.refs_9_.refs_10_.refs_11_.refs_12_.refs_13_.refs_14_.refs_15_ = bf16[384,288,128]{2,1,0:T(8,128)(2,1)} async-done(((bf16[3,288,128]{2,1,0:T(8,128)(2,1)}), bf16[384,288,128]{2,1,0:T(8,128)(2,1)}) %all-gather.2.cloned.1.call-update) | async-done | bytes 28311568 | tf_op jit(solution)/shard_map/all_gather | solution.py:717
  126.8 5.0 assemble.8.w_ref
  135.7 13.5 %attend_fwd.2 = (f32[384,1024]{1,0:T(8,128)S(1)}, bf16[192,1024]{1,0:T(8,128)(2,1)S(1)}, f32[3,1,1024]{2,1,0:T(1,128)S(1)}, bf16[4,192,256]{2,1,0:T(8,128)(2,1)S(1)}) custom-call(bf16[4,576,768]{2,1,0:T(8,128)(2,1)} %copy-done.3, bf16[256,768]{1,0:T(8,128)(2,1)S(1)} %multiply_convert_fusion.a0.refs_2_, ...), custom_call_target="tpu_custom_call" | custom-call | flops 10000000000 | bytes 6000000 | tf_op jit(solution)/shard_map/attend_fwd/pallas_call | solution.py:206
  157.3 5.9 assemble.10.up_ref.refs_18_
  165.4 5.9 assemble.11.down_ref
  176.8 10.4 %mix_fwd.2 = (f32[256,768]{1,0:T(8,128)S(1)}, f32[4,256,768]{2,1,0:T(8,128)}, bf16[768,256]{1,0:T(8,128)(2,1)S(1)}, f32[256,768]{1,0:T(8,128)S(1)}, bf16[256,768]{1,0:T(8,128)(2,1)S(1)}) custom-call(f32[256,768]{1,0:T(8,128)S(1)} %copy-done.6, bf16[192,256]{1,0:T(8,128)(2,1)S(1)} %get-tuple-element.307.o0, bf16[192,256]{1,0:T(8,128)(2,1)} %collective-permute-done.6.o1, ...), custom_call_target="tpu_custom_call" | custom-call | flops 6000000000 | bytes 17000000 | tf_op jit(solution)/shard_map/mix_fwd/pallas_call | solution.py:337
  202.0 5.0 assemble.12.w_ref
  209.6 13.5 %attend_fwd.3 = (f32[384,1024]{1,0:T(8,128)S(1)}, bf16[192,1024]{1,0:T(8,128)(2,1)S(1)}, f32[3,1,1024]{2,1,0:T(1,128)S(1)}, bf16[4,192,256]{2,1,0:T(8,128)(2,1)S(1)}) custom-call(bf16[4,576,768]{2,1,0:T(8,128)(2,1)} %copy-done.4, bf16[256,768]{1,0:T(8,128)(2,1)S(1)} %get-tuple-element.108.a0.refs_2_, bf16[256,768]{1,0:T(8,128)(2,1)S(1)} %collective-permute-done.9.a1.refs_3_, ...), custom_call_target="tpu_custom_call" | custom-call | flops 10000000000 | bytes 6000000 | tf_op jit(solution)/shard_map/attend_fwd/pallas_call | solution.py:206
  234.6 5.9 assemble.14.up_ref.refs_18_
  242.7 5.9 assemble.15.down_ref
  254.0 10.2 %mix_fwd.3 = (f32[256,768]{1,0:T(8,128)S(1)}, f32[4,256,768]{2,1,0:T(8,128)}, bf16[768,256]{1,0:T(8,128)(2,1)}, f32[256,768]{1,0:T(8,128)S(1)}, bf16[256,768]{1,0:T(8,128)(2,1)}) custom-call(f32[256,768]{1,0:T(8,128)S(1)} %get-tuple-element.107.x_ref, bf16[192,256]{1,0:T(8,128)(2,1)S(1)} %get-tuple-element.303.o0, ...), custom_call_target="tpu_custom_call" | custom-call | flops 6000000000 | bytes 17000000 | tf_op jit(solution)/shard_map/mix_fwd/pallas_call | solution.py:337
  278.4 10.4 %mix_bwd.2 = (bf16[4,256,768]{2,1,0:T(8,128)(2,1)}, f32[256,768]{1,0:T(8,128)S(1)}, bf16[256,768]{1,0:T(8,128)(2,1)}, f32[1,768]{1,0:T(1,128)S(1)}, bf16[4,192,256]{2,1,0:T(8,128)(2,1)S(1)}) custom-call(f32[256,768]{1,0:T(8,128)S(1)} %get-tuple-element.246.g_ref, bf16[256,768]{1,0:T(8,128)(2,1)S(1)} %get-tuple-element.245.low_ref.refs_9_, ...), custom_call_target="tpu_custom_call" | custom-call | flops 6000000000 | bytes 17000000 | tf_op jit(solution)/shard_map/mix_bwd/pallas_call | solution.py:379
  295.4 19.2 %attend_bwd.2 = (bf16[4,576,256]{2,1,0:T(8,128)(2,1)S(1)}, f32[64,2]{1,0:T(8,128)S(1)}) custom-call(f32[384,1024]{1,0:T(8,128)S(1)} %copy-done.70, bf16[192,1024]{1,0:T(8,128)(2,1)S(1)} %copy-done.74, f32[3,1,1024]{2,1,0:T(1,128)S(1)} %copy-done.78, bf16[192,256]{1,0:T(8,128)(2,1)S(1)} %get-tuple-element.299.g0, ...), custom_call_target="tpu_custom_call" | custom-call | flops 20000000000 | bytes 6000000 | tf_op jit(solution)/shard_map/attend_bwd/pallas_call | solution.py:282
  343.4 5.5 collective-permute-done.61.refs_8_
  350.8 10.1 %mix_bwd.3 = (bf16[4,256,768]{2,1,0:T(8,128)(2,1)}, f32[256,768]{1,0:T(8,128)S(1)}, bf16[256,768]{1,0:T(8,128)(2,1)S(1)}, f32[1,768]{1,0:T(1,128)S(1)}, bf16[4,192,256]{2,1,0:T(8,128)(2,1)S(1)}) custom-call(f32[256,768]{1,0:T(8,128)S(1)} %get-tuple-element.122.g_ref, bf16[256,768]{1,0:T(8,128)(2,1)S(1)} %get-tuple-element.123.low_ref.refs_9_, ...), custom_call_target="tpu_custom_call" | custom-call | flops 6000000000 | bytes 17000000 | tf_op jit(solution)/shard_map/mix_bwd/pallas_call | solution.py:379
  367.8 7.1 collective-permute-done.63.refs_11_
  377.5 5.1 collective-permute-done.64.refs_12_
  383.4 10.6 %mlp_grads.2 = (bf16[16,960,128]{2,1,0:T(8,128)(2,1)}, bf16[16,960,128]{2,1,0:T(8,128)(2,1)}) custom-call(s32[96]{0:T(128)} %get-tuple-element.247.refs_0_, bf16[768,256]{1,0:T(8,128)(2,1)} %get-tuple-element.131.refs_1_, bf16[768,256]{1,0:T(8,128)(2,1)} %collective-permute-done.56.refs_2_, bf16[768,256]{1,0:T(8,128)(2,1)} %collective-permute-done.57.refs_3_, ...), custom_call_target="tpu_custom_call" | custom-call | flops 4000000000 | bytes 10000000 | tf_op jit(solution)/shard_map/mlp_grads/pallas_call | solution.py:486
  396.7 19.1 %attend_bwd.3 = (bf16[4,576,256]{2,1,0:T(8,128)(2,1)S(1)}, f32[64,2]{1,0:T(8,128)S(1)}) custom-call(f32[384,1024]{1,0:T(8,128)S(1)} %copy-done.68, bf16[192,1024]{1,0:T(8,128)(2,1)S(1)} %copy-done.72, f32[3,1,1024]{2,1,0:T(1,128)S(1)} %copy-done.76, bf16[192,256]{1,0:T(8,128)(2,1)S(1)} %get-tuple-element.295.g0, ...), custom_call_target="tpu_custom_call" | custom-call | flops 20000000000 | bytes 6000000 | tf_op jit(solution)/shard_map/attend_bwd/pallas_call | solution.py:282
  432.2 4.9 input_bwd.3
  462.4 4.8 collective-permute-done.50.refs_10_
  468.8 8.0 %collective-permute-done.51.refs_11_ = bf16[256,768]{1,0:T(8,128)(2,1)S(1)} collective-permute-done((bf16[256,768]{1,0:T(8,128)(2,1)S(1)}, bf16[256,768]{1,0:T(8,128)(2,1)S(1)}, u32[]{:S(2)}, u32[]{:S(2)}) %collective-permute-start.51) | collective-permute-done | bytes 393248 | tf_op jit(solution)/shard_map/ppermute | solution.py:651
  476.9 4.6 collective-permute-done.52.refs_12_
  482.2 10.5 %mlp_grads.3 = (bf16[16,960,128]{2,1,0:T(8,128)(2,1)}, bf16[16,960,128]{2,1,0:T(8,128)(2,1)}) custom-call(s32[96]{0:T(128)} %get-tuple-element.247.refs_0_, bf16[768,256]{1,0:T(8,128)(2,1)} %copy-done.40, bf16[768,256]{1,0:T(8,128)(2,1)} %collective-permute-done.44.refs_2_, ...), custom_call_target="tpu_custom_call", output_to_operand_aliasing={{0}: (19, {}), {1}: (20, {})} | custom-call | flops 4000000000 | bytes 10000000 | tf_op jit(solution)/shard_map/mlp_grads/pallas_call | solution.py:486
  506.2 18.1 %collective-permute-start.77 = (bf16[16,960,128]{2,1,0:T(8,128)(2,1)}, bf16[16,960,128]{2,1,0:T(8,128)(2,1)S(1)}, u32[]{:S(2)}, u32[]{:S(2)}) collective-permute-start(bf16[16,960,128]{2,1,0:T(8,128)(2,1)} %get-tuple-element.281), channel_id=1, source_target_pairs={{0,4},{4,0},{8,12},{12,8},{16,20},{20,16},{24,28},{28,24},{32,36},... | collective-permute-start | bytes 11796488 | tf_op jit(solution)/shard_map/ppermute | solution.py:651
  524.3 6.6 collective-permute-done.77
  530.9 6.6 convert_add_fusion
  549.4 13.2 %collective-permute-done.78 = bf16[4,960,128]{2,1,0:T(8,128)(2,1)} collective-permute-done((bf16[4,960,128]{2,1,0:T(8,128)(2,1)}, bf16[4,960,128]{2,1,0:T(8,128)(2,1)}, u32[]{:S(2)}, u32[]{:S(2)}) %collective-permute-start.78) | collective-permute-done | bytes 983072 | tf_op jit(solution)/shard_map/ppermute | solution.py:651
  562.6 22.4 %collective-permute-done.79 = bf16[4,960,128]{2,1,0:T(8,128)(2,1)} collective-permute-done((bf16[4,960,128]{2,1,0:T(8,128)(2,1)}, bf16[4,960,128]{2,1,0:T(8,128)(2,1)}, u32[]{:S(2)}, u32[]{:S(2)}) %collective-permute-start.79) | collective-permute-done | bytes 983072 | tf_op jit(solution)/shard_map/ppermute | solution.py:651
  624.6 5.7 collective-permute-start.87
  653.1 6.0 soap_mid.1
  665.4 43.5 %soap_late.1 = (f32[3,192,192]{2,1,0:T(8,128)}, f32[3,192,192]{2,1,0:T(8,128)}, f32[3,192,192]{2,1,0:T(8,128)}, f32[3,192,192]{2,1,0:T(8,128)}, f32[3,192,192]{2...) custom-call(f32[1,1]{1,0:T(1,128)} %bitcast.73.f_ref, ...), custom_call_target="tpu_custom_call" | custom-call | flops 1000000000 | bytes 10000000 | tf_op jit(solution)/shard_map/soap_late/pallas_call | solution.py:631
  (747 shorter events, 327.4 us)
Async XLA Ops:
  7.2 119.6 %all-gather.2.cloned.1.call-start = ((), (), s32[]{:S(2)}) async-start(), calls=%async_computation | async-start | bytes 28532736 | tf_op jit(solution)/shard_map/all_gather | solution.py:717
  38.2 95.4 %collective-permute-start.3 = (bf16[256,768]{1,0:T(8,128)(2,1)S(1)}, bf16[256,768]{1,0:T(8,128)(2,1)S(1)}, u32[]{:S(2)}, u32[]{:S(2)}) collective-permute-start(bf16[256,768]{1,0:T(8,128)(2,1)S(1)} %multiply_convert_fusion.a0.refs_2_), channel_id=1, source_target_pairs={{0,1},{1,0},{2,3},{3,2},{4,5},{5,4},{6,7},{7,6},{8,9},{9,8},{10,11... | collective-permute-start | bytes 1179656 | tf_op jit(solution)/shard_map/ppermute | solution.py:651
  38.4 97.3 %collective-permute-start.4 = (bf16[256,768]{1,0:T(8,128)(2,1)S(1)}, bf16[256,768]{1,0:T(8,128)(2,1)S(1)}, u32[]{:S(2)}, u32[]{:S(2)}) collective-permute-start(bf16[256,768]{1,0:T(8,128)(2,1)S(1)} %multiply_convert_fusion.a0.refs_2_), channel_id=1, source_target_pairs={{0,2},{1,3},{2,0},{3,1},{4,6},{5,7},{6,4},{7,5},{8,10},{9,11},{10,... | collective-permute-start | bytes 1179656 | tf_op jit(solution)/shard_map/ppermute | solution.py:651
  42.1 93.6 %collective-permute-start.5 = (bf16[256,768]{1,0:T(8,128)(2,1)S(1)}, bf16[256,768]{1,0:T(8,128)(2,1)S(1)}, u32[]{:S(2)}, u32[]{:S(2)}) collective-permute-start(bf16[256,768]{1,0:T(8,128)(2,1)S(1)} %multiply_convert_fusion.a0.refs_2_), channel_id=1, source_target_pairs={{0,3},{1,2},{2,1},{3,0},{4,7},{5,6},{6,5},{7,4},{8,11},{9,10},{10,... | collective-permute-start | bytes 1179656 | tf_op jit(solution)/shard_map/ppermute | solution.py:651
  44.6 108.8 %collective-permute-start.29 = (f32[8,128]{1,0:T(8,128)S(1)}, f32[8,128]{1,0:T(8,128)S(1)}, u32[]{:S(2)}, u32[]{:S(2)}) collective-permute-start(f32[8,128]{1,0:T(8,128)S(1)} %broadcast_add_fusion), channel_id=1, source_target_pairs={{0,8},{4,12},{8,0},{12,4},{16,24},{20,28},{24,16},{28,20},{32,40},... | collective-permute-start | bytes 12296 | tf_op jit(solution)/shard_map/ppermute | solution.py:651
  46.3 107.7 %collective-permute-start.30 = (f32[8,128]{1,0:T(8,128)S(1)}, f32[8,128]{1,0:T(8,128)S(1)}, u32[]{:S(2)}, u32[]{:S(2)}) collective-permute-start(f32[8,128]{1,0:T(8,128)S(1)} %broadcast_add_fusion), channel_id=1, source_target_pairs={{0,16},{4,20},{8,24},{12,28},{16,0},{20,4},{24,8},{28,12},{32,48},... | collective-permute-start | bytes 12296 | tf_op jit(solution)/shard_map/ppermute | solution.py:651
  150.1 26.6 %collective-permute-start.6 = (bf16[192,256]{1,0:T(8,128)(2,1)}, bf16[192,256]{1,0:T(8,128)(2,1)}, u32[]{:S(2)}, u32[]{:S(2)}) collective-permute-start(bf16[192,256]{1,0:T(8,128)(2,1)} %get-tuple-element.306), channel_id=1, source_target_pairs={{0,1},{1,0},{2,3},{3,2},{4,5},{5,4},{6,7},{7,6},{8,9},{9,8},{10,11... | collective-permute-start | bytes 294920 | tf_op jit(solution)/shard_map/ppermute | solution.py:651
  151.0 25.8 %collective-permute-start.7 = (bf16[192,256]{1,0:T(8,128)(2,1)}, bf16[192,256]{1,0:T(8,128)(2,1)}, u32[]{:S(2)}, u32[]{:S(2)}) collective-permute-start(bf16[192,256]{1,0:T(8,128)(2,1)} %get-tuple-element.305), channel_id=1, source_target_pairs={{0,2},{1,3},{2,0},{3,1},{4,6},{5,7},{6,4},{7,5},{8,10},{9,11},{10,... | collective-permute-start | bytes 294920 | tf_op jit(solution)/shard_map/ppermute | solution.py:651
  155.9 37.8 %collective-permute-start.32 = (f32[8,128]{1,0:T(8,128)}, f32[8,128]{1,0:T(8,128)}, u32[]{:S(2)}, u32[]{:S(2)}) collective-permute-start(f32[8,128]{1,0:T(8,128)} %add_add_fusion.4), channel_id=1, source_target_pairs={{0,32},{4,36},{8,40},{12,44},{16,48},{20,52},{24,56},{28,60},{32,0... | collective-permute-start | bytes 12296 | tf_op jit(solution)/shard_map/ppermute | solution.py:651
  197.6 31.4 %collective-permute-start.18 = (bf16[192,1000]{1,0:T(8,128)(2,1)}, bf16[192,1000]{1,0:T(8,128)(2,1)S(1)}, u32[]{:S(2)}, u32[]{:S(2)}) collective-permute-start(bf16[192,1000]{1,0:T(8,128)(2,1)} %convert_element_type.95), channel_id=1, source_target_pairs={{0,1},{1,0},{2,3},{3,2},{4,5},{5,4},{6,7},{7,6},{8,9},{9,8},{10,11... | collective-permute-start | bytes 1152008 | tf_op jit(solution)/shard_map/ppermute | solution.py:651
  198.4 31.5 %collective-permute-start.19 = (bf16[192,1000]{1,0:T(8,128)(2,1)}, bf16[192,1000]{1,0:T(8,128)(2,1)S(1)}, u32[]{:S(2)}, u32[]{:S(2)}) collective-permute-start(bf16[192,1000]{1,0:T(8,128)(2,1)} %convert_element_type.95), channel_id=1, source_target_pairs={{0,2},{1,3},{2,0},{3,1},{4,6},{5,7},{6,4},{7,5},{8,10},{9,11},{10,... | collective-permute-start | bytes 1152008 | tf_op jit(solution)/shard_map/ppermute | solution.py:651
  225.7 28.3 %collective-permute-start.12 = (bf16[192,256]{1,0:T(8,128)(2,1)}, bf16[192,256]{1,0:T(8,128)(2,1)}, u32[]{:S(2)}, u32[]{:S(2)}) collective-permute-start(bf16[192,256]{1,0:T(8,128)(2,1)} %get-tuple-element.302), channel_id=1, source_target_pairs={{0,1},{1,0},{2,3},{3,2},{4,5},{5,4},{6,7},{7,6},{8,9},{9,8},{10,11... | collective-permute-start | bytes 294920 | tf_op jit(solution)/shard_map/ppermute | solution.py:651
  225.7 28.3 %collective-permute-start.13 = (bf16[192,256]{1,0:T(8,128)(2,1)}, bf16[192,256]{1,0:T(8,128)(2,1)}, u32[]{:S(2)}, u32[]{:S(2)}) collective-permute-start(bf16[192,256]{1,0:T(8,128)(2,1)} %get-tuple-element.301), channel_id=1, source_target_pairs={{0,2},{1,3},{2,0},{3,1},{4,6},{5,7},{6,4},{7,5},{8,10},{9,11},{10,... | collective-permute-start | bytes 294920 | tf_op jit(solution)/shard_map/ppermute | solution.py:651
  228.9 25.0 %collective-permute-start.14 = (bf16[192,256]{1,0:T(8,128)(2,1)}, bf16[192,256]{1,0:T(8,128)(2,1)}, u32[]{:S(2)}, u32[]{:S(2)}) collective-permute-start(bf16[192,256]{1,0:T(8,128)(2,1)} %get-tuple-element.300), channel_id=1, source_target_pairs={{0,3},{1,2},{2,1},{3,0},{4,7},{5,6},{6,5},{7,4},{8,11},{9,10},{10,... | collective-permute-start | bytes 294920 | tf_op jit(solution)/shard_map/ppermute | solution.py:651
  293.3 29.2 %collective-permute-start.56 = (bf16[768,256]{1,0:T(8,128)(2,1)}, bf16[768,256]{1,0:T(8,128)(2,1)}, u32[]{:S(2)}, u32[]{:S(2)}) collective-permute-start(bf16[768,256]{1,0:T(8,128)(2,1)} %get-tuple-element.131.refs_1_), channel_id=1, source_target_pairs={{0,1},{1,0},{2,3},{3,2},{4,5},{5,4},{6,7},{7,6},{8,9},{9,8},{10,11... | collective-permute-start | bytes 1179656 | tf_op jit(solution)/shard_map/ppermute | solution.py:651
  293.3 31.3 %collective-permute-start.57 = (bf16[768,256]{1,0:T(8,128)(2,1)}, bf16[768,256]{1,0:T(8,128)(2,1)}, u32[]{:S(2)}, u32[]{:S(2)}) collective-permute-start(bf16[768,256]{1,0:T(8,128)(2,1)} %get-tuple-element.131.refs_1_), channel_id=1, source_target_pairs={{0,2},{1,3},{2,0},{3,1},{4,6},{5,7},{6,4},{7,5},{8,10},{9,11},{10,... | collective-permute-start | bytes 1179656 | tf_op jit(solution)/shard_map/ppermute | solution.py:651
  348.9 26.0 %collective-permute-start.63 = (bf16[256,768]{1,0:T(8,128)(2,1)S(1)}, bf16[256,768]{1,0:T(8,128)(2,1)S(1)}, u32[]{:S(2)}, u32[]{:S(2)}) collective-permute-start(bf16[256,768]{1,0:T(8,128)(2,1)S(1)} %copy-done.36), channel_id=1, source_target_pairs={{0,2},{1,3},{2,0},{3,1},{4,6},{5,7},{6,4},{7,5},{8,10},{9,11},{10,... | collective-permute-start | bytes 1179656 | tf_op jit(solution)/shard_map/ppermute | solution.py:651
  350.8 31.8 %collective-permute-start.64 = (bf16[256,768]{1,0:T(8,128)(2,1)S(1)}, bf16[256,768]{1,0:T(8,128)(2,1)S(1)}, u32[]{:S(2)}, u32[]{:S(2)}) collective-permute-start(bf16[256,768]{1,0:T(8,128)(2,1)S(1)} %copy-done.36), channel_id=1, source_target_pairs={{0,3},{1,2},{2,1},{3,0},{4,7},{5,6},{6,5},{7,4},{8,11},{9,10},{10,... | collective-permute-start | bytes 1179656 | tf_op jit(solution)/shard_map/ppermute | solution.py:651
  361.0 66.0 %collective-permute-start.44 = (bf16[768,256]{1,0:T(8,128)(2,1)S(1)}, bf16[768,256]{1,0:T(8,128)(2,1)}, u32[]{:S(2)}, u32[]{:S(2)}) collective-permute-start(bf16[768,256]{1,0:T(8,128)(2,1)S(1)} %copy-done.41), channel_id=1, source_target_pairs={{0,1},{1,0},{2,3},{3,2},{4,5},{5,4},{6,7},{7,6},{8,9},{9,8},{10,11... | collective-permute-start | bytes 1179656 | tf_op jit(solution)/shard_map/ppermute | solution.py:651
  365.9 62.4 %collective-permute-start.45 = (bf16[768,256]{1,0:T(8,128)(2,1)S(1)}, bf16[768,256]{1,0:T(8,128)(2,1)}, u32[]{:S(2)}, u32[]{:S(2)}) collective-permute-start(bf16[768,256]{1,0:T(8,128)(2,1)S(1)} %copy-done.41), channel_id=1, source_target_pairs={{0,2},{1,3},{2,0},{3,1},{4,6},{5,7},{6,4},{7,5},{8,10},{9,11},{10,... | collective-permute-start | bytes 1179656 | tf_op jit(solution)/shard_map/ppermute | solution.py:651
  367.7 26.3 %collective-permute-start.41 = (bf16[192,256]{1,0:T(8,128)(2,1)S(1)}, bf16[192,256]{1,0:T(8,128)(2,1)S(1)}, u32[]{:S(2)}, u32[]{:S(2)}) collective-permute-start(bf16[192,256]{1,0:T(8,128)(2,1)S(1)} %get-tuple-element.294), channel_id=1, source_target_pairs={{0,1},{1,0},{2,3},{3,2},{4,5},{5,4},{6,7},{7,6},{8,9},{9,8},{10,11... | collective-permute-start | bytes 294920 | tf_op jit(solution)/shard_map/ppermute | solution.py:651
  444.6 32.3 %collective-permute-start.51 = (bf16[256,768]{1,0:T(8,128)(2,1)S(1)}, bf16[256,768]{1,0:T(8,128)(2,1)S(1)}, u32[]{:S(2)}, u32[]{:S(2)}) collective-permute-start(bf16[256,768]{1,0:T(8,128)(2,1)S(1)} %copy-done.47), channel_id=1, source_target_pairs={{0,2},{1,3},{2,0},{3,1},{4,6},{5,7},{6,4},{7,5},{8,10},{9,11},{10,... | collective-permute-start | bytes 1179656 | tf_op jit(solution)/shard_map/ppermute | solution.py:651
  450.4 31.1 %collective-permute-start.52 = (bf16[256,768]{1,0:T(8,128)(2,1)S(1)}, bf16[256,768]{1,0:T(8,128)(2,1)S(1)}, u32[]{:S(2)}, u32[]{:S(2)}) collective-permute-start(bf16[256,768]{1,0:T(8,128)(2,1)S(1)} %copy-done.47), channel_id=1, source_target_pairs={{0,3},{1,2},{2,1},{3,0},{4,7},{5,6},{6,5},{7,4},{8,11},{9,10},{10,... | collective-permute-start | bytes 1179656 | tf_op jit(solution)/shard_map/ppermute | solution.py:651
  460.1 36.7 %collective-permute-start.74 = (f32[4096]{0:T(1024)}, f32[4096]{0:T(1024)S(1)}, u32[]{:S(2)}, u32[]{:S(2)}) collective-permute-start(f32[4096]{0:T(1024)} %constant_dynamic-update-slice_fusion), channel_id=1, source_target_pairs={{0,1},{1,0},{2,3},{3,2},{4,5},{5,4},{6,7},{7,6},{8,9},{9,8},{10,11... | collective-permute-start | bytes 49160 | tf_op jit(solution)/shard_map/ppermute | solution.py:651
  461.2 37.1 %collective-permute-start.75 = (f32[4096]{0:T(1024)}, f32[4096]{0:T(1024)S(1)}, u32[]{:S(2)}, u32[]{:S(2)}) collective-permute-start(f32[4096]{0:T(1024)} %constant_dynamic-update-slice_fusion), channel_id=1, source_target_pairs={{0,2},{1,3},{2,0},{3,1},{4,6},{5,7},{6,4},{7,5},{8,10},{9,11},{10,... | collective-permute-start | bytes 49160 | tf_op jit(solution)/shard_map/ppermute | solution.py:651
  467.2 31.1 %collective-permute-start.76 = (f32[4096]{0:T(1024)}, f32[4096]{0:T(1024)S(1)}, u32[]{:S(2)}, u32[]{:S(2)}) collective-permute-start(f32[4096]{0:T(1024)} %constant_dynamic-update-slice_fusion), channel_id=1, source_target_pairs={{0,3},{1,2},{2,1},{3,0},{4,7},{5,6},{6,5},{7,4},{8,11},{9,10},{10,... | collective-permute-start | bytes 49160 | tf_op jit(solution)/shard_map/ppermute | solution.py:651
  506.2 24.7 %collective-permute-start.77 = (bf16[16,960,128]{2,1,0:T(8,128)(2,1)}, bf16[16,960,128]{2,1,0:T(8,128)(2,1)S(1)}, u32[]{:S(2)}, u32[]{:S(2)}) collective-permute-start(bf16[16,960,128]{2,1,0:T(8,128)(2,1)} %get-tuple-element.281), channel_id=1, source_target_pairs={{0,4},{4,0},{8,12},{12,8},{16,20},{20,16},{24,28},{28,24},{32,36},... | collective-permute-start | bytes 11796488 | tf_op jit(solution)/shard_map/ppermute | solution.py:651
  539.3 45.7 %collective-permute-start.79 = (bf16[4,960,128]{2,1,0:T(8,128)(2,1)}, bf16[4,960,128]{2,1,0:T(8,128)(2,1)}, u32[]{:S(2)}, u32[]{:S(2)}) collective-permute-start(bf16[4,960,128]{2,1,0:T(8,128)(2,1)} %get-tuple-element.256), channel_id=1, source_target_pairs={{0,64},{4,68},{8,72},{12,76},{16,80},{20,84},{24,88},{28,92},{32,9... | collective-permute-start | bytes 2949128 | tf_op jit(solution)/shard_map/ppermute | solution.py:651
  542.1 45.3 %collective-permute-start.80 = (bf16[4,960,128]{2,1,0:T(8,128)(2,1)}, bf16[4,960,128]{2,1,0:T(8,128)(2,1)}, u32[]{:S(2)}, u32[]{:S(2)}) collective-permute-start(bf16[4,960,128]{2,1,0:T(8,128)(2,1)} %get-tuple-element.255), channel_id=1, source_target_pairs={{0,96},{4,100},{8,104},{12,108},{16,112},{20,116},{24,120},{28,124... | collective-permute-start | bytes 2949128 | tf_op jit(solution)/shard_map/ppermute | solution.py:651
  548.1 58.1 %collective-permute-start.21 = (f32[8,128]{1,0:T(8,128)S(1)}, f32[8,128]{1,0:T(8,128)S(1)}, u32[]{:S(2)}, u32[]{:S(2)}) collective-permute-start(f32[8,128]{1,0:T(8,128)S(1)} %broadcast_in_dim.137), channel_id=1, source_target_pairs={{0,4},{4,0},{8,12},{12,8},{16,20},{20,16},{24,28},{28,24},{32,36},... | collective-permute-start | bytes 12296 | tf_op jit(solution)/shard_map/ppermute | solution.py:651
  607.0 24.7 %collective-permute-start.23 = (f32[8,128]{1,0:T(8,128)S(1)}, f32[8,128]{1,0:T(8,128)S(1)}, u32[]{:S(2)}, u32[]{:S(2)}) collective-permute-start(f32[8,128]{1,0:T(8,128)S(1)} %broadcast_add_fusion.1), channel_id=1, source_target_pairs={{0,16},{4,20},{8,24},{12,28},{16,0},{20,4},{24,8},{28,12},{32,48},... | collective-permute-start | bytes 12296 | tf_op jit(solution)/shard_map/ppermute | solution.py:651
  646.3 75.8 %collective-permute-start.100 = (f32[4,4,96,128]{3,2,1,0:T(8,128)S(1)}, f32[4,4,96,128]{3,2,1,0:T(8,128)}, u32[]{:S(2)}, u32[]{:S(2)}) collective-permute-start(f32[4,4,96,128]{3,2,1,0:T(8,128)S(1)} %get-tuple-element.279), channel_id=1, source_target_pairs={{0,4},{4,0},{8,12},{12,8},{16,20},{20,16},{24,28},{28,24},{32,36},... | collective-permute-start | bytes 2359304 | tf_op jit(solution)/shard_map/ppermute | solution.py:651
  (249 other events, 3335.0 us)
Sparse Core Ops, SparseCore 0:
  11.6 115.1 all-gather.1

commit v2 on v1

--- a/solution.py
+++ b/solution.py
@@ -99,6 +99,28 @@
     return value * gauss_parts(value)[0]
 
 
+def widen(parts, axis):
+    return jnp.concatenate(
+        [lax.slice_in_dim(x, 0, 128, axis=axis) for x in parts]
+        + [lax.slice_in_dim(x, 128, TILE, axis=axis) for x in parts],
+        axis=axis,
+    )
+
+
+def wide_part(array, k, axis):
+    return jnp.concatenate(
+        [
+            lax.dynamic_slice_in_dim(array, 128 * k, 128, axis),
+            lax.dynamic_slice_in_dim(array, 512 + 64 * k, 64, axis),
+        ],
+        axis=axis,
+    )
+
+
+def wide_back(vector):
+    return jnp.concatenate([vector[:512].reshape(4, 128), vector[512:].reshape(4, 64)], axis=1).reshape(D)
+
+
 def pack_tile(tile):
     half = TILE // 2
     right = tile[..., 128:]
@@ -123,43 +145,76 @@
     )
 
 
-def assemble(table, slots, blocks):
-    rows = len(blocks)
-    flat = [block for line in blocks for block in line]
-
-    def kernel(table_ref, *refs):
-        out_ref = refs[-1]
-        for i in range(rows):
-            for t in range(4):
-                out_ref[0, TILE * i : TILE * i + TILE, TILE * t : TILE * t + TILE] = unpack_tile(
-                    refs[4 * i + t][0]
-                )
-
-    def spec(block):
-        return pl.BlockSpec((1, PACK, 128), lambda r, table_ref: (table_ref[r * 96 + block], 0, 0))
-
-    return pl.pallas_call(
+def assemble(table, slots, groups):
+    half = TILE // 2
+    sizes = [4 * len(group) for group in groups]
+    lines = sum(sizes)
+    wanted = [96 * r + block for group in groups for r in range(4) for line in group for block in line]
+
+    def kernel(table_ref, slots_ref, *refs):
+        outs = refs[: len(groups)]
+        tiles, stage, in_sems, out_sems = refs[len(groups) :]
+
+        def fetch(at, place):
+            return pltpu.make_async_copy(slots_ref.at[place], tiles.at[at], in_sems.at[at])
+
+        for at, entry in enumerate(wanted):
+            fetch(at, table_ref[entry]).start()
+        base = 0
+        for out_ref, size in zip(outs, sizes):
+
+            def step(line, carry):
+                at = base + line
+                for t in range(4):
+                    fetch(4 * at + t, 0).wait()
+                for t in range(4):
+                    stage[at, :, 128 * t : 128 * t + 128] = tiles[4 * at + t, :TILE]
+                for t in (0, 2):
+                    first = tiles[4 * at + t, TILE:]
+                    second = tiles[4 * at + t + 1, TILE:]
+                    cols = slice(512 + 64 * t, 640 + 64 * t)
+                    stage[at, :half, cols] = jnp.concatenate([first[:, :64], second[:, :64]], axis=1)
+                    stage[at, half:, cols] = jnp.concatenate([first[:, 64:], second[:, 64:]], axis=1)
+                pltpu.make_async_copy(stage.at[at], out_ref.at[line], out_sems.at[at]).start()
+                return carry
+
+            lax.fori_loop(0, size, step, 0)
+            base += size
+        base = 0
+        for out_ref, size in zip(outs, sizes):
+
+            def finish(line, carry):
+                pltpu.make_async_copy(stage.at[base + line], out_ref.at[line], out_sems.at[base + line]).wait()
+                return carry
+
+            lax.fori_loop(0, size, finish, 0)
+            base += size
+
+    mats = pl.pallas_call(
         kernel,
-        grid_spec=pltpu.PrefetchScalarGridSpec(
-            num_scalar_prefetch=1,
-            grid=(4,),
-            in_specs=[spec(block) for block in flat],
-            out_specs=pl.BlockSpec((1, rows * TILE, D), lambda r, table_ref: (r, 0, 0)),
-        ),
-        out_shape=shape((4, rows * TILE, D), bf16),
-        compiler_params=params(32),
-        cost_estimate=cost(0, 16 * rows * TILE * TILE * 4),
+        in_specs=[SM, ANY],
+        out_specs=[ANY] * len(groups),
+        out_shape=[shape((size, TILE, D), bf16) for size in sizes],
+        scratch_shapes=[
+            pltpu.VMEM((4 * lines, PACK, 128), bf16),
+            pltpu.VMEM((lines, TILE, D), bf16),
+            pltpu.SemaphoreType.DMA((4 * lines,)),
+            pltpu.SemaphoreType.DMA((lines,)),
+        ],
+        compiler_params=params(60),
+        cost_estimate=cost(0, 4 * lines * TILE * TILE * 4),
         name="assemble",
-    )(table, *([slots] * len(flat)))
-
-
-def layer_weights(table, slots, depth):
+    )(table, slots)
+    return [mat.reshape(4, len(group) * TILE, D) for mat, group in zip(mats, groups)]
+
+
+def layer_blocks(depth):
     base = 48 * depth
-    qkv = assemble(table, slots, [[base + 3 * r + c for r in range(4)] for c in range(3)])
-    out = assemble(table, slots, [[base + 12 + t for t in range(4)]])
-    up = assemble(table, slots, [[base + 16 + 4 * r + t for r in range(4)] for t in range(4)])
-    down = assemble(table, slots, [[base + 32 + 4 * t + r for r in range(4)] for t in range(4)])
-    return qkv, out.reshape(D, D), up, down
+    qkv = [[base + 3 * r + c for r in range(4)] for c in range(3)]
+    out = [[base + 12 + t for t in range(4)]]
+    up = [[base + 16 + 4 * r + t for r in range(4)] for t in range(4)]
+    down = [[base + 32 + 4 * t + r for r in range(4)] for t in range(4)]
+    return [qkv, out, up, down]
 
 
 def column_norm(values):
@@ -168,7 +223,7 @@
     return centered * inverse, inverse
 
 
-def attend_fwd(w_ref, a0, a1, a2, a3, gain_ref, qid_ref, kid_ref, pre_ref, v_ref, lse_ref, o_ref, q_s, k_s):
+def attend_fwd(w_ref, a0, a1, a2, a3, gain_ref, qid_ref, kid_ref, pre_ref, v_ref, lse_ref, o0, o1, o2, o3, q_s, k_s, o_s):
     for c in range(3):
         for r, a_ref in enumerate((a0, a1, a2, a3)):
             cols = slice(OWN * r, OWN * r + OWN)
@@ -196,10 +251,12 @@
         total = jnp.sum(weights, 0, keepdims=True)
         lse_ref[h, :, cols] = top + jnp.log(total)
         probs = (weights * (1.0 / total)).astype(bf16)
-        o_ref[t, rows, :] = mm(v_ref[rows, :], probs).astype(bf16)
+        o_s[t, rows, :] = mm(v_ref[rows, :], probs).astype(bf16)
         return carry
 
     lax.fori_loop(0, 4 * HEADS, step, 0)
+    for r, ref in enumerate((o0, o1, o2, o3)):
+        ref[...] = o_s[r]
 
 
 def run_attend_fwd(w, acts, gains, qid, kid):
@@ -207,15 +264,19 @@
         attend_fwd,
         grid=(1,),
         in_specs=[pl.BlockSpec((1, 3 * TILE, D), lambda i: (0, 0, 0))] + [VM] * 7,
-        out_specs=[VM] * 4,
+        out_specs=[VM] * 7,
         out_shape=[
             shape((2 * TILE, TOKENS)),
             shape((TILE, TOKENS), bf16),
             shape((HEADS, 1, TOKENS)),
-            shape((4, TILE, OWN), bf16),
+        ]
+        + [shape((TILE, OWN), bf16)] * 4,
+        scratch_shapes=[
+            pltpu.VMEM((4, TILE, OWN), bf16),
+            pltpu.VMEM((HEADS, TOKENS, HD), bf16),
+            pltpu.VMEM((4, TILE, OWN), bf16),
         ],
-        scratch_shapes=[pltpu.VMEM((4, TILE, OWN), bf16), pltpu.VMEM((HEADS, TOKENS, HD), bf16)],
-        compiler_params=params(48),
+        compiler_params=params(60),
         cost_estimate=cost(10**10, 6 * 10**6, 3 * 2**20),
         name="attend_fwd",
     )(w, *acts, gains, qid, kid)
@@ -223,8 +284,9 @@
 
 def attend_bwd(
     pre_ref, v_ref, lse_ref, g0, g1, g2, g3, gain_ref, qid_ref, kid_ref,
-    dp_ref, dgain_ref, q_s, qn_s, k_s, kt_s, vn_s, do_s, dq_s, dk_s, dv_s,
+    p0, p1, p2, p3, dgain_ref, q_s, qn_s, k_s, kt_s, vn_s, do_s, dq_s, dk_s, dv_s,
 ):
+    dp_refs = (p0, p1, p2, p3)
     for r, ref in enumerate((g0, g1, g2, g3)):
         do_s[r] = ref[...]
     for h in range(HEADS):
@@ -270,20 +332,20 @@
                 - normed * jnp.mean(scaled * normed, 0, keepdims=True)
             )
             for r in range(4):
-                dp_ref[r, base : base + HD, :] = back[:, OWN * r : OWN * r + OWN].astype(bf16)
+                dp_refs[r][base : base + HD, :] = back[:, OWN * r : OWN * r + OWN].astype(bf16)
         dgain_ref[:, c : c + 1] = total
     for h in range(HEADS):
         back = dv_s[h].T.astype(bf16)
         for r in range(4):
-            dp_ref[r, 2 * TILE + HD * h : 2 * TILE + HD * h + HD, :] = back[:, OWN * r : OWN * r + OWN]
+            dp_refs[r][2 * TILE + HD * h : 2 * TILE + HD * h + HD, :] = back[:, OWN * r : OWN * r + OWN]
 
 
 def run_attend_bwd(pre, v, lse, grads, gains, qid, kid):
     return pl.pallas_call(
         attend_bwd,
         in_specs=[VM] * 10,
-        out_specs=[VM] * 2,
-        out_shape=[shape((4, 3 * TILE, OWN), bf16), shape((HD, 2))],
+        out_specs=[VM] * 5,
+        out_shape=[shape((3 * TILE, OWN), bf16)] * 4 + [shape((HD, 2))],
         scratch_shapes=[
             pltpu.VMEM((TILE, TOKENS), bf16),
             pltpu.VMEM((HEADS, TOKENS, HD), bf16),
@@ -302,7 +364,7 @@
 
 
 def mix_fwd(x_ref, o0, o1, o2, o3, w_out, gain_ref, next_ref, up_ref, down_ref,
-            mid_ref, u_ref, ct_ref, x_out, a_out, c_s):
+            mid_ref, u_ref, c_ref, x_out, a_out):
     r = pl.program_id(0)
 
     @pl.when(r == 0)
@@ -312,11 +374,10 @@
             mid = mid + mm(ref[...], w_out[TILE * k : TILE * k + TILE, :], 0, 0)
         mid_ref[...] = mid
         low = (normalize(mid)[0] * gain_ref[...]).astype(bf16)
-        c_s[...] = low
-        ct_ref[...] = low.T
+        c_ref[...] = low
         x_out[...] = mid
 
-    u = mm(c_s[...], up_ref[0], 1, 1)
+    u = mm(c_ref[...], up_ref[0], 1, 1)
     u_ref[0] = u
     x_out[...] += mm(gelu(u).astype(bf16), down_ref[0])
 
@@ -338,17 +399,16 @@
         mix_fwd,
         grid=(4,),
         in_specs=[whole(OWN, D)] + [whole(TILE, OWN)] * 4 + [whole(D, D), whole(1, D), whole(1, D), part(D, D), part(D, D)],
-        out_specs=[whole(OWN, D), part(OWN, D), whole(D, OWN), whole(OWN, D), whole(OWN, D)],
-        out_shape=[shape((OWN, D)), shape((4, OWN, D)), shape((D, OWN), bf16), shape((OWN, D)), shape((OWN, D), bf16)],
-        scratch_shapes=[pltpu.VMEM((OWN, D), bf16)],
-        compiler_params=params(48),
+        out_specs=[whole(OWN, D), part(OWN, D), whole(OWN, D), whole(OWN, D), whole(OWN, D)],
+        out_shape=[shape((OWN, D)), shape((4, OWN, D)), shape((OWN, D), bf16), shape((OWN, D)), shape((OWN, D), bf16)],
+        compiler_params=params(60),
         cost_estimate=cost(6 * 10**9, 17 * 10**6, 10**6),
         name="mix_fwd",
     )(x, *outs, w_out, gain, gain_next, up, down)
 
 
 def mix_bwd(g_ref, low_ref, mid_ref, u_ref, gain_ref, w_out, up_ref, down_ref,
-            du_ref, mid_grad, mid_low, dgain_ref, do_ref, acc):
+            mid_grad, mid_low, dgain_ref, do0, do1, do2, do3, acc):
     r = pl.program_id(0)
 
     @pl.when(r == 0)
@@ -359,7 +419,6 @@
     u = u_ref[0]
     cdf, bell = gauss_parts(u)
     du = (df * (cdf + u * bell * 0.3989422804014327)).astype(bf16)
-    du_ref[0] = du
     acc[...] += mm(du, up_ref[0])
 
     @pl.when(r == 3)
@@ -371,8 +430,8 @@
         mid_grad[...] = total
         low = total.astype(bf16)
         mid_low[...] = low
-        for k in range(4):
-            do_ref[k] = mm(w_out[TILE * k : TILE * k + TILE, :], low, 1, 1).astype(bf16)
+        for k, ref in enumerate((do0, do1, do2, do3)):
+            ref[...] = mm(w_out[TILE * k : TILE * k + TILE, :], low, 1, 1).astype(bf16)
 
 
 def run_mix_bwd(grad, grad_low, mid, u, gain, w_out, up, down):
@@ -380,10 +439,10 @@
         mix_bwd,
         grid=(4,),
         in_specs=[whole(OWN, D), whole(OWN, D), whole(OWN, D), part(OWN, D), whole(1, D), whole(D, D), part(D, D), part(D, D)],
-        out_specs=[part(OWN, D), whole(OWN, D), whole(OWN, D), whole(1, D), whole(4, TILE, OWN)],
-        out_shape=[shape((4, OWN, D), bf16), shape((OWN, D)), shape((OWN, D), bf16), shape((1, D)), shape((4, TILE, OWN), bf16)],
+        out_specs=[whole(OWN, D), whole(OWN, D), whole(1, D)] + [whole(TILE, OWN)] * 4,
+        out_shape=[shape((OWN, D)), shape((OWN, D), bf16), shape((1, D))] + [shape((TILE, OWN), bf16)] * 4,
         scratch_shapes=[pltpu.VMEM((OWN, D), f32)],
-        compiler_params=params(48),
+        compiler_params=params(60),
         cost_estimate=cost(6 * 10**9, 17 * 10**6, 10**6),
         name="mix_bwd",
     )(grad, grad_low, mid, u, gain, w_out, up, down)
@@ -412,10 +471,23 @@
     )(mid_grad, *grads, w, x, gain)
 
 
-def send_tiles(places, stage, sems, keep, send, tiles, base):
-    for i, (block, tile) in enumerate(tiles):
-        at = base + i
-        stage[at] = pack_tile(tile.astype(bf16))
+def pack_wide(line, t):
+    half = TILE // 2
+    right = line[:, 512 + 64 * t : 576 + 64 * t]
+    return jnp.concatenate(
+        [
+            line[:, 128 * t : 128 * t + 128],
+            jnp.concatenate([right[:half], right[half:]], axis=1),
+        ],
+        axis=0,
+    )
+
+
+def send_line(places, stage, sems, keep, send, line, blocks, base):
+    line = line.astype(bf16)
+    for t, block in enumerate(blocks):
+        at = base + t
+        stage[at] = pack_wide(line, t)
         place = places[block]
         rows = pl.ds(pl.multiple_of((place % 3) * PACK, 16), PACK)
 
@@ -433,85 +505,132 @@
         pltpu.make_async_copy(stage.at[at], keep.at[0, pl.ds(0, PACK)], sems.at[at]).wait()
 
 
-def cut(line, count=4):
-    return [line[:, TILE * t : TILE * t + TILE] for t in range(count)]
-
-
-def mlp_grads(depth, places, *refs):
-    ct, du, low, mid_low = (refs[0:4], refs[4:8], refs[8:12], refs[12:16])
-    o_ref, up_ref = refs[16:18]
-    keep, send, stage, f_s, sems = refs[-5:]
+def mlp_grads(depth, places, act_ref, low_ref, up_ref, down_ref, *refs):
+    keep, send, token, stage, sems = refs[-5:]
     base = 48 * depth
+    for i in range(4):
+        rows = slice(TILE * i, TILE * i + TILE)
+        u = mm(up_ref[0, rows, :], act_ref[...], 1, 1)
+        df = mm(down_ref[0, rows, :], low_ref[...], 1, 1)
+        cdf, bell = gauss_parts(u)
+        f_low = (u * cdf).astype(bf16)
+        du_low = (df * (cdf + u * bell * 0.3989422804014327)).astype(bf16)
+        line = mm(du_low, act_ref[...])
+        send_line(places, stage, sems, keep, send, line, [base + 16 + 4 * t + i for t in range(4)], 4 * i)
+        line = mm(f_low, low_ref[...])
+        send_line(places, stage, sems, keep, send, line, [base + 32 + 4 * i + t for t in range(4)], 16 + 4 * i)
+    token[...] = jnp.zeros_like(token)
+    wait_tiles(stage, sems, keep, 32)
+
+
+def head_grads(depth, places, index, mid_ref, *refs):
+    outs, grads, acts = (refs[0:4], refs[4:8], refs[8:12])
+    keep, send, token, stage, sems = refs[-5:]
+    base = 48 * depth
+    parts = []
     for r in range(4):
-        f_s[r] = gelu(mm(up_ref[0], ct[r][...])).astype(bf16)
-
-    def rows_of(pieces, others, i):
-        rows = slice(TILE * i, TILE * i + TILE)
-        total = mm(pieces[0][rows, :], others[0][...])
-        for r in range(1, 4):
-            total = total + mm(pieces[r][rows, :], others[r][...])
-        return total
-
-    line = rows_of([o_ref.at[r] for r in range(4)], mid_low, 0)
-    send_tiles(places, stage, sems, keep, send, [(base + 12 + t, x) for t, x in enumerate(cut(line))], 0)
-    for i in range(4):
-        line = rows_of(ct, du, i)
-        tiles = [(base + 16 + 4 * i + t, x) for t, x in enumerate(cut(line))]
-        send_tiles(places, stage, sems, keep, send, tiles, 4 + 4 * i)
-    for i in range(4):
-        line = rows_of([f_s.at[r] for r in range(4)], low, i)
-        tiles = [(base + 32 + 4 * i + t, x) for t, x in enumerate(cut(line))]
-        send_tiles(places, stage, sems, keep, send, tiles, 20 + 4 * i)
-    wait_tiles(stage, sems, keep, 36)
-
-
-def qkv_grads(depth, places, *refs):
-    dp_ref, acts = (refs[0], refs[1:5])
-    keep, send, stage, sems = refs[-4:]
-    base = 48 * depth
+        rows = pl.ds(pl.multiple_of((index[0] ^ r) * OWN, OWN), OWN)
+        parts.append(mm(outs[r][...], mid_ref[rows, :]))
+    line = (parts[0] + parts[1]) + (parts[2] + parts[3])
+    send_line(places, stage, sems, keep, send, line, [base + 12 + t for t in range(4)], 12)
     for c in range(3):
         rows = slice(TILE * c, TILE * c + TILE)
-        line = mm(dp_ref[0, rows, :], acts[0][...])
-        for r in range(1, 4):
-            line = line + mm(dp_ref[r, rows, :], acts[r][...])
-        tiles = [(base + 3 * t + c, x) for t, x in enumerate(cut(line))]
-        send_tiles(places, stage, sems, keep, send, tiles, 4 * c)
-    wait_tiles(stage, sems, keep, 12)
-
-
-def grads_call(kernel, name, places, args, specs, buffers, scratch, flops):
-    out = [shape((16, ROWS, 128), bf16)] * 2
+        parts = [mm(grads[r][rows, :], acts[r][...]) for r in range(4)]
+        line = (parts[0] + parts[1]) + (parts[2] + parts[3])
+        send_line(places, stage, sems, keep, send, line, [base + 3 * t + c for t in range(4)], 4 * c)
+    token[...] = jnp.zeros_like(token)
+    wait_tiles(stage, sems, keep, 16)
+
+
+def grads_call(kernel, name, scalars, args, specs, buffers, count, flops):
     given = list(buffers) if buffers is not None else []
-    first = 1 + len(args)
-    return pl.pallas_call(
+    first = len(scalars) + len(args)
+    *buffers, token = pl.pallas_call(
         kernel,
         grid=(1,),
-        in_specs=[SM] + specs + [ANY] * len(given),
-        out_specs=[ANY] * 2,
-        out_shape=out,
+        in_specs=[SM] * len(scalars) + specs + [ANY] * len(given),
+        out_specs=[ANY, ANY, VM],
+        out_shape=[shape((16, ROWS, 128), bf16)] * 2 + [shape((8, 128))],
         input_output_aliases={first + i: i for i in range(len(given))},
-        scratch_shapes=scratch,
+        scratch_shapes=[pltpu.VMEM((count, PACK, 128), bf16), pltpu.SemaphoreType.DMA((count,))],
         compiler_params=params(56),
         cost_estimate=cost(flops, 10**7),
         name=name,
-    )(places, *args, *given)
-
-
-def run_mlp_grads(depth, places, ct, du, low, mid_low, o, up, buffers):
-    specs = [VM] * 17 + [pl.BlockSpec((1, D, D), lambda i: (0, 0, 0))]
+    )(*scalars, *args, *given)
+    return buffers, token
+
+
+def run_mlp_grads(depth, places, act, low, up, down, buffers):
+    first = pl.BlockSpec((1, D, D), lambda i: (0, 0, 0))
     return grads_call(
-        lambda *refs: mlp_grads(depth, *refs), "mlp_grads", places,
-        [*ct, *du, *low, *mid_low, o, up], specs, buffers,
-        [pltpu.VMEM((36, PACK, 128), bf16), pltpu.VMEM((4, D, OWN), bf16), pltpu.SemaphoreType.DMA((36,))],
-        4 * 10**9,
-    )
-
-
-def run_qkv_grads(depth, places, dp, acts, buffers):
+        lambda *refs: mlp_grads(depth, *refs), "mlp_grads", [places],
+        [act, low, up, down], [VM] * 2 + [first] * 2, buffers, 32, 5 * 10**9,
+    )
+
+
+def run_head_grads(depth, places, index, mid_low, outs, grads, acts, buffers):
     return grads_call(
-        lambda *refs: qkv_grads(depth, *refs), "qkv_grads", places, [dp, *acts], [VM] * 5, buffers,
-        [pltpu.VMEM((12, PACK, 128), bf16), pltpu.SemaphoreType.DMA((12,))], 10**9,
-    )
+        lambda *refs: head_grads(depth, *refs), "head_grads", [places, index],
+        [mid_low, *outs, *grads, *acts], [VM] * 13, buffers, 16, 2 * 10**9,
+    )
+
+
+def add_core(keep, got, own_a, a1, a2, a3, own_b, b1, b2, b3):
+    step = pl.program_id(0)
+    half = ROWS // 2
+    total = keep[...].astype(f32) + got[...].astype(f32)
+
+    @pl.when(step == 0)
+    def _():
+        own_a[...] = total[:, :half]
+
+    for k, ref in ((1, a1), (2, a2), (3, a3)):
+
+        @pl.when(step == k)
+        def _():
+            ref[...] = total[:, :half].astype(bf16)
+
+    own_b[0] = total[0, half:]
+    for k, ref in ((1, b1), (2, b2), (3, b3)):
+        ref[0] = total[k, half:].astype(bf16)
+
+
+def run_add_core(keep, got):
+    half = ROWS // 2
+    block = pl.BlockSpec((4, ROWS, 128), lambda r: (r, 0, 0))
+    one, many = (whole(4, half, 128), part(half, 128))
+    return pl.pallas_call(
+        add_core, grid=(4,), in_specs=[block] * 2, out_specs=[one] * 4 + [many] * 4,
+        out_shape=([shape((4, half, 128))] + [shape((4, half, 128), bf16)] * 3) * 2,
+        compiler_params=params(32), cost_estimate=cost(10**7, 14 * 10**6), name="add_core",
+    )(keep, got)
+
+
+def add_axis(*refs):
+    ins, outs = (refs[:8], refs[8:])
+    for side in range(2):
+        own, r1, r2, r3 = ins[4 * side : 4 * side + 4]
+        for k in range(4):
+            total = (own[k] + r1[k].astype(f32)) + (r2[k].astype(f32) + r3[k].astype(f32))
+            out = outs[4 * side + k]
+            out[...] = total.astype(out.dtype)
+
+
+def run_add_axis(a, b):
+    half = ROWS // 2
+    return pl.pallas_call(
+        add_axis, in_specs=[VM] * 8, out_specs=[VM] * 8,
+        out_shape=([shape((half, 128))] + [shape((half, 128), bf16)] * 3) * 2,
+        compiler_params=params(32), cost_estimate=cost(10**7, 6 * 10**6), name="add_axis",
+    )(*a, *b)
+
+
+def gate(array, *others):
+    return pl.pallas_call(
+        lambda *refs: None, in_specs=[ANY] * (1 + len(others)), out_specs=ANY,
+        out_shape=shape(array.shape, array.dtype), input_output_aliases={0: 0},
+        compiler_params=params(16), name="gate",
+    )(array, *others)
 
 
 def soap_early(first, stat_l, stat_r, left, right, turned_ref, l_ref, r_ref):
@@ -566,17 +685,15 @@
 
 
 def soap_late(
-    f_ref, grad, first, second, stat_l, stat_r, left, right, weight, turned, turned_first, xl, xr, yl, yr, gl, gr,
-    weight_ref, first_ref, second_ref, sl_ref, sr_ref, left_ref, right_ref, low_ref, panels,
+    f_ref, second, left, right, weight, turned, turned_first, xl, xr, yl, yr,
+    weight_ref, left_ref, right_ref, low_ref, panels,
 ):
     factor = f_ref[0, 0]
     bias_one = 1.0 - first_decay**STEP
     bias_two = 1.0 - second_decay**STEP
     for n in range(3):
-        first_ref[n] = first_decay * first[n] + (1.0 - first_decay) * (grad[n] * factor)
         rotated = turned[n] * factor
         second_new = second_decay * second[n] + (1.0 - second_decay) * rotated * rotated
-        second_ref[n] = second_new
         scaled = (
             (first_decay * turned_first[n] + (1.0 - first_decay) * rotated)
             / bias_one
@@ -586,8 +703,6 @@
         weight_new = weight[n] * (1.0 - matrix_rate * weight_decay) - matrix_rate * back
         weight_ref[n] = weight_new
         low_ref[n] = weight_new.astype(bf16)
-        sl_ref[n] = second_decay * stat_l[n] + (1.0 - second_decay) * (factor * (factor * gl[n]))
-        sr_ref[n] = second_decay * stat_r[n] + (1.0 - second_decay) * (factor * (factor * gr[n]))
         for side, (old, new) in enumerate(((xl, yl), (xr, yr))):
             product = second_decay * old[n] + (1.0 - second_decay) * (factor * (factor * new[n]))
             for j in range(3):
@@ -629,8 +744,8 @@
 
 def run_soap_late(*args):
     return pl.pallas_call(
-        soap_late, in_specs=[SM] + [VM] * 16, out_specs=[VM] * 8,
-        out_shape=tiles_of_three(7) + [shape((3, TILE, TILE), bf16)],
+        soap_late, in_specs=[SM] + [VM] * 10, out_specs=[VM] * 4,
+        out_shape=tiles_of_three(3) + [shape((3, TILE, TILE), bf16)],
         scratch_shapes=[pltpu.VMEM((6, 3, TILE, 64), f32)],
         compiler_params=params(56), cost_estimate=cost(10**9, 10**7), name="soap_late",
     )(*args)
@@ -708,21 +823,18 @@
         jnp.where(owners[None, :] == my_slots[:, None], jnp.arange(96)[None, :], 0), axis=1
     )
     kind = my_blocks % 48
-    grad_flips = (kind < 12).astype(jnp.int32)
-    weight_flips = (kind < 12) | ((kind >= 16) & (kind < 32))
+    flips = (kind < 12) | ((kind >= 16) & (kind < 32))
 
     master = tiled(soap_weight)
     low = master.astype(bf16)
-    low = jnp.where(weight_flips[:, None, None], jnp.swapaxes(low, 1, 2), low)
+    low = jnp.where(flips[:, None, None], jnp.swapaxes(low, 1, 2), low)
     slots = lax.all_gather(pack_tile(low), ("dp", "mp"), axis=0, tiled=True)
 
-    embed_parts = jnp.stack(gather_mp(embed_weight.astype(bf16)))
-    embed_low = by_partner(embed_parts, mp_index).transpose(1, 0, 2).reshape(D, D)
-    head_mine = head_weight.astype(bf16)
-    head_low = by_partner(jnp.stack(gather_mp(head_mine)), mp_index).reshape(D, CLASSES)
+    head_low = lax.all_gather(head_weight.astype(bf16), "mp", axis=0, tiled=True)
 
     split_one = (2 * LAYERS + 1) * D
-    gain_rows = vectors[:split_one].reshape(2 * LAYERS + 1, 1, D)
+    gain_rows = vectors[:split_one].reshape(2 * LAYERS + 1, 4, TILE)
+    gain_rows = widen([gain_rows[:, t] for t in range(4)], 1)[:, None, :]
     head_gains = vectors[split_one : split_one + 2 * LAYERS * HD].reshape(LAYERS, 2, HD)
     class_bias = vectors[vectors.shape[0] - CLASSES :]
 
@@ -743,27 +855,45 @@
     left, right = (tiled(basis_left), tiled(basis_right))
     turned_first, left_old, right_old = run_soap_early(first_tiles, left_stat, right_stat, left, right)
 
-    resid = jnp.dot(tokens[0], embed_low, preferred_element_type=f32).astype(bf16).astype(f32)
+    embedded = jnp.dot(tokens.reshape(TOKENS, D), embed_weight.astype(bf16), preferred_element_type=f32)
+    embedded = embedded.astype(bf16).reshape(4, OWN, TILE)
+    embedded = by_partner(jnp.stack(trade_mp([embedded[r] for r in range(4)])), mp_index)
+    resid = widen([embedded[t] for t in range(4)], 1).astype(f32)
     act = (normalize(resid)[0] * gain_rows[0]).astype(bf16)
 
-    weights = [layer_weights(table, slots, depth) for depth in range(LAYERS)]
+    blocks = [layer_blocks(depth) for depth in range(LAYERS)]
+    weights = [assemble(table, slots, blocks[0][:1]) + assemble(table, slots, blocks[0][1:])]
+    weights += [assemble(table, slots, blocks[depth]) for depth in range(1, LAYERS)]
+    index = jnp.full((1,), mp_index, jnp.int32)
     saved = []
+    normed = None
     for depth in range(LAYERS):
         qkv, out, up, down = weights[depth]
+        out = out.reshape(D, D)
         gains = head_gains[depth].T
         acts = gather_mp(act)
-        pre, v, lse, o = run_attend_fwd(qkv, acts, gains, query_ids, key_ids)
-        outs = trade_mp([o[r] for r in range(4)])
-        mid, u, ct, resid_next, act = run_mix_fwd(
+        if depth == 0:
+            acts[0] = gate(acts[0], turned_first, second_tiles)
+        else:
+            normed = gate(normed, *acts[1:], qkv)
+            saved[-1].append(lax.all_gather(normed, "mp", axis=0, tiled=True))
+        pre, v, lse, *o = run_attend_fwd(qkv, acts, gains, query_ids, key_ids)
+        outs = trade_mp(o)
+        if depth == 0:
+            outs[0] = gate(outs[0], head_low)
+        mid, u, normed, resid_next, act = run_mix_fwd(
             resid, outs, out, gain_rows[2 * depth + 1], gain_rows[2 * depth + 2], up, down
         )
-        saved.append((resid, acts, pre, v, lse, o, mid, u, gather_mp(ct)))
+        saved.append([resid, acts, pre, v, lse, o, mid, u])
         resid = resid_next
-
+    saved[-1].append(lax.all_gather(normed, "mp", axis=0, tiled=True))
+
+    resid = gate(resid, saved[0][-1])
     final, final_inverse = normalize(resid)
     gain_last = gain_rows[2 * LAYERS]
     pooled = total_mp(jnp.dot(member.T, final * gain_last, precision=highest)) / divisor[:, None]
-    pooled_low = pooled.astype(bf16)
+    pooled = jnp.concatenate([pooled[:, :512].reshape(IMGS, 4, 128), pooled[:, 512:].reshape(IMGS, 4, 64)], axis=2)
+    pooled_low = pooled.reshape(IMGS, D).astype(bf16)
     logits = jnp.dot(pooled_low, head_low, preferred_element_type=f32) + class_bias
     row_max = jnp.max(logits, -1, keepdims=True)
     exps = jnp.exp(logits - row_max)
@@ -771,45 +901,55 @@
     log_norm = row_max[:, 0] + jnp.log(row_sum[:, 0])
     onehot = (jnp.arange(CLASSES)[None, :] == labels.reshape(-1)[:, None]).astype(f32)
     local_loss = jnp.sum((log_norm - jnp.sum(onehot * logits, -1)) * present)
-    loss_total = total_dp(jnp.full((8, 128), local_loss, f32))[0, 0]
     grad_logits = (exps / row_sum - onehot) * present[:, None] / image_total
     grad_bias = jnp.sum(grad_logits, 0)
     grad_logit_low = grad_logits.astype(bf16)
     pooled_mine = lax.dynamic_slice_in_dim(pooled_low, mp_index * TILE, TILE, 1)
     grad_head = jnp.dot(pooled_mine.T, grad_logit_low, preferred_element_type=f32)
     grad_pooled = jnp.dot(grad_logit_low, head_low.T, preferred_element_type=f32)
-    grad_final = jnp.dot(member, grad_pooled / divisor[:, None], precision=highest)
-    gain_grads = [jnp.sum(grad_final * final, 0)]
+    grad_pooled = grad_pooled / divisor[:, None]
+    grad_pooled = widen([grad_pooled[:, TILE * t : TILE * t + TILE] for t in range(4)], 1)
+    grad_final = jnp.dot(member, grad_pooled, precision=highest)
+    gain_grads = [wide_back(jnp.sum(grad_final * final, 0))]
     grad = norm_back(grad_final, gain_last, final, final_inverse)
     grad_low = grad.astype(bf16)
 
-    buffers = None
+    buffers = waiting = None
     head_gain_grads = []
     for depth in reversed(range(LAYERS)):
         qkv, out, up, down = weights[depth]
-        resid, acts, pre, v, lse, o, mid, u, ct = saved[depth]
+        resid, acts, pre, v, lse, o, mid, u, normed = saved[depth]
         gains = head_gains[depth].T
-        lows = gather_mp(grad_low)
-        du, mid_grad, mid_low, gain_two, do = run_mix_bwd(
+        out = out.reshape(D, D)
+        lows = lax.all_gather(grad_low, "mp", axis=0, tiled=True)
+        mid_grad, mid_low, gain_two, *do = run_mix_bwd(
             grad, grad_low, mid, u, gain_rows[2 * depth + 1], out, up, down
         )
-        dos = trade_mp([do[r] for r in range(4)])
-        dus = trade_mp([du[r] for r in range(4)])
-        mid_lows = gather_mp(mid_low)
-        dp, gain_heads = run_attend_bwd(pre, v, lse, dos, gains, query_ids, key_ids)
-        dps = trade_mp([dp[r] for r in range(4)])
+        dos = trade_mp(do)
+        mid_lows = lax.all_gather(gate(mid_low, *dos[1:]), "mp", axis=0, tiled=True)
+        if waiting is None:
+            pre = gate(pre, normed)
+        else:
+            deeper, given, *rest = waiting
+            buffers, token = run_head_grads(deeper, places, index, gate(given, do[0]), *rest, buffers)
+            pre = gate(pre, token)
+        *dp, gain_heads = run_attend_bwd(pre, v, lse, dos, gains, query_ids, key_ids)
+        dps = trade_mp(dp)
+        buffers, token = run_mlp_grads(depth, places, normed, lows, up, down, buffers)
+        mid_grad = gate(mid_grad, token)
         grad, grad_low, gain_one = run_input_bwd(mid_grad, dps, qkv, resid, gain_rows[2 * depth])
-        buffers = run_mlp_grads(depth, places, ct, dus, lows, mid_lows, o, up, buffers)
-        buffers = run_qkv_grads(depth, places, dp, acts, buffers)
-        gain_grads = [gain_one[0], gain_two[0]] + gain_grads
+        waiting = (depth, mid_lows, o, dp, acts)
+        gain_grads = [wide_back(gain_one[0]), wide_back(gain_two[0])] + gain_grads
         head_gain_grads.insert(0, gain_heads.T)
 
-    pieces = [
-        lax.dynamic_slice_in_dim(grad_low, (mp_index ^ r) * TILE, TILE, 1) for r in range(4)
-    ]
-    columns = jnp.concatenate(trade_mp(pieces), axis=0)
-    grad_embed = jnp.dot(tokens.reshape(TOKENS, D).T, columns, preferred_element_type=f32)
-    embed_rows = pack_rows(grad_embed)
+    deeper, *rest = waiting
+    buffers, token = run_head_grads(deeper, places, index, *rest, buffers)
+
+    columns = trade_mp([wide_part(grad_low, mp_index ^ r, 1) for r in range(4)])
+    columns[0] = gate(columns[0], token)
+    columns = jnp.concatenate(columns, axis=0)
+    grad_embed = jnp.dot(columns.T, tokens.reshape(TOKENS, D), preferred_element_type=f32)
+    embed_rows = grad_embed.reshape(32, EMBED_ROWS, 128)
     head_rows = jnp.pad(grad_head, ((0, 0), (0, 24))).reshape(32, HEAD_ROWS, 128)
     vector_part = jnp.concatenate([jnp.concatenate(gain_grads), jnp.stack(head_gain_grads).reshape(-1)])
     vector_sum = jnp.concatenate([total_mp(vector_part), grad_bias, jnp.zeros((24,), f32)])
@@ -819,10 +959,18 @@
     keep_buffer = buffers[0].at[:, 3 * PACK :].set(small[:, 0])
     send_buffer = buffers[1].at[:, 3 * PACK :].set(small[:, 1])
 
-    both = keep_buffer.astype(f32) + swap_dp(send_buffer, 1).astype(f32)
-    both = both.reshape(4, 4, ROWS, 128)
-    both = sum_four([both[0]] + [swap_dp(both[r].astype(bf16), 8 * r).astype(f32) for r in (1, 2, 3)])
-    mine = sum_four([both[0]] + [swap_dp(both[r].astype(bf16), 2 * r).astype(f32) for r in (1, 2, 3)])
+    sums = run_add_core(keep_buffer, swap_dp(send_buffer, 1))
+    sums = run_add_axis(
+        [sums[0]] + [swap_dp(sums[r], 8 * r) for r in (1, 2, 3)],
+        [sums[4]] + [swap_dp(sums[4 + r], 2 * r) for r in (1, 2, 3)],
+    )
+    mine = jnp.concatenate(
+        [
+            sum_four([sums[0]] + [swap_dp(sums[r], 2 * r).astype(f32) for r in (1, 2, 3)]),
+            sum_four([sums[4]] + [swap_dp(sums[4 + r], 8 * r).astype(f32) for r in (1, 2, 3)]),
+        ],
+        axis=0,
+    )
     mine_slots = mine[: 3 * PACK]
     share = mine[3 * PACK :]
     cut_at = EMBED_ROWS + HEAD_ROWS
@@ -831,47 +979,53 @@
         + jnp.sum(share[:cut_at] * share[:cut_at])
         + jnp.sum(share[cut_at:] * share[cut_at:]) * 0.25
     )
-    squares = total_dp(total_mp(jnp.full((8, 128), local_squares, f32)))[0, 0]
+    def flat(tiles):
+        return tiles.reshape(3, TILE * TILE)
+
+    grad_tiles, turned, left_new, right_new, gram_left, gram_right = run_soap_mid(
+        flips.astype(jnp.int32), mine_slots.reshape(3, PACK, 128), left, right
+    )
+    rows = jnp.arange(8)[:, None] + jnp.zeros((8, 128), jnp.int32)
+    squares = total_mp(jnp.where(rows == 0, local_squares, local_loss * 0.25))
+    squares = squares + swap_dp(squares, 1)
+    squares = sum_four([squares] + [swap_dp(squares, 2 * r) for r in (1, 2, 3)])
+    flats = [flat(grad_tiles), flat(turned), flat(gram_left), flat(gram_right)]
+    squares = gate(squares, *flats)
+    squares = sum_four([squares] + [swap_dp(squares, 8 * r) for r in (1, 2, 3)])
+    squares, loss_total = (squares[0, 0], squares[1, 0])
+    shares = lax.all_gather(share, "dp", axis=0)
     grad_norm = jnp.sqrt(squares)
     factor = clip_limit / jnp.maximum(grad_norm, clip_limit)
 
-    grad_tiles, turned, left_new, right_new, gram_left, gram_right = run_soap_mid(
-        grad_flips, mine_slots.reshape(3, PACK, 128), left, right
-    )
-    soap_new = run_soap_late(
-        factor.reshape(1, 1), grad_tiles, first_tiles, second_tiles, left_stat, right_stat, left, right, master,
-        turned, turned_first, left_old, right_old, left_new, right_new, gram_left, gram_right,
-    )
-    soap_new = [entry.reshape(3, TILE * TILE) for entry in soap_new]
-
-    shares = jnp.stack([share] + [swap_dp(share, 2 * r) for r in (1, 2, 3)])
-    shares = jnp.stack([shares] + [swap_dp(shares, 8 * r) for r in (1, 2, 3)])
-    shares = jnp.stack([shares, swap_dp(shares, 1)], axis=2).reshape(32, SMALL, 128)
-    shares = by_partner(shares, dp_index)
-    grad_embed = unpack_rows(shares[:, :EMBED_ROWS])
+    grad_flat, turned_flat, gram_left, gram_right = flats
+    weight_new, left_basis, right_basis, weight_low = run_soap_late(
+        factor.reshape(1, 1), second_tiles, left, right, master, turned, turned_first,
+        left_old, right_old, left_new, right_new,
+    )
+    turned_flat = turned_flat * factor
+    soap_new = (
+        flat(weight_new),
+        first_decay * soap_first + (1.0 - first_decay) * (grad_flat * factor),
+        second_decay * soap_second + (1.0 - second_decay) * turned_flat * turned_flat,
+        second_decay * stat_left + (1.0 - second_decay) * (factor * (factor * gram_left)),
+        second_decay * stat_right + (1.0 - second_decay) * (factor * (factor * gram_right)),
+        flat(left_basis),
+        flat(right_basis),
+        flat(weight_low),
+    )
+
+    grad_embed = shares[:, :EMBED_ROWS].reshape(TILE, D)
     grad_head = shares[:, EMBED_ROWS:cut_at].reshape(TILE, 1024)[:, :CLASSES]
     grad_vector = shares[:, cut_at:].reshape(32, 1536)[:, :160].reshape(-1)[: vectors.shape[0]]
     embed_new = adamw(
-        embed_weight, grad_embed * factor, embed_first, embed_second, matrix_rate, weight_decay
-    )
+        embed_weight.T, grad_embed * factor, embed_first.T, embed_second.T, matrix_rate, weight_decay
+    )
+    embed_new = tuple(entry.T for entry in embed_new)
     head_new = adamw(
         head_weight, grad_head * factor, head_first, head_second, matrix_rate, weight_decay
     )
     vector_new = adamw(vectors, grad_vector * factor, vector_first, vector_second, vector_rate, 0.0)
     return (loss_total, image_total, grad_norm, *soap_new, *embed_new, *head_new, *vector_new)
-
-
-def pack_rows(array):
-    rows = array.reshape(32, 24, TILE)
-    right = rows[:, :, 128:]
-    right = jnp.concatenate([right[:, :12], right[:, 12:]], axis=2)
-    return jnp.concatenate([rows[:, :, :128], right], axis=1)
-
-
-def unpack_rows(packed):
-    right = packed[:, 24:]
-    right = jnp.concatenate([right[:, :, :64], right[:, :, 64:]], axis=1)
-    return jnp.concatenate([packed[:, :24], right], axis=2).reshape(D, TILE)
 
 
 def solution(mesh):

time: 761 us -> 619 us (0.81)
  waiting for transfers between devices: 189 us -> 134 us
  starting transfers between devices: 149 us -> 100 us
  local copies, waits for them, and re-layouts: 95.7 us -> 76.2 us
  other arithmetic: 49.9 us -> 31.6 us
    ppermute x101 -> x66, waiting for transfers between devices: 112 us -> 51.4 us  [swap(): return lax.ppermute(array, axis, [(i, i ^ r) for i in range(size)])]
    ppermute x101 -> x66, starting transfers between devices: 149 us -> 99.7 us  [swap(): return lax.ppermute(array, axis, [(i, i ^ r) for i in range(size)])]
    all_gather x0 -> x8, waiting for transfers between devices: none -> 9.87 us  [the longest x2 9.14 us: shards(): mid_lows = lax.all_gather(gate(mid_low, *dos[1:]), 'mp', axis=0, tiled=True)]
    another operation x9 -> x3, other arithmetic: 9.16 us -> 0.14 us
    pallas_call x15 -> x25, Pallas kernels: 151 us -> 145 us  [the longest x1 41.2 us: run_soap_late(): pl.pallas_call(soap_late, in_specs=[SM] + [VM] * 10, out_specs=[VM] * 4,...]
    unnamed x370 -> x239, local copies, waits for them, and re-layouts: 41 us -> 38.9 us
  transfers between devices with their start and end apart: 102 -> 75, of which waited for: 30 -> 21; matrix products, arithmetic and copies ran while one was open for 12% -> 10% of each run, Pallas kernels for 29% -> 37%
where the time goes in v2:
time: 619 us; the launch traced here: 608 us
  Pallas kernels  239 us (39%)
  waiting for transfers between devices  134 us (22%)
  starting transfers between devices  100 us (16%)
  local copies, waits for them, and re-layouts  76.2 us (12%)
  other arithmetic  31.6 us (5%)
  between operations  20.6 us (3%)
  matrix products  6.24 us (1%)
    ppermute x66, starting transfers between devices, swap(): return lax.ppermute(array, axis, [(i, i ^ r) for i in range(size)])  99.7 us
    all_gather x1, waiting for transfers between devices, shards(): slots = lax.all_gather(pack_tile(low), ('dp', 'mp'), axis=0, tiled=True)  72.4 us
    ppermute x66, waiting for transfers between devices, swap(): return lax.ppermute(array, axis, [(i, i ^ r) for i in range(size)])  51.4 us
    pallas_call x1, Pallas kernels, run_soap_late(): pl.pallas_call(soap_late, in_specs=[SM] + [VM] * 10, out_specs=[VM] * 4,...  41.2 us
    unnamed x239, local copies, waits for them, and re-layouts  38.9 us
    pallas_call x2, Pallas kernels, run_attend_bwd(): pl.pallas_call(attend_bwd, in_specs=[VM] * 10, out_specs=[VM] * 5, out_sh...  38.2 us
    pallas_call x4, Pallas kernels, grads_call(): pl.pallas_call(kernel, grid=(1,), in_specs=[SM] * len(scalars) + specs +...  35.9 us
    pallas_call x2, Pallas kernels, run_attend_fwd(): pl.pallas_call(attend_fwd, grid=(1,), in_specs=[pl.BlockSpec((1, 3 * TILE...  29.4 us
  transfers between devices with their start and end apart: 75, of which 21 were waited for; matrix products, arithmetic and copies ran while one was open for 10% of the time, Pallas kernels for 37%

profile of v2, /device:TPU:1, one launch (start us, length us, event | category | flops | bytes accessed | tf_op | source)
XLA Modules:
  0.0 607.7 jit_solution(6189181382499078488)
XLA Ops:
  14.3 3.3 collective-permute-start.2
  43.5 4.0 collective-permute-done.5.a3.refs_14_
  48.4 72.4 %all-gather.11.cloned.1.call-done.slots_ref = bf16[384,288,128]{2,1,0:T(8,128)(2,1)} async-done(((bf16[3,288,128]{2,1,0:T(8,128)(2,1)}), bf16[384,288,128]{2,1,0:T(8,128)(2,1)}) %all-gather.11.cloned.1.call-update) | async-done | bytes 28311568 | tf_op jit(solution)/shard_map/all_gather | solution.py:831
  120.8 4.2 assemble.3
  125.0 14.7 %attend_fwd.2 = (f32[384,1024]{1,0:T(8,128)}, bf16[192,1024]{1,0:T(8,128)(2,1)}, f32[3,1,1024]{2,1,0:T(1,128)}, bf16[192,256]{1,0:T(8,128)(2,1)}, bf16[192,256]{...) custom-call(bf16[4,576,768]{2,1,0:T(8,128)(2,1)} %bitcast.130, bf16[256,768]{1,0:T(8,128)(2,1)} %copy-done.13, ...), custom_call_target="tpu_custom_call" | custom-call | flops 10000000000 | bytes 6000000 | tf_op jit(solution)/shard_map/attend_fwd/pallas_call | solution.py:263
  145.6 10.3 %assemble.4 = (bf16[4,192,768]{2,1,0:T(8,128)(2,1)}, bf16[16,192,768]{2,1,0:T(8,128)(2,1)}, bf16[16,192,768]{2,1,0:T(8,128)(2,1)}) custom-call(s32[384]{0:T(512)} %add.333.table_ref, bf16[384,288,128]{2,1,0:T(8,128)(2,1)} %all-gather.11.cloned.1.call-done.slots_ref), custom_call_target="tpu_custom_call" | custom-call | bytes 21233664 | tf_op jit(solution)/shard_map/assemble/pallas_call | solution.py:193
  158.7 11.2 %mix_fwd.2 = (f32[256,768]{1,0:T(8,128)}, f32[4,256,768]{2,1,0:T(8,128)}, bf16[256,768]{1,0:T(8,128)(2,1)}, f32[256,768]{1,0:T(8,128)}, bf16[256,768]{1,0:T(8,128)(2,1)}) custom-call(f32[256,768]{1,0:T(8,128)} %convert_element_type.70.x_ref, bf16[192,256]{1,0:T(8,128)(2,1)} %copy-done.39, bf16[192,256]{1,0:T(8,128)(2,1)} %copy-done.111, ...), custom_call_target="tpu_custom_call" | custom-call | flops 6000000000 | bytes 17000000 | tf_op jit(solution)/shard_map/mix_fwd/pallas_call | solution.py:398
  173.4 13.0 %assemble.5 = (bf16[12,192,768]{2,1,0:T(8,128)(2,1)}, bf16[4,192,768]{2,1,0:T(8,128)(2,1)}, bf16[16,192,768]{2,1,0:T(8,128)(2,1)}, bf16[16,192,768]{2,1,0:T(8,128)(2,1)}) custom-call(s32[384]{0:T(512)} %add.333.table_ref, bf16[384,288,128]{2,1,0:T(8,128)(2,1)} %all-gather.11.cloned.1.call-done.slots_ref), custom_call_target="tpu_custom_call" | custom-call | bytes 28311552 | tf_op jit(solution)/shard_map/assemble/pallas_call | solution.py:193
  200.2 14.7 %attend_fwd.3 = (f32[384,1024]{1,0:T(8,128)}, bf16[192,1024]{1,0:T(8,128)(2,1)}, f32[3,1,1024]{2,1,0:T(1,128)}, bf16[192,256]{1,0:T(8,128)(2,1)}, bf16[192,256]{...) custom-call(bf16[4,576,768]{2,1,0:T(8,128)(2,1)} %bitcast.112, ...), custom_call_target="tpu_custom_call" | custom-call | flops 10000000000 | bytes 6000000 | tf_op jit(solution)/shard_map/attend_fwd/pallas_call | solution.py:263
  222.4 10.2 %collective-permute-start.22 = (f32[8,128]{1,0:T(8,128)S(1)}, f32[8,128]{1,0:T(8,128)S(1)}, u32[]{:S(2)}, u32[]{:S(2)}) collective-permute-start(f32[8,128]{1,0:T(8,128)S(1)} %add_add_fusion.6), channel_id=1, source_target_pairs={{0,32},{4,36},{8,40},{12,44},{16,48},{20,52},{24,56},{28,60},{32,0... | collective-permute-start | bytes 12296 | tf_op jit(solution)/shard_map/ppermute | solution.py:766
  233.3 11.3 %mix_fwd.3 = (f32[256,768]{1,0:T(8,128)}, f32[4,256,768]{2,1,0:T(8,128)}, bf16[256,768]{1,0:T(8,128)(2,1)}, f32[256,768]{1,0:T(8,128)}, bf16[256,768]{1,0:T(8,128)(2,1)}) custom-call(f32[256,768]{1,0:T(8,128)} %get-tuple-element.153.x_ref, bf16[192,256]{1,0:T(8,128)(2,1)} %get-tuple-element.156.o0.refs_3_, bf16[192,256]{1,0:T(8,128)(2,1)} %copy-done.108, ...), custom_call_target="tpu_custom_call" | custom-call | flops 6000000000 | bytes 17000000 | tf_op jit(solution)/shard_map/mix_fwd/pallas_call | solution.py:398
  266.6 11.9 %mix_bwd.2 = (f32[256,768]{1,0:T(8,128)}, bf16[256,768]{1,0:T(8,128)(2,1)}, f32[1,768]{1,0:T(1,128)}, bf16[192,256]{1,0:T(8,128)(2,1)}, bf16[192,256]{1,0:T(8,12...) custom-call(f32[256,768]{1,0:T(8,128)} %get-tuple-element.263.g_ref, ...), custom_call_target="tpu_custom_call" | custom-call | flops 6000000000 | bytes 17000000 | tf_op jit(solution)/shard_map/mix_bwd/pallas_call | solution.py:438
  292.4 19.1 %attend_bwd.2 = (bf16[576,256]{1,0:T(8,128)(2,1)S(1)}, bf16[576,256]{1,0:T(8,128)(2,1)S(1)}, bf16[576,256]{1,0:T(8,128)(2,1)S(1)}, bf16[576,256]{1,0:T(8,128)(2,1)S(1)}, f32[64,2]{1,0:T(8,128)S(1)}) custom-call(f32[384,1024]{1,0:T(8,128)S(1)} %gate.18.pre_ref, bf16[192,1024]{1,0:T(8,128)(2,1)S(1)} %copy-done.63, f32[3,1,1024]{2,1,0:T(1,128)S(1)} %copy-done.65, ...), custom_call_target="tpu_custom_call" | custom-call | flops 20000000000 | bytes 6000000 | tf_op jit(solution)/shard_map/attend_bwd/pallas_call | solution.py:344
  317.0 12.4 %mlp_grads.2 = (bf16[16,960,128]{2,1,0:T(8,128)(2,1)}, bf16[16,960,128]{2,1,0:T(8,128)(2,1)}, f32[8,128]{1,0:T(8,128)}) custom-call(s32[96]{0:T(128)} %get-tuple-element.264.refs_0_, bf16[1024,768]{1,0:T(8,128)(2,1)} %all-gather.17.cloned.1.call-done.refs_1_, bf16[1024,768]{1,0:T(8,128)(2,1)} %all-gather.19.cloned.1.call-done.refs_2_, ...), custom_call_target="tpu_custom_call" | custom-call | flops 5000000000 | bytes 10000000 | tf_op jit(solution)/shard_map/mlp_grads/pallas_call | solution.py:548
  330.6 4.7 input_bwd.2
  336.2 11.6 %mix_bwd.3 = (f32[256,768]{1,0:T(8,128)}, bf16[256,768]{1,0:T(8,128)(2,1)}, f32[1,768]{1,0:T(1,128)}, bf16[192,256]{1,0:T(8,128)(2,1)}, bf16[192,256]{1,0:T(8,12...) custom-call(f32[256,768]{1,0:T(8,128)} %copy-done.60, bf16[256,768]{1,0:T(8,128)(2,1)} %get-tuple-element.182.low_ref, ...), custom_call_target="tpu_custom_call" | custom-call | flops 6000000000 | bytes 17000000 | tf_op jit(solution)/shard_map/mix_bwd/pallas_call | solution.py:438
  357.3 5.6 head_grads.2
  364.7 19.1 %attend_bwd.3 = (bf16[576,256]{1,0:T(8,128)(2,1)S(1)}, bf16[576,256]{1,0:T(8,128)(2,1)S(1)}, bf16[576,256]{1,0:T(8,128)(2,1)S(1)}, bf16[576,256]{1,0:T(8,128)(2,1)S(1)}, f32[64,2]{1,0:T(8,128)S(1)}) custom-call(f32[384,1024]{1,0:T(8,128)S(1)} %gate.22.pre_ref, bf16[192,1024]{1,0:T(8,128)(2,1)S(1)} %copy-done.62, f32[3,1,1024]{2,1,0:T(1,128)S(1)} %copy-done.64, ...), custom_call_target="tpu_custom_call" | custom-call | flops 20000000000 | bytes 6000000 | tf_op jit(solution)/shard_map/attend_bwd/pallas_call | solution.py:344
  389.1 12.4 %mlp_grads.3 = (bf16[16,960,128]{2,1,0:T(8,128)(2,1)}, bf16[16,960,128]{2,1,0:T(8,128)(2,1)}, f32[8,128]{1,0:T(8,128)}) custom-call(s32[96]{0:T(128)} %get-tuple-element.264.refs_0_, bf16[1024,768]{1,0:T(8,128)(2,1)} %all-gather.15.cloned.1.call-done.refs_1_, ...), custom_call_target="tpu_custom_call", output_to_operand_aliasing={{0}: (5, {}), {1}: (6, {})} | custom-call | flops 5000000000 | bytes 10000000 | tf_op jit(solution)/shard_map/mlp_grads/pallas_call | solution.py:548
  402.7 4.8 input_bwd.3
  416.3 9.1 %all-gather.21.cloned.1.call-done.refs_2_ = bf16[1024,768]{1,0:T(8,128)(2,1)} async-done(((bf16[256,768]{1,0:T(8,128)(2,1)}), bf16[1024,768]{1,0:T(8,128)(2,1)}) %all-gather.21.cloned.1.call-update) | async-done | bytes 1572880 | tf_op jit(solution)/shard_map/all_gather | solution.py:929
  425.4 5.6 head_grads.3
  435.7 6.6 %collective-permute-done.43.got = bf16[16,960,128]{2,1,0:T(8,128)(2,1)S(1)} collective-permute-done((bf16[16,960,128]{2,1,0:T(8,128)(2,1)}, bf16[16,960,128]{2,1,0:T(8,128)(2,1)S(1)}, u32[]{:S(2)}, u32[]{:S(2)}) %collective-permute-start.43) | collective-permute-done | bytes 3932192 | tf_op jit(solution)/shard_map/ppermute | solution.py:766
  454.6 4.5 collective-permute-done.44.refs_1_
  462.0 9.9 %collective-permute-done.45.refs_2_ = bf16[4,480,128]{2,1,0:T(8,128)(2,1)S(1)} collective-permute-done((bf16[4,480,128]{2,1,0:T(8,128)(2,1)S(1)}, bf16[4,480,128]{2,1,0:T(8,128)(2,1)S(1)}, u32[]{:S(2)}, u32[]{:S(2)}) %collective-permute-start.45) | collective-permute-done | bytes 491552 | tf_op jit(solution)/shard_map/ppermute | solution.py:766
  475.2 7.2 %collective-permute-done.49.refs_7_ = bf16[4,480,128]{2,1,0:T(8,128)(2,1)S(1)} collective-permute-done((bf16[4,480,128]{2,1,0:T(8,128)(2,1)S(1)}, bf16[4,480,128]{2,1,0:T(8,128)(2,1)S(1)}, u32[]{:S(2)}, u32[]{:S(2)}) %collective-permute-start.49) | collective-permute-done | bytes 491552 | tf_op jit(solution)/shard_map/ppermute | solution.py:766
  488.6 3.4 collective-permute-start.51
  499.8 3.4 collective-permute-start.57
  506.9 5.0 collective-permute-start.59
  517.1 6.0 soap_mid.1
  541.8 41.2 %soap_late.1 = (f32[3,192,192]{2,1,0:T(8,128)}, f32[3,192,192]{2,1,0:T(8,128)}, f32[3,192,192]{2,1,0:T(8,128)}, bf16[3,192,192]{2,1,0:T(8,128)(2,1)}) custom-call(f32[1,1]{1,0:T(1,128)} %bitcast.48.f_ref, f32[3,192,192]{2,1,0:T(8,128)} %copy-done.12, f32[3,192,192]{2,1,0:T(8,128)} %copy-done.17, f32[3,192,192]{2,1,0:T(8,128)} %reshape.487.right, ...), custom_call_target="tpu_custom_call" | custom-call | flops 1000000000 | bytes 10000000 | tf_op jit(solution)/shard_map/soap_late/pallas_call | solution.py:746
  594.8 3.0 fusion.20
  (608 shorter events, 211.2 us)
Async XLA Ops:
  7.2 113.6 %all-gather.11.cloned.1.call-start = ((), (), s32[]{:S(2)}) async-start(), calls=%async_computation | async-start | bytes 28532736 | tf_op jit(solution)/shard_map/all_gather | solution.py:831
  11.3 144.6 %all-gather.13.cloned.1.call-start = ((), (), s32[]{:S(2)}) async-start(), calls=%async_computation.1 | async-start | bytes 1966080 | tf_op jit(solution)/shard_map/all_gather | solution.py:833
  19.1 225.6 %all-gather.15.cloned.1.call-start = ((), (), s32[]{:S(2)}) async-start(), calls=%async_computation.2 | async-start | bytes 1966080 | tf_op jit(solution)/shard_map/all_gather | solution.py:879
  25.8 21.8 %collective-permute-start.5 = (bf16[256,768]{1,0:T(8,128)(2,1)S(1)}, bf16[256,768]{1,0:T(8,128)(2,1)}, u32[]{:S(2)}, u32[]{:S(2)}) collective-permute-start(bf16[256,768]{1,0:T(8,128)(2,1)S(1)} %multiply_convert_fusion.refs_0_), channel_id=1, source_target_pairs={{0,3},{1,2},{2,1},{3,0},{4,7},{5,6},{6,5},{7,4},{8,11},{9,10},{10,... | collective-permute-start | bytes 1179656 | tf_op jit(solution)/shard_map/ppermute | solution.py:766
  28.6 19.0 %collective-permute-start.4 = (bf16[256,768]{1,0:T(8,128)(2,1)S(1)}, bf16[256,768]{1,0:T(8,128)(2,1)}, u32[]{:S(2)}, u32[]{:S(2)}) collective-permute-start(bf16[256,768]{1,0:T(8,128)(2,1)S(1)} %multiply_convert_fusion.refs_0_), channel_id=1, source_target_pairs={{0,2},{1,3},{2,0},{3,1},{4,6},{5,7},{6,4},{7,5},{8,10},{9,11},{10,... | collective-permute-start | bytes 1179656 | tf_op jit(solution)/shard_map/ppermute | solution.py:766
  29.1 18.5 %collective-permute-start.3 = (bf16[256,768]{1,0:T(8,128)(2,1)S(1)}, bf16[256,768]{1,0:T(8,128)(2,1)}, u32[]{:S(2)}, u32[]{:S(2)}) collective-permute-start(bf16[256,768]{1,0:T(8,128)(2,1)S(1)} %multiply_convert_fusion.refs_0_), channel_id=1, source_target_pairs={{0,1},{1,0},{2,3},{3,2},{4,5},{5,4},{6,7},{7,6},{8,9},{9,8},{10,11... | collective-permute-start | bytes 1179656 | tf_op jit(solution)/shard_map/ppermute | solution.py:766
  139.7 18.3 %collective-permute-start.6 = (bf16[192,256]{1,0:T(8,128)(2,1)}, bf16[192,256]{1,0:T(8,128)(2,1)S(1)}, u32[]{:S(2)}, u32[]{:S(2)}) collective-permute-start(bf16[192,256]{1,0:T(8,128)(2,1)} %get-tuple-element.147.refs_4_), channel_id=1, source_target_pairs={{0,1},{1,0},{2,3},{3,2},{4,5},{5,4},{6,7},{7,6},{8,9},{9,8},{10,11... | collective-permute-start | bytes 294920 | tf_op jit(solution)/shard_map/ppermute | solution.py:766
  170.0 19.5 %collective-permute-start.11 = (bf16[256,768]{1,0:T(8,128)(2,1)}, bf16[256,768]{1,0:T(8,128)(2,1)S(1)}, u32[]{:S(2)}, u32[]{:S(2)}) collective-permute-start(bf16[256,768]{1,0:T(8,128)(2,1)} %get-tuple-element.155.a0.refs_11_), channel_id=1, source_target_pairs={{0,3},{1,2},{2,1},{3,0},{4,7},{5,6},{6,5},{7,4},{8,11},{9,10},{10,... | collective-permute-start | bytes 1179656 | tf_op jit(solution)/shard_map/ppermute | solution.py:766
  192.0 93.9 %all-gather.17.cloned.1.call-start = ((), (), s32[]{:S(2)}) async-start(), calls=%async_computation.3 | async-start | bytes 1966080 | tf_op jit(solution)/shard_map/all_gather | solution.py:889
  197.1 20.9 %collective-permute-start.20 = (f32[8,128]{1,0:T(8,128)S(1)}, f32[8,128]{1,0:T(8,128)S(1)}, u32[]{:S(2)}, u32[]{:S(2)}) collective-permute-start(f32[8,128]{1,0:T(8,128)S(1)} %broadcast_add_fusion), channel_id=1, source_target_pairs={{0,16},{4,20},{8,24},{12,28},{16,0},{20,4},{24,8},{28,12},{32,48},... | collective-permute-start | bytes 12296 | tf_op jit(solution)/shard_map/ppermute | solution.py:766
  199.4 19.4 %collective-permute-start.21 = (f32[8,128]{1,0:T(8,128)S(1)}, f32[8,128]{1,0:T(8,128)S(1)}, u32[]{:S(2)}, u32[]{:S(2)}) collective-permute-start(f32[8,128]{1,0:T(8,128)S(1)} %broadcast_add_fusion), channel_id=1, source_target_pairs={{0,24},{4,28},{8,16},{12,20},{16,8},{20,12},{24,0},{28,4},{32,56},... | collective-permute-start | bytes 12296 | tf_op jit(solution)/shard_map/ppermute | solution.py:766
  200.2 18.6 %collective-permute-start.19 = (f32[8,128]{1,0:T(8,128)S(1)}, f32[8,128]{1,0:T(8,128)S(1)}, u32[]{:S(2)}, u32[]{:S(2)}) collective-permute-start(f32[8,128]{1,0:T(8,128)S(1)} %broadcast_add_fusion), channel_id=1, source_target_pairs={{0,8},{4,12},{8,0},{12,4},{16,24},{20,28},{24,16},{28,20},{32,40},... | collective-permute-start | bytes 12296 | tf_op jit(solution)/shard_map/ppermute | solution.py:766
  219.4 35.2 %collective-permute-start.24 = (f32[8,128]{1,0:T(8,128)S(1)}, f32[8,128]{1,0:T(8,128)S(1)}, u32[]{:S(2)}, u32[]{:S(2)}) collective-permute-start(f32[8,128]{1,0:T(8,128)S(1)} %add_add_fusion.6), channel_id=1, source_target_pairs={{0,96},{4,100},{8,104},{12,108},{16,112},{20,116},{24,120},{28,124... | collective-permute-start | bytes 12296 | tf_op jit(solution)/shard_map/ppermute | solution.py:766
  221.9 34.0 %collective-permute-start.23 = (f32[8,128]{1,0:T(8,128)S(1)}, f32[8,128]{1,0:T(8,128)S(1)}, u32[]{:S(2)}, u32[]{:S(2)}) collective-permute-start(f32[8,128]{1,0:T(8,128)S(1)} %add_add_fusion.6), channel_id=1, source_target_pairs={{0,64},{4,68},{8,72},{12,76},{16,80},{20,84},{24,88},{28,92},{32,9... | collective-permute-start | bytes 12296 | tf_op jit(solution)/shard_map/ppermute | solution.py:766
  222.4 33.4 %collective-permute-start.22 = (f32[8,128]{1,0:T(8,128)S(1)}, f32[8,128]{1,0:T(8,128)S(1)}, u32[]{:S(2)}, u32[]{:S(2)}) collective-permute-start(f32[8,128]{1,0:T(8,128)S(1)} %add_add_fusion.6), channel_id=1, source_target_pairs={{0,32},{4,36},{8,40},{12,44},{16,48},{20,52},{24,56},{28,60},{32,0... | collective-permute-start | bytes 12296 | tf_op jit(solution)/shard_map/ppermute | solution.py:766
  256.4 60.6 %all-gather.19.cloned.1.call-start = ((), (), s32[]{:S(2)}) async-start(), calls=%async_computation.4 | async-start | bytes 1966080 | tf_op jit(solution)/shard_map/all_gather | solution.py:924
  263.3 90.6 %all-gather.23.cloned.1.call-start = ((), (), s32[]{:S(2)}) async-start(), calls=%async_computation.6 | async-start | bytes 1966080 | tf_op jit(solution)/shard_map/all_gather | solution.py:929
  288.3 100.8 %all-gather.25.cloned.1.call-start = ((), (), s32[]{:S(2)}) async-start(), calls=%async_computation.7 | async-start | bytes 1966080 | tf_op jit(solution)/shard_map/all_gather | solution.py:924
  312.3 17.9 %collective-permute-start.28 = (bf16[576,256]{1,0:T(8,128)(2,1)S(1)}, bf16[576,256]{1,0:T(8,128)(2,1)}, u32[]{:S(2)}, u32[]{:S(2)}) collective-permute-start(bf16[576,256]{1,0:T(8,128)(2,1)S(1)} %get-tuple-element.178.refs_8_), channel_id=1, source_target_pairs={{0,1},{1,0},{2,3},{3,2},{4,5},{5,4},{6,7},{7,6},{8,9},{9,8},{10,11... | collective-permute-start | bytes 884744 | tf_op jit(solution)/shard_map/ppermute | solution.py:766
  312.5 17.7 %collective-permute-start.29 = (bf16[576,256]{1,0:T(8,128)(2,1)S(1)}, bf16[576,256]{1,0:T(8,128)(2,1)}, u32[]{:S(2)}, u32[]{:S(2)}) collective-permute-start(bf16[576,256]{1,0:T(8,128)(2,1)S(1)} %get-tuple-element.179.refs_9_), channel_id=1, source_target_pairs={{0,2},{1,3},{2,0},{3,1},{4,6},{5,7},{6,4},{7,5},{8,10},{9,11},{10,... | collective-permute-start | bytes 884744 | tf_op jit(solution)/shard_map/ppermute | solution.py:766
  349.2 76.2 %all-gather.21.cloned.1.call-start = ((), (), s32[]{:S(2)}) async-start(), calls=%async_computation.5 | async-start | bytes 1966080 | tf_op jit(solution)/shard_map/all_gather | solution.py:929
  384.1 18.3 %collective-permute-start.34 = (bf16[576,256]{1,0:T(8,128)(2,1)S(1)}, bf16[576,256]{1,0:T(8,128)(2,1)S(1)}, u32[]{:S(2)}, u32[]{:S(2)}) collective-permute-start(bf16[576,256]{1,0:T(8,128)(2,1)S(1)} %get-tuple-element.198.refs_8_), channel_id=1, source_target_pairs={{0,1},{1,0},{2,3},{3,2},{4,5},{5,4},{6,7},{7,6},{8,9},{9,8},{10,11... | collective-permute-start | bytes 884744 | tf_op jit(solution)/shard_map/ppermute | solution.py:766
  384.1 18.3 %collective-permute-start.35 = (bf16[576,256]{1,0:T(8,128)(2,1)S(1)}, bf16[576,256]{1,0:T(8,128)(2,1)S(1)}, u32[]{:S(2)}, u32[]{:S(2)}) collective-permute-start(bf16[576,256]{1,0:T(8,128)(2,1)S(1)} %get-tuple-element.199.refs_9_), channel_id=1, source_target_pairs={{0,2},{1,3},{2,0},{3,1},{4,6},{5,7},{6,4},{7,5},{8,10},{9,11},{10,... | collective-permute-start | bytes 884744 | tf_op jit(solution)/shard_map/ppermute | solution.py:766
  388.9 201.0 %all-gather.27.cloned.1.call-start = ((), (), s32[]{:S(2)}) async-start(), calls=%async_computation.8 | async-start | bytes 1622016 | tf_op jit(solution)/shard_map/all_gather | solution.py:996
  411.4 20.3 %collective-permute-start.37 = (bf16[256,192]{1,0:T(8,128)(2,1)S(1)}, bf16[256,192]{1,0:T(8,128)(2,1)S(1)}, u32[]{:S(2)}, u32[]{:S(2)}) collective-permute-start(bf16[256,192]{1,0:T(8,128)(2,1)S(1)} %pad_maximum_fusion.4), channel_id=1, source_target_pairs={{0,1},{1,0},{2,3},{3,2},{4,5},{5,4},{6,7},{7,6},{8,9},{9,8},{10,11... | collective-permute-start | bytes 294920 | tf_op jit(solution)/shard_map/ppermute | solution.py:766
  411.5 20.2 %collective-permute-start.38 = (bf16[256,192]{1,0:T(8,128)(2,1)S(1)}, bf16[256,192]{1,0:T(8,128)(2,1)S(1)}, u32[]{:S(2)}, u32[]{:S(2)}) collective-permute-start(bf16[256,192]{1,0:T(8,128)(2,1)S(1)} %pad_maximum_fusion.5), channel_id=1, source_target_pairs={{0,2},{1,3},{2,0},{3,1},{4,6},{5,7},{6,4},{7,5},{8,10},{9,11},{10,... | collective-permute-start | bytes 294920 | tf_op jit(solution)/shard_map/ppermute | solution.py:766
  414.1 17.6 %collective-permute-start.39 = (bf16[256,192]{1,0:T(8,128)(2,1)S(1)}, bf16[256,192]{1,0:T(8,128)(2,1)S(1)}, u32[]{:S(2)}, u32[]{:S(2)}) collective-permute-start(bf16[256,192]{1,0:T(8,128)(2,1)S(1)} %pad_maximum_fusion.6), channel_id=1, source_target_pairs={{0,3},{1,2},{2,1},{3,0},{4,7},{5,6},{6,5},{7,4},{8,11},{9,10},{10,... | collective-permute-start | bytes 294920 | tf_op jit(solution)/shard_map/ppermute | solution.py:766
  447.9 24.0 %collective-permute-start.45 = (bf16[4,480,128]{2,1,0:T(8,128)(2,1)S(1)}, bf16[4,480,128]{2,1,0:T(8,128)(2,1)S(1)}, u32[]{:S(2)}, u32[]{:S(2)}) collective-permute-start(bf16[4,480,128]{2,1,0:T(8,128)(2,1)S(1)} %get-tuple-element.219), channel_id=1, source_target_pairs={{0,64},{4,68},{8,72},{12,76},{16,80},{20,84},{24,88},{28,92},{32,9... | collective-permute-start | bytes 1474568 | tf_op jit(solution)/shard_map/ppermute | solution.py:766
  450.3 23.5 %collective-permute-start.46 = (bf16[4,480,128]{2,1,0:T(8,128)(2,1)S(1)}, bf16[4,480,128]{2,1,0:T(8,128)(2,1)S(1)}, u32[]{:S(2)}, u32[]{:S(2)}) collective-permute-start(bf16[4,480,128]{2,1,0:T(8,128)(2,1)S(1)} %get-tuple-element.220), channel_id=1, source_target_pairs={{0,96},{4,100},{8,104},{12,108},{16,112},{20,116},{24,120},{28,124... | collective-permute-start | bytes 1474568 | tf_op jit(solution)/shard_map/ppermute | solution.py:766
  450.5 23.3 %collective-permute-start.47 = (bf16[4,480,128]{2,1,0:T(8,128)(2,1)S(1)}, bf16[4,480,128]{2,1,0:T(8,128)(2,1)S(1)}, u32[]{:S(2)}, u32[]{:S(2)}) collective-permute-start(bf16[4,480,128]{2,1,0:T(8,128)(2,1)S(1)} %get-tuple-element.222), channel_id=1, source_target_pairs={{0,8},{4,12},{8,0},{12,4},{16,24},{20,28},{24,16},{28,20},{32,40},... | collective-permute-start | bytes 1474568 | tf_op jit(solution)/shard_map/ppermute | solution.py:766
  451.8 23.4 %collective-permute-start.48 = (bf16[4,480,128]{2,1,0:T(8,128)(2,1)S(1)}, bf16[4,480,128]{2,1,0:T(8,128)(2,1)S(1)}, u32[]{:S(2)}, u32[]{:S(2)}) collective-permute-start(bf16[4,480,128]{2,1,0:T(8,128)(2,1)S(1)} %get-tuple-element.223), channel_id=1, source_target_pairs={{0,16},{4,20},{8,24},{12,28},{16,0},{20,4},{24,8},{28,12},{32,48},... | collective-permute-start | bytes 1474568 | tf_op jit(solution)/shard_map/ppermute | solution.py:766
  459.1 23.3 %collective-permute-start.49 = (bf16[4,480,128]{2,1,0:T(8,128)(2,1)S(1)}, bf16[4,480,128]{2,1,0:T(8,128)(2,1)S(1)}, u32[]{:S(2)}, u32[]{:S(2)}) collective-permute-start(bf16[4,480,128]{2,1,0:T(8,128)(2,1)S(1)} %get-tuple-element.224), channel_id=1, source_target_pairs={{0,24},{4,28},{8,16},{12,20},{16,8},{20,12},{24,0},{28,4},{32,56},... | collective-permute-start | bytes 1474568 | tf_op jit(solution)/shard_map/ppermute | solution.py:766
  (159 other events, 1140.8 us)
Sparse Core Ops, SparseCore 0:
  11.6 109.1 all-gather.10
  123.0 28.2 all-gather.12
  192.1 27.1 all-gather.14
  256.5 29.2 all-gather.16
  287.9 29.0 all-gather.18
  318.5 27.4 all-gather.22
  349.3 30.9 all-gather.24
  389.0 36.3 all-gather.20
  532.8 43.4 all-gather.26

commit v3 on v2

--- a/solution.py
+++ b/solution.py
@@ -223,18 +223,26 @@
     return centered * inverse, inverse
 
 
+def by_three(step):
+    def turn(i, carry):
+        for j in range(3):
+            carry = step(3 * i + j, carry)
+        return carry
+
+    lax.fori_loop(0, 4 * HEADS // 3, turn, 0)
+
+
 def attend_fwd(w_ref, a0, a1, a2, a3, gain_ref, qid_ref, kid_ref, pre_ref, v_ref, lse_ref, o0, o1, o2, o3, q_s, k_s, o_s):
-    for c in range(3):
-        for r, a_ref in enumerate((a0, a1, a2, a3)):
-            cols = slice(OWN * r, OWN * r + OWN)
-            part = mm(w_ref[0, TILE * c : TILE * c + TILE, :], a_ref[...], 1, 1)
-            if c == 2:
-                v_ref[:, cols] = part.astype(bf16)
-                continue
-            pre_ref[TILE * c : TILE * c + TILE, cols] = part
+    for r, a_ref in enumerate((a0, a1, a2, a3)):
+        cols = slice(OWN * r, OWN * r + OWN)
+        projected = mm(w_ref[0], a_ref[...], 1, 1)
+        v_ref[:, cols] = projected[2 * TILE :].astype(bf16)
+        pre_ref[:, cols] = projected[: 2 * TILE]
+        for c in range(2):
             for h in range(HEADS):
                 rows = slice(HD * h, HD * h + HD)
-                low = (column_norm(part[rows, :])[0] * gain_ref[:, c : c + 1]).astype(bf16)
+                part = projected[TILE * c + HD * h : TILE * c + HD * h + HD]
+                low = (column_norm(part)[0] * gain_ref[:, c : c + 1]).astype(bf16)
                 if c == 0:
                     q_s[r, rows, :] = low * bf16(0.125)
                 else:
@@ -254,7 +262,7 @@
         o_s[t, rows, :] = mm(v_ref[rows, :], probs).astype(bf16)
         return carry
 
-    lax.fori_loop(0, 4 * HEADS, step, 0)
+    by_three(step)
     for r, ref in enumerate((o0, o1, o2, o3)):
         ref[...] = o_s[r]
 
@@ -317,7 +325,7 @@
         dk_s[h] += mm(grad_scores, qn_s[h, cols, :])
         return carry
 
-    lax.fori_loop(0, 4 * HEADS, step, 0)
+    by_three(step)
     for c in range(2):
         total = jnp.zeros((HD, 1), f32)
         for h in range(HEADS):
@@ -357,7 +365,7 @@
             pltpu.VMEM((HEADS, TOKENS, HD), f32),
             pltpu.VMEM((HEADS, TOKENS, HD), f32),
         ],
-        compiler_params=params(48),
+        compiler_params=params(60),
         cost_estimate=cost(2 * 10**10, 6 * 10**6, 3 * 2**20),
         name="attend_bwd",
     )(pre, v, lse, *grads, gains, qid, kid)
@@ -654,68 +662,115 @@
     gr_ref[0] = mm_full(grad_t, grad, 1, 0)
 
 
-def factor_inverses(grams):
+def factor_inverses(grams, fillers=()):
     size = 64
+    fillers = list(fillers)
     row = lax.broadcasted_iota(jnp.int32, (8, 128), 0)
     lane = lax.broadcasted_iota(jnp.int32, (8, 128), 1)
-    states = []
+    on_diagonal = lax.broadcasted_iota(jnp.int32, (size, size), 0) == lax.broadcasted_iota(
+        jnp.int32, (size, size), 1
+    )
+    states, scales = ([], [])
     for gram in grams:
-        wide = jnp.concatenate([gram, jnp.zeros((size, size), f32)], axis=1)
+        diagonal = jnp.where(on_diagonal, gram, 0.0)
+        scale_row = lax.rsqrt(jnp.sum(diagonal, axis=0, keepdims=True))
+        scale_column = lax.rsqrt(jnp.sum(diagonal, axis=1, keepdims=True))
+        scales.append(scale_row)
+        wide = jnp.concatenate([gram * scale_row * scale_column, jnp.zeros((size, size), f32)], axis=1)
         states.append(
             [jnp.where(lane == row + (size + 8 * t), 1.0, wide[8 * t : 8 * t + 8, :]) for t in range(8)]
         )
-    for k in range(size):
+    for k in range(0, size, 2):
         home, at = divmod(k, 8)
         for tiles in states:
-            pivot = tiles[home][at : at + 1, k : k + 1]
-            line = tiles[home][at : at + 1, :] * (1.0 / pivot)
+            own = tiles[home]
+            first, second = (own[at : at + 1, :], own[at + 1 : at + 2, :])
+            a, b, c = (
+                jnp.broadcast_to(entry, (1, 128))
+                for entry in (first[:, k : k + 1], first[:, k + 1 : k + 2], second[:, k + 1 : k + 2])
+            )
+            inverse = 1.0 / (a * c - b * b)
+            line_first = (c * first - b * second) * inverse
+            line_second = (a * second - b * first) * inverse
             for t in range(home, 8):
-                update = tiles[t][:, k : k + 1] * line
+                update = tiles[t][:, k : k + 1] * line_first + tiles[t][:, k + 1 : k + 2] * line_second
                 if t == home:
-                    update = jnp.where(row > at, update, 0.0)
+                    inside = jnp.where(row == at + 1, first * (b / a), 0.0)
+                    update = jnp.where(row > at + 1, update, inside)
                 tiles[t] = tiles[t] - update
+        if fillers:
+            fillers.pop(0)()
+    for filler in fillers:
+        filler()
     inverses = []
-    for tiles in states:
+    for tiles, scale_row in zip(states, scales):
         done = []
         for t in range(8):
             diagonal = jnp.sum(jnp.where(lane == row + 8 * t, tiles[t], 0.0), axis=1, keepdims=True)
             done.append(tiles[t] * lax.rsqrt(diagonal))
-        inverses.append(jnp.concatenate(done, axis=0)[:, size:])
+        inverses.append(jnp.concatenate(done, axis=0)[:, size:] * scale_row)
     return inverses
 
 
 def soap_late(
     f_ref, second, left, right, weight, turned, turned_first, xl, xr, yl, yr,
-    weight_ref, left_ref, right_ref, low_ref, panels,
+    weight_ref, left_ref, right_ref, low_ref, panels, work,
 ):
     factor = f_ref[0, 0]
     bias_one = 1.0 - first_decay**STEP
     bias_two = 1.0 - second_decay**STEP
-    for n in range(3):
+    outs = (left_ref, right_ref)
+
+    def product(i):
+        n, (old, new) = (i // 2, ((xl, yl), (xr, yr))[i % 2])
+        total = second_decay * old[n] + (1.0 - second_decay) * (factor * (factor * new[n]))
+        for j in range(3):
+            panels[i, j] = total[:, 64 * j : 64 * j + 64]
+
+    def scaled(n):
         rotated = turned[n] * factor
         second_new = second_decay * second[n] + (1.0 - second_decay) * rotated * rotated
-        scaled = (
+        work[n] = (
             (first_decay * turned_first[n] + (1.0 - first_decay) * rotated)
             / bias_one
             / (jnp.sqrt(second_new / bias_two) + adam_epsilon)
         )
-        back = mm_split(mm_split(left[n], scaled, 1, 0), right[n], 1, 1)
+
+    def half_back(n):
+        work[n] = mm_split(left[n], work[n], 1, 0)
+
+    def move(n):
+        back = mm_split(work[n], right[n], 1, 1)
         weight_new = weight[n] * (1.0 - matrix_rate * weight_decay) - matrix_rate * back
         weight_ref[n] = weight_new
         low_ref[n] = weight_new.astype(bf16)
-        for side, (old, new) in enumerate(((xl, yl), (xr, yr))):
-            product = second_decay * old[n] + (1.0 - second_decay) * (factor * (factor * new[n]))
-            for j in range(3):
-                panels[2 * n + side, j] = product[:, 64 * j : 64 * j + 64]
-    outs = (left_ref, right_ref)
-    for j in range(3):
-        inverses = factor_inverses([mm_full(panels[i, j], panels[i, j], 0, 0) for i in range(6)])
+
+    def remove(i, basis, k):
+        panel = panels[i, k]
+        panels[i, k] = panel - mm_full(basis, mm_full(basis, panel, 0, 0), 1, 0)
+
+    def grams(j):
+        return [mm_full(panels[i, j], panels[i, j], 0, 0) for i in range(6)]
+
+    def bases(j, inverses):
+        found = []
         for i in range(6):
             basis = mm_full(panels[i, j], inverses[i], 1, 1)
             outs[i % 2][i // 2, :, 64 * j : 64 * j + 64] = basis
-            for k in range(j + 1, 3):
-                panel = panels[i, k]
-                panels[i, k] = panel - mm_full(basis, mm_full(basis, panel, 0, 0), 1, 0)
+            found.append(basis)
+        return found
+
+    for i in range(6):
+        product(i)
+    pieces = [lambda step=step, n=n: step(n) for n in range(3) for step in (scaled, half_back, move)]
+    found = bases(0, factor_inverses(grams(0), pieces))
+    for i in range(6):
+        remove(i, found[i], 1)
+    pieces = [lambda i=i, basis=found[i]: remove(i, basis, 2) for i in range(6)]
+    found = bases(1, factor_inverses(grams(1), pieces))
+    for i in range(6):
+        remove(i, found[i], 2)
+    bases(2, factor_inverses(grams(2)))
 
 
 def tile_spec():
@@ -746,7 +801,7 @@
     return pl.pallas_call(
         soap_late, in_specs=[SM] + [VM] * 10, out_specs=[VM] * 4,
         out_shape=tiles_of_three(3) + [shape((3, TILE, TILE), bf16)],
-        scratch_shapes=[pltpu.VMEM((6, 3, TILE, 64), f32)],
+        scratch_shapes=[pltpu.VMEM((6, 3, TILE, 64), f32), pltpu.VMEM((3, TILE, TILE), f32)],
         compiler_params=params(56), cost_estimate=cost(10**9, 10**7), name="soap_late",
     )(*args)
 
@@ -848,7 +903,8 @@
     present = (counts > 0).astype(f32)
     divisor = jnp.maximum(counts, 1.0)
     member = ((ids[0][:, None] == jnp.arange(IMGS)[None, :]) & kept[0][:, None]).astype(f32)
-    image_total = total_dp(jnp.full((8, 128), jnp.sum(present), f32))[0, 0]
+    image_sum = total_dp(jnp.full((8, 128), jnp.sum(present), f32))
+    image_total = image_sum[0, 0]
 
     first_tiles, second_tiles = (tiled(soap_first), tiled(soap_second))
     left_stat, right_stat = (tiled(stat_left), tiled(stat_right))
@@ -873,7 +929,7 @@
         gains = head_gains[depth].T
         acts = gather_mp(act)
         if depth == 0:
-            acts[0] = gate(acts[0], turned_first, second_tiles)
+            acts[0] = gate(acts[0], turned_first, second_tiles, image_sum)
         else:
             normed = gate(normed, *acts[1:], qkv)
             saved[-1].append(lax.all_gather(normed, "mp", axis=0, tiled=True))

time: 619 us -> 586 us (0.947)
  Pallas kernels: 239 us -> 216 us
  starting transfers between devices: 100 us -> 93.7 us
    pallas_call x1, Pallas kernels: 41.2 us -> 23.5 us  [run_soap_late(): pl.pallas_call(soap_late, in_specs=[SM] + [VM] * 10, out_specs=[VM] * 4,...]
    all_gather x1, waiting for transfers between devices: 72.4 us -> 56.1 us  [shards(): slots = lax.all_gather(pack_tile(low), ('dp', 'mp'), axis=0, tiled=True)]
    ppermute x66, waiting for transfers between devices: 51.4 us -> 63.5 us  [swap(): return lax.ppermute(array, axis, [(i, i ^ r) for i in range(size)])]
    all_gather x2, waiting for transfers between devices: 0.68 us -> 8.6 us  [shards(): lows = lax.all_gather(grad_low, 'mp', axis=0, tiled=True)]
    ppermute x66, starting transfers between devices: 99.7 us -> 92.6 us  [swap(): return lax.ppermute(array, axis, [(i, i ^ r) for i in range(size)])]
    all_gather x2, waiting for transfers between devices: 9.14 us -> 2.32 us  [shards(): mid_lows = lax.all_gather(gate(mid_low, *dos[1:]), 'mp', axis=0, tiled=True)]
    unnamed x239 -> x193, local copies, waits for them, and re-layouts: 38.9 us -> 38.4 us
  transfers between devices with their start and end apart: 75 -> 75, of which waited for: 21 -> 27; matrix products, arithmetic and copies ran while one was open for 10% -> 9% of each run, Pallas kernels for 37% -> 35%
where the time goes in v3:
time: 586 us; the launch traced here: 578 us
  Pallas kernels  216 us (37%)
  waiting for transfers between devices  136 us (23%)
  starting transfers between devices  93.7 us (16%)
  local copies, waits for them, and re-layouts  75.5 us (13%)
  other arithmetic  30 us (5%)
  between operations  20.3 us (3%)
  matrix products  6.24 us (1%)
    ppermute x66, starting transfers between devices, swap(): return lax.ppermute(array, axis, [(i, i ^ r) for i in range(size)])  92.6 us
    ppermute x66, waiting for transfers between devices, swap(): return lax.ppermute(array, axis, [(i, i ^ r) for i in range(size)])  63.5 us
    all_gather x1, waiting for transfers between devices, shards(): slots = lax.all_gather(pack_tile(low), ('dp', 'mp'), axis=0, tiled=True)  56.1 us
    unnamed x193, local copies, waits for them, and re-layouts  38.4 us
    pallas_call x4, Pallas kernels, grads_call(): pl.pallas_call(kernel, grid=(1,), in_specs=[SM] * len(scalars) + specs +...  35.9 us
    pallas_call x2, Pallas kernels, run_attend_bwd(): pl.pallas_call(attend_bwd, in_specs=[VM] * 10, out_specs=[VM] * 5, out_sh...  35.2 us
    pallas_call x2, Pallas kernels, run_attend_fwd(): pl.pallas_call(attend_fwd, grid=(1,), in_specs=[pl.BlockSpec((1, 3 * TILE...  27.6 us
    pallas_call x3, Pallas kernels, assemble(): pl.pallas_call(kernel, in_specs=[SM, ANY], out_specs=[ANY] * len(groups),...  27.5 us
  transfers between devices with their start and end apart: 75, of which 27 were waited for; matrix products, arithmetic and copies ran while one was open for 9% of the time, Pallas kernels for 35%

profile of v3, /device:TPU:1, one launch (start us, length us, event | category | flops | bytes accessed | tf_op | source)
XLA Modules:
  0.0 577.6 jit_solution(18187906470619769423)
XLA Ops:
  26.6 3.7 collective-permute-start.5
  58.8 5.4 collective-permute-done.12.a3.refs_14_
  65.0 56.1 %all-gather.11.cloned.1.call-done.slots_ref = bf16[384,288,128]{2,1,0:T(8,128)(2,1)} async-done(((bf16[3,288,128]{2,1,0:T(8,128)(2,1)}), bf16[384,288,128]{2,1,0:T(8,128)(2,1)}) %all-gather.11.cloned.1.call-update) | async-done | bytes 28311568 | tf_op jit(solution)/shard_map/all_gather | solution.py:886
  121.1 4.3 assemble.3
  125.4 13.8 %attend_fwd.2 = (f32[384,1024]{1,0:T(8,128)}, bf16[192,1024]{1,0:T(8,128)(2,1)}, f32[3,1,1024]{2,1,0:T(1,128)}, bf16[192,256]{1,0:T(8,128)(2,1)}, bf16[192,256]{...) custom-call(bf16[4,576,768]{2,1,0:T(8,128)(2,1)} %bitcast.116, bf16[256,768]{1,0:T(8,128)(2,1)} %copy-done.13, ...), custom_call_target="tpu_custom_call" | custom-call | flops 10000000000 | bytes 6000000 | tf_op jit(solution)/shard_map/attend_fwd/pallas_call | solution.py:271
  144.9 10.2 %assemble.4 = (bf16[4,192,768]{2,1,0:T(8,128)(2,1)}, bf16[16,192,768]{2,1,0:T(8,128)(2,1)}, bf16[16,192,768]{2,1,0:T(8,128)(2,1)}) custom-call(s32[384]{0:T(512)} %add.333.table_ref, bf16[384,288,128]{2,1,0:T(8,128)(2,1)} %all-gather.11.cloned.1.call-done.slots_ref), custom_call_target="tpu_custom_call" | custom-call | bytes 21233664 | tf_op jit(solution)/shard_map/assemble/pallas_call | solution.py:193
  157.9 11.2 %mix_fwd.2 = (f32[256,768]{1,0:T(8,128)}, f32[4,256,768]{2,1,0:T(8,128)}, bf16[256,768]{1,0:T(8,128)(2,1)}, f32[256,768]{1,0:T(8,128)}, bf16[256,768]{1,0:T(8,128)(2,1)}) custom-call(f32[256,768]{1,0:T(8,128)} %convert_element_type.70.x_ref, bf16[192,256]{1,0:T(8,128)(2,1)} %copy-done.41, bf16[192,256]{1,0:T(8,128)(2,1)} %copy-done.85, ...), custom_call_target="tpu_custom_call" | custom-call | flops 6000000000 | bytes 17000000 | tf_op jit(solution)/shard_map/mix_fwd/pallas_call | solution.py:406
  172.5 13.0 %assemble.5 = (bf16[12,192,768]{2,1,0:T(8,128)(2,1)}, bf16[4,192,768]{2,1,0:T(8,128)(2,1)}, bf16[16,192,768]{2,1,0:T(8,128)(2,1)}, bf16[16,192,768]{2,1,0:T(8,128)(2,1)}) custom-call(s32[384]{0:T(512)} %add.333.table_ref, bf16[384,288,128]{2,1,0:T(8,128)(2,1)} %all-gather.11.cloned.1.call-done.slots_ref), custom_call_target="tpu_custom_call" | custom-call | bytes 28311552 | tf_op jit(solution)/shard_map/assemble/pallas_call | solution.py:193
  192.5 13.8 %attend_fwd.3 = (f32[384,1024]{1,0:T(8,128)}, bf16[192,1024]{1,0:T(8,128)(2,1)}, f32[3,1,1024]{2,1,0:T(1,128)}, bf16[192,256]{1,0:T(8,128)(2,1)}, bf16[192,256]{...) custom-call(bf16[4,576,768]{2,1,0:T(8,128)(2,1)} %bitcast.112, ...), custom_call_target="tpu_custom_call" | custom-call | flops 10000000000 | bytes 6000000 | tf_op jit(solution)/shard_map/attend_fwd/pallas_call | solution.py:271
  207.1 3.5 collective-permute-start.20
  212.5 7.4 %collective-permute-done.20.o2 = bf16[192,256]{1,0:T(8,128)(2,1)S(1)} collective-permute-done((bf16[192,256]{1,0:T(8,128)(2,1)}, bf16[192,256]{1,0:T(8,128)(2,1)S(1)}, u32[]{:S(2)}, u32[]{:S(2)}) %collective-permute-start.20) | collective-permute-done | bytes 98336 | tf_op jit(solution)/shard_map/ppermute | solution.py:821
  220.5 11.4 %mix_fwd.3 = (f32[256,768]{1,0:T(8,128)}, f32[4,256,768]{2,1,0:T(8,128)}, bf16[256,768]{1,0:T(8,128)(2,1)}, f32[256,768]{1,0:T(8,128)}, bf16[256,768]{1,0:T(8,128)(2,1)}) custom-call(f32[256,768]{1,0:T(8,128)} %get-tuple-element.153.x_ref, bf16[192,256]{1,0:T(8,128)(2,1)} %get-tuple-element.156.o0.refs_3_, bf16[192,256]{1,0:T(8,128)(2,1)} %copy-done.88, ...), custom_call_target="tpu_custom_call" | custom-call | flops 6000000000 | bytes 17000000 | tf_op jit(solution)/shard_map/mix_fwd/pallas_call | solution.py:406
  250.7 11.7 %mix_bwd.2 = (f32[256,768]{1,0:T(8,128)}, bf16[256,768]{1,0:T(8,128)(2,1)}, f32[1,768]{1,0:T(1,128)}, bf16[192,256]{1,0:T(8,128)(2,1)}, bf16[192,256]{1,0:T(8,12...) custom-call(f32[256,768]{1,0:T(8,128)} %get-tuple-element.263.g_ref, ...), custom_call_target="tpu_custom_call" | custom-call | flops 6000000000 | bytes 17000000 | tf_op jit(solution)/shard_map/mix_bwd/pallas_call | solution.py:446
  274.4 17.6 %attend_bwd.2 = (bf16[576,256]{1,0:T(8,128)(2,1)}, bf16[576,256]{1,0:T(8,128)(2,1)}, bf16[576,256]{1,0:T(8,128)(2,1)}, bf16[576,256]{1,0:T(8,128)(2,1)}, f32[64,2]{1,0:T(8,128)}) custom-call(f32[384,1024]{1,0:T(8,128)} %copy-done.29, bf16[192,1024]{1,0:T(8,128)(2,1)} %get-tuple-element.171.v_ref, f32[3,1,1024]{2,1,0:T(1,128)} %get-tuple-element.172.lse_ref, ...), custom_call_target="tpu_custom_call" | custom-call | flops 20000000000 | bytes 6000000 | tf_op jit(solution)/shard_map/attend_bwd/pallas_call | solution.py:352
  296.9 8.6 %all-gather.19.cloned.1.call-done.refs_2_ = bf16[1024,768]{1,0:T(8,128)(2,1)} async-done(((bf16[256,768]{1,0:T(8,128)(2,1)}), bf16[1024,768]{1,0:T(8,128)(2,1)}) %all-gather.19.cloned.1.call-update) | async-done | bytes 1572880 | tf_op jit(solution)/shard_map/all_gather | solution.py:980
  305.5 12.4 %mlp_grads.2 = (bf16[16,960,128]{2,1,0:T(8,128)(2,1)}, bf16[16,960,128]{2,1,0:T(8,128)(2,1)}, f32[8,128]{1,0:T(8,128)}) custom-call(s32[96]{0:T(128)} %get-tuple-element.264.refs_0_, bf16[1024,768]{1,0:T(8,128)(2,1)} %all-gather.17.cloned.1.call-done.refs_1_, bf16[1024,768]{1,0:T(8,128)(2,1)} %all-gather.19.cloned.1.call-done.refs_2_, ...), custom_call_target="tpu_custom_call" | custom-call | flops 5000000000 | bytes 10000000 | tf_op jit(solution)/shard_map/mlp_grads/pallas_call | solution.py:556
  319.2 4.4 input_bwd.2
  324.5 11.6 %mix_bwd.3 = (f32[256,768]{1,0:T(8,128)}, bf16[256,768]{1,0:T(8,128)(2,1)}, f32[1,768]{1,0:T(1,128)}, bf16[192,256]{1,0:T(8,128)(2,1)}, bf16[192,256]{1,0:T(8,12...) custom-call(f32[256,768]{1,0:T(8,128)} %copy-done.57, bf16[256,768]{1,0:T(8,128)(2,1)} %get-tuple-element.182.low_ref, ...), custom_call_target="tpu_custom_call" | custom-call | flops 6000000000 | bytes 17000000 | tf_op jit(solution)/shard_map/mix_bwd/pallas_call | solution.py:446
  345.7 5.6 head_grads.2
  353.9 17.6 %attend_bwd.3 = (bf16[576,256]{1,0:T(8,128)(2,1)}, bf16[576,256]{1,0:T(8,128)(2,1)}, bf16[576,256]{1,0:T(8,128)(2,1)}, bf16[576,256]{1,0:T(8,128)(2,1)}, f32[64,2]{1,0:T(8,128)}) custom-call(f32[384,1024]{1,0:T(8,128)} %copy-done.27, bf16[192,1024]{1,0:T(8,128)(2,1)} %get-tuple-element.195.v_ref, f32[3,1,1024]{2,1,0:T(1,128)} %get-tuple-element.196.lse_ref, ...), custom_call_target="tpu_custom_call" | custom-call | flops 20000000000 | bytes 6000000 | tf_op jit(solution)/shard_map/attend_bwd/pallas_call | solution.py:352
  372.6 3.3 collective-permute-start.35
  379.3 12.4 %mlp_grads.3 = (bf16[16,960,128]{2,1,0:T(8,128)(2,1)}, bf16[16,960,128]{2,1,0:T(8,128)(2,1)}, f32[8,128]{1,0:T(8,128)}) custom-call(s32[96]{0:T(128)} %get-tuple-element.264.refs_0_, bf16[1024,768]{1,0:T(8,128)(2,1)} %all-gather.15.cloned.1.call-done.refs_1_, ...), custom_call_target="tpu_custom_call", output_to_operand_aliasing={{0}: (5, {}), {1}: (6, {})} | custom-call | flops 5000000000 | bytes 10000000 | tf_op jit(solution)/shard_map/mlp_grads/pallas_call | solution.py:556
  392.9 4.6 input_bwd.3
  408.6 5.6 head_grads.3
  420.8 6.6 %collective-permute-done.43.got = bf16[16,960,128]{2,1,0:T(8,128)(2,1)S(1)} collective-permute-done((bf16[16,960,128]{2,1,0:T(8,128)(2,1)}, bf16[16,960,128]{2,1,0:T(8,128)(2,1)S(1)}, u32[]{:S(2)}, u32[]{:S(2)}) %collective-permute-start.43) | collective-permute-done | bytes 3932192 | tf_op jit(solution)/shard_map/ppermute | solution.py:821
  439.1 5.2 collective-permute-done.44.refs_1_
  446.5 10.5 %collective-permute-done.45.refs_2_ = bf16[4,480,128]{2,1,0:T(8,128)(2,1)S(1)} collective-permute-done((bf16[4,480,128]{2,1,0:T(8,128)(2,1)S(1)}, bf16[4,480,128]{2,1,0:T(8,128)(2,1)S(1)}, u32[]{:S(2)}, u32[]{:S(2)}) %collective-permute-start.45) | collective-permute-done | bytes 491552 | tf_op jit(solution)/shard_map/ppermute | solution.py:821
  459.7 7.8 %collective-permute-done.49.refs_7_ = bf16[4,480,128]{2,1,0:T(8,128)(2,1)S(1)} collective-permute-done((bf16[4,480,128]{2,1,0:T(8,128)(2,1)S(1)}, bf16[4,480,128]{2,1,0:T(8,128)(2,1)S(1)}, u32[]{:S(2)}, u32[]{:S(2)}) %collective-permute-start.49) | collective-permute-done | bytes 491552 | tf_op jit(solution)/shard_map/ppermute | solution.py:821
  473.2 3.4 collective-permute-start.51
  491.6 5.2 collective-permute-start.59
  501.9 6.0 %soap_mid.1 = (f32[3,192,192]{2,1,0:T(8,128)S(1)}, f32[3,192,192]{2,1,0:T(8,128)S(1)}, f32[3,192,192]{2,1,0:T(8,128)S(1)}, f32[3,192,192]{2,1,0:T(8,128)S(1)}, f...) custom-call(s32[3]{0:T(128)S(1)} %get-tuple-element.258.flip_ref, f32[3,288,128]{2,1,0:T(8,128)S(1)} %bitcast.115, ...), custom_call_target="tpu_custom_call" | custom-call | flops 1000000000 | bytes 4000000 | tf_op jit(solution)/shard_map/soap_mid/pallas_call | solution.py:792
  526.7 23.5 %soap_late.1 = (f32[3,192,192]{2,1,0:T(8,128)}, f32[3,192,192]{2,1,0:T(8,128)}, f32[3,192,192]{2,1,0:T(8,128)}, bf16[3,192,192]{2,1,0:T(8,128)(2,1)}) custom-call(f32[1,1]{1,0:T(1,128)} %bitcast.48.f_ref, f32[3,192,192]{2,1,0:T(8,128)} %copy-done.12, f32[3,192,192]{2,1,0:T(8,128)} %copy-done.17, f32[3,192,192]{2,1,0:T(8,128)} %copy-done.19, ...), custom_call_target="tpu_custom_call" | custom-call | flops 1000000000 | bytes 10000000 | tf_op jit(solution)/shard_map/soap_late/pallas_call | solution.py:801
  (562 shorter events, 219.9 us)
Async XLA Ops:
  7.2 113.9 %all-gather.11.cloned.1.call-start = ((), (), s32[]{:S(2)}) async-start(), calls=%async_computation | async-start | bytes 28532736 | tf_op jit(solution)/shard_map/all_gather | solution.py:886
  11.3 143.9 %all-gather.13.cloned.1.call-start = ((), (), s32[]{:S(2)}) async-start(), calls=%async_computation.1 | async-start | bytes 1966080 | tf_op jit(solution)/shard_map/all_gather | solution.py:888
  17.3 20.1 %collective-permute-start.2 = (bf16[256,192]{0,1:T(8,128)(2,1)S(1)}, bf16[256,192]{0,1:T(8,128)(2,1)S(1)}, u32[]{:S(2)}, u32[]{:S(2)}) collective-permute-start(bf16[256,192]{0,1:T(8,128)(2,1)S(1)} %get-tuple-element.287), channel_id=1, source_target_pairs={{0,3},{1,2},{2,1},{3,0},{4,7},{5,6},{6,5},{7,4},{8,11},{9,10},{10,... | collective-permute-start | bytes 294920 | tf_op jit(solution)/shard_map/ppermute | solution.py:821
  19.9 17.5 %collective-permute-start.1 = (bf16[256,192]{0,1:T(8,128)(2,1)S(1)}, bf16[256,192]{0,1:T(8,128)(2,1)S(1)}, u32[]{:S(2)}, u32[]{:S(2)}) collective-permute-start(bf16[256,192]{0,1:T(8,128)(2,1)S(1)} %get-tuple-element.288), channel_id=1, source_target_pairs={{0,2},{1,3},{2,0},{3,1},{4,6},{5,7},{6,4},{7,5},{8,10},{9,11},{10,... | collective-permute-start | bytes 294920 | tf_op jit(solution)/shard_map/ppermute | solution.py:821
  21.2 210.7 %all-gather.15.cloned.1.call-start = ((), (), s32[]{:S(2)}) async-start(), calls=%async_computation.2 | async-start | bytes 1966080 | tf_op jit(solution)/shard_map/all_gather | solution.py:935
  39.4 24.8 %collective-permute-start.12 = (bf16[256,768]{1,0:T(8,128)(2,1)S(1)}, bf16[256,768]{1,0:T(8,128)(2,1)}, u32[]{:S(2)}, u32[]{:S(2)}) collective-permute-start(bf16[256,768]{1,0:T(8,128)(2,1)S(1)} %multiply_convert_fusion.refs_0_), channel_id=1, source_target_pairs={{0,3},{1,2},{2,1},{3,0},{4,7},{5,6},{6,5},{7,4},{8,11},{9,10},{10,... | collective-permute-start | bytes 1179656 | tf_op jit(solution)/shard_map/ppermute | solution.py:821
  41.5 22.7 %collective-permute-start.11 = (bf16[256,768]{1,0:T(8,128)(2,1)S(1)}, bf16[256,768]{1,0:T(8,128)(2,1)}, u32[]{:S(2)}, u32[]{:S(2)}) collective-permute-start(bf16[256,768]{1,0:T(8,128)(2,1)S(1)} %multiply_convert_fusion.refs_0_), channel_id=1, source_target_pairs={{0,2},{1,3},{2,0},{3,1},{4,6},{5,7},{6,4},{7,5},{8,10},{9,11},{10,... | collective-permute-start | bytes 1179656 | tf_op jit(solution)/shard_map/ppermute | solution.py:821
  42.2 22.8 %collective-permute-start.10 = (bf16[256,768]{1,0:T(8,128)(2,1)S(1)}, bf16[256,768]{1,0:T(8,128)(2,1)}, u32[]{:S(2)}, u32[]{:S(2)}) collective-permute-start(bf16[256,768]{1,0:T(8,128)(2,1)S(1)} %multiply_convert_fusion.refs_0_), channel_id=1, source_target_pairs={{0,1},{1,0},{2,3},{3,2},{4,5},{5,4},{6,7},{7,6},{8,9},{9,8},{10,11... | collective-permute-start | bytes 1179656 | tf_op jit(solution)/shard_map/ppermute | solution.py:821
  139.2 18.0 %collective-permute-start.13 = (bf16[192,256]{1,0:T(8,128)(2,1)}, bf16[192,256]{1,0:T(8,128)(2,1)S(1)}, u32[]{:S(2)}, u32[]{:S(2)}) collective-permute-start(bf16[192,256]{1,0:T(8,128)(2,1)} %get-tuple-element.147.refs_4_), channel_id=1, source_target_pairs={{0,1},{1,0},{2,3},{3,2},{4,5},{5,4},{6,7},{7,6},{8,9},{9,8},{10,11... | collective-permute-start | bytes 294920 | tf_op jit(solution)/shard_map/ppermute | solution.py:821
  140.4 16.8 %collective-permute-start.14 = (bf16[192,256]{1,0:T(8,128)(2,1)}, bf16[192,256]{1,0:T(8,128)(2,1)S(1)}, u32[]{:S(2)}, u32[]{:S(2)}) collective-permute-start(bf16[192,256]{1,0:T(8,128)(2,1)} %get-tuple-element.148.refs_5_), channel_id=1, source_target_pairs={{0,2},{1,3},{2,0},{3,1},{4,6},{5,7},{6,4},{7,5},{8,10},{9,11},{10,... | collective-permute-start | bytes 294920 | tf_op jit(solution)/shard_map/ppermute | solution.py:821
  169.2 19.4 %collective-permute-start.18 = (bf16[256,768]{1,0:T(8,128)(2,1)}, bf16[256,768]{1,0:T(8,128)(2,1)S(1)}, u32[]{:S(2)}, u32[]{:S(2)}) collective-permute-start(bf16[256,768]{1,0:T(8,128)(2,1)} %get-tuple-element.155.a0.refs_11_), channel_id=1, source_target_pairs={{0,3},{1,2},{2,1},{3,0},{4,7},{5,6},{6,5},{7,4},{8,11},{9,10},{10,... | collective-permute-start | bytes 1179656 | tf_op jit(solution)/shard_map/ppermute | solution.py:821
  171.7 17.0 %collective-permute-start.17 = (bf16[256,768]{1,0:T(8,128)(2,1)}, bf16[256,768]{1,0:T(8,128)(2,1)S(1)}, u32[]{:S(2)}, u32[]{:S(2)}) collective-permute-start(bf16[256,768]{1,0:T(8,128)(2,1)} %get-tuple-element.155.a0.refs_11_), channel_id=1, source_target_pairs={{0,2},{1,3},{2,0},{3,1},{4,6},{5,7},{6,4},{7,5},{8,10},{9,11},{10,... | collective-permute-start | bytes 1179656 | tf_op jit(solution)/shard_map/ppermute | solution.py:821
  171.7 17.4 %collective-permute-start.16 = (bf16[256,768]{1,0:T(8,128)(2,1)}, bf16[256,768]{1,0:T(8,128)(2,1)S(1)}, u32[]{:S(2)}, u32[]{:S(2)}) collective-permute-start(bf16[256,768]{1,0:T(8,128)(2,1)} %get-tuple-element.155.a0.refs_11_), channel_id=1, source_target_pairs={{0,1},{1,0},{2,3},{3,2},{4,5},{5,4},{6,7},{7,6},{8,9},{9,8},{10,11... | collective-permute-start | bytes 1179656 | tf_op jit(solution)/shard_map/ppermute | solution.py:821
  191.2 79.9 %all-gather.17.cloned.1.call-start = ((), (), s32[]{:S(2)}) async-start(), calls=%async_computation.3 | async-start | bytes 1966080 | tf_op jit(solution)/shard_map/all_gather | solution.py:945
  243.7 61.8 %all-gather.19.cloned.1.call-start = ((), (), s32[]{:S(2)}) async-start(), calls=%async_computation.4 | async-start | bytes 1966080 | tf_op jit(solution)/shard_map/all_gather | solution.py:980
  249.1 93.2 %all-gather.23.cloned.1.call-start = ((), (), s32[]{:S(2)}) async-start(), calls=%async_computation.6 | async-start | bytes 1966080 | tf_op jit(solution)/shard_map/all_gather | solution.py:985
  273.8 105.5 %all-gather.25.cloned.1.call-start = ((), (), s32[]{:S(2)}) async-start(), calls=%async_computation.7 | async-start | bytes 1966080 | tf_op jit(solution)/shard_map/all_gather | solution.py:980
  292.9 25.8 %collective-permute-start.28 = (bf16[576,256]{1,0:T(8,128)(2,1)}, bf16[576,256]{1,0:T(8,128)(2,1)S(1)}, u32[]{:S(2)}, u32[]{:S(2)}) collective-permute-start(bf16[576,256]{1,0:T(8,128)(2,1)} %get-tuple-element.178.refs_8_), channel_id=1, source_target_pairs={{0,1},{1,0},{2,3},{3,2},{4,5},{5,4},{6,7},{7,6},{8,9},{9,8},{10,11... | collective-permute-start | bytes 884744 | tf_op jit(solution)/shard_map/ppermute | solution.py:821
  294.0 24.7 %collective-permute-start.29 = (bf16[576,256]{1,0:T(8,128)(2,1)}, bf16[576,256]{1,0:T(8,128)(2,1)S(1)}, u32[]{:S(2)}, u32[]{:S(2)}) collective-permute-start(bf16[576,256]{1,0:T(8,128)(2,1)} %get-tuple-element.179.refs_9_), channel_id=1, source_target_pairs={{0,2},{1,3},{2,0},{3,1},{4,6},{5,7},{6,4},{7,5},{8,10},{9,11},{10,... | collective-permute-start | bytes 884744 | tf_op jit(solution)/shard_map/ppermute | solution.py:821
  295.6 23.1 %collective-permute-start.30 = (bf16[576,256]{1,0:T(8,128)(2,1)}, bf16[576,256]{1,0:T(8,128)(2,1)S(1)}, u32[]{:S(2)}, u32[]{:S(2)}) collective-permute-start(bf16[576,256]{1,0:T(8,128)(2,1)} %get-tuple-element.180.refs_10_), channel_id=1, source_target_pairs={{0,3},{1,2},{2,1},{3,0},{4,7},{5,6},{6,5},{7,4},{8,11},{9,10},{10,... | collective-permute-start | bytes 884744 | tf_op jit(solution)/shard_map/ppermute | solution.py:821
  337.5 71.1 %all-gather.21.cloned.1.call-start = ((), (), s32[]{:S(2)}) async-start(), calls=%async_computation.5 | async-start | bytes 1966080 | tf_op jit(solution)/shard_map/all_gather | solution.py:985
  337.9 15.3 %collective-permute-start.31 = (bf16[192,256]{1,0:T(8,128)(2,1)}, bf16[192,256]{1,0:T(8,128)(2,1)S(1)}, u32[]{:S(2)}, u32[]{:S(2)}) collective-permute-start(bf16[192,256]{1,0:T(8,128)(2,1)} %get-tuple-element.186), channel_id=1, source_target_pairs={{0,1},{1,0},{2,3},{3,2},{4,5},{5,4},{6,7},{7,6},{8,9},{9,8},{10,11... | collective-permute-start | bytes 294920 | tf_op jit(solution)/shard_map/ppermute | solution.py:821
  372.5 20.0 %collective-permute-start.34 = (bf16[576,256]{1,0:T(8,128)(2,1)}, bf16[576,256]{1,0:T(8,128)(2,1)S(1)}, u32[]{:S(2)}, u32[]{:S(2)}) collective-permute-start(bf16[576,256]{1,0:T(8,128)(2,1)} %get-tuple-element.198.refs_8_), channel_id=1, source_target_pairs={{0,1},{1,0},{2,3},{3,2},{4,5},{5,4},{6,7},{7,6},{8,9},{9,8},{10,11... | collective-permute-start | bytes 884744 | tf_op jit(solution)/shard_map/ppermute | solution.py:821
  372.6 19.9 %collective-permute-start.35 = (bf16[576,256]{1,0:T(8,128)(2,1)}, bf16[576,256]{1,0:T(8,128)(2,1)S(1)}, u32[]{:S(2)}, u32[]{:S(2)}) collective-permute-start(bf16[576,256]{1,0:T(8,128)(2,1)} %get-tuple-element.199.refs_9_), channel_id=1, source_target_pairs={{0,2},{1,3},{2,0},{3,1},{4,6},{5,7},{6,4},{7,5},{8,10},{9,11},{10,... | collective-permute-start | bytes 884744 | tf_op jit(solution)/shard_map/ppermute | solution.py:821
  375.9 16.6 %collective-permute-start.36 = (bf16[576,256]{1,0:T(8,128)(2,1)}, bf16[576,256]{1,0:T(8,128)(2,1)S(1)}, u32[]{:S(2)}, u32[]{:S(2)}) collective-permute-start(bf16[576,256]{1,0:T(8,128)(2,1)} %get-tuple-element.200.refs_10_), channel_id=1, source_target_pairs={{0,3},{1,2},{2,1},{3,0},{4,7},{5,6},{6,5},{7,4},{8,11},{9,10},{10,... | collective-permute-start | bytes 884744 | tf_op jit(solution)/shard_map/ppermute | solution.py:821
  379.0 181.0 %all-gather.27.cloned.1.call-start = ((), (), s32[]{:S(2)}) async-start(), calls=%async_computation.8 | async-start | bytes 1622016 | tf_op jit(solution)/shard_map/all_gather | solution.py:1052
  433.0 24.0 %collective-permute-start.45 = (bf16[4,480,128]{2,1,0:T(8,128)(2,1)S(1)}, bf16[4,480,128]{2,1,0:T(8,128)(2,1)S(1)}, u32[]{:S(2)}, u32[]{:S(2)}) collective-permute-start(bf16[4,480,128]{2,1,0:T(8,128)(2,1)S(1)} %get-tuple-element.219), channel_id=1, source_target_pairs={{0,64},{4,68},{8,72},{12,76},{16,80},{20,84},{24,88},{28,92},{32,9... | collective-permute-start | bytes 1474568 | tf_op jit(solution)/shard_map/ppermute | solution.py:821
  435.4 23.5 %collective-permute-start.46 = (bf16[4,480,128]{2,1,0:T(8,128)(2,1)S(1)}, bf16[4,480,128]{2,1,0:T(8,128)(2,1)S(1)}, u32[]{:S(2)}, u32[]{:S(2)}) collective-permute-start(bf16[4,480,128]{2,1,0:T(8,128)(2,1)S(1)} %get-tuple-element.220), channel_id=1, source_target_pairs={{0,96},{4,100},{8,104},{12,108},{16,112},{20,116},{24,120},{28,124... | collective-permute-start | bytes 1474568 | tf_op jit(solution)/shard_map/ppermute | solution.py:821
  435.7 23.3 %collective-permute-start.47 = (bf16[4,480,128]{2,1,0:T(8,128)(2,1)S(1)}, bf16[4,480,128]{2,1,0:T(8,128)(2,1)S(1)}, u32[]{:S(2)}, u32[]{:S(2)}) collective-permute-start(bf16[4,480,128]{2,1,0:T(8,128)(2,1)S(1)} %get-tuple-element.222), channel_id=1, source_target_pairs={{0,8},{4,12},{8,0},{12,4},{16,24},{20,28},{24,16},{28,20},{32,40},... | collective-permute-start | bytes 1474568 | tf_op jit(solution)/shard_map/ppermute | solution.py:821
  436.5 23.2 %collective-permute-start.48 = (bf16[4,480,128]{2,1,0:T(8,128)(2,1)S(1)}, bf16[4,480,128]{2,1,0:T(8,128)(2,1)S(1)}, u32[]{:S(2)}, u32[]{:S(2)}) collective-permute-start(bf16[4,480,128]{2,1,0:T(8,128)(2,1)S(1)} %get-tuple-element.223), channel_id=1, source_target_pairs={{0,16},{4,20},{8,24},{12,28},{16,0},{20,4},{24,8},{28,12},{32,48},... | collective-permute-start | bytes 1474568 | tf_op jit(solution)/shard_map/ppermute | solution.py:821
  444.2 23.2 %collective-permute-start.49 = (bf16[4,480,128]{2,1,0:T(8,128)(2,1)S(1)}, bf16[4,480,128]{2,1,0:T(8,128)(2,1)S(1)}, u32[]{:S(2)}, u32[]{:S(2)}) collective-permute-start(bf16[4,480,128]{2,1,0:T(8,128)(2,1)S(1)} %get-tuple-element.224), channel_id=1, source_target_pairs={{0,24},{4,28},{8,16},{12,20},{16,8},{20,12},{24,0},{28,4},{32,56},... | collective-permute-start | bytes 1474568 | tf_op jit(solution)/shard_map/ppermute | solution.py:821
  497.6 15.7 %collective-permute-start.62 = (f32[8,128]{1,0:T(8,128)S(1)}, f32[8,128]{1,0:T(8,128)S(1)}, u32[]{:S(2)}, u32[]{:S(2)}) collective-permute-start(f32[8,128]{1,0:T(8,128)S(1)} %add.384), channel_id=1, source_target_pairs={{0,24},{4,28},{8,16},{12,20},{16,8},{20,12},{24,0},{28,4},{32,56},... | collective-permute-start | bytes 12296 | tf_op jit(solution)/shard_map/ppermute | solution.py:821
  (136 other events, 823.1 us)
Sparse Core Ops, SparseCore 0:
  11.6 109.4 all-gather.10
  123.3 28.4 all-gather.12
  191.3 31.2 all-gather.14
  243.8 27.2 all-gather.16
  273.2 32.2 all-gather.18
  307.0 28.0 all-gather.22
  337.6 27.9 all-gather.24
  379.1 29.3 all-gather.20
  517.7 42.3 all-gather.26

commit v4 on v3

--- a/solution.py
+++ b/solution.py
@@ -37,6 +37,10 @@
 VM = pl.BlockSpec(memory_space=pltpu.VMEM)
 SM = pl.BlockSpec(memory_space=pltpu.SMEM)
 ANY = pl.BlockSpec(memory_space=pl.ANY)
+
+
+def in_hbm(*arrays):
+    return [pltpu.with_memory_space_constraint(array, pltpu.HBM) for array in arrays]
 
 
 def params(mib):
@@ -287,7 +291,7 @@
         compiler_params=params(60),
         cost_estimate=cost(10**10, 6 * 10**6, 3 * 2**20),
         name="attend_fwd",
-    )(w, *acts, gains, qid, kid)
+    )(*in_hbm(w), *acts, gains, qid, kid)
 
 
 def attend_bwd(
@@ -371,89 +375,100 @@
     )(pre, v, lse, *grads, gains, qid, kid)
 
 
-def mix_fwd(x_ref, o0, o1, o2, o3, w_out, gain_ref, next_ref, up_ref, down_ref,
-            mid_ref, u_ref, c_ref, x_out, a_out):
-    r = pl.program_id(0)
-
-    @pl.when(r == 0)
-    def _():
-        mid = x_ref[...]
-        for k, ref in enumerate((o0, o1, o2, o3)):
-            mid = mid + mm(ref[...], w_out[TILE * k : TILE * k + TILE, :], 0, 0)
-        mid_ref[...] = mid
-        low = (normalize(mid)[0] * gain_ref[...]).astype(bf16)
-        c_ref[...] = low
-        x_out[...] = mid
-
-    u = mm(c_ref[...], up_ref[0], 1, 1)
-    u_ref[0] = u
-    x_out[...] += mm(gelu(u).astype(bf16), down_ref[0])
-
-    @pl.when(r == 3)
-    def _():
-        a_out[...] = (normalize(x_out[...])[0] * next_ref[...]).astype(bf16)
-
-
-def whole(*dims):
-    return pl.BlockSpec(dims, lambda r: (0,) * len(dims))
-
-
-def part(*dims):
-    return pl.BlockSpec((1, *dims), lambda r: (r,) + (0,) * len(dims))
+def fetches(sources, targets, sems):
+    copies = [
+        pltpu.make_async_copy(source, target, sems.at[at])
+        for at, (source, target) in enumerate(zip(sources, targets))
+    ]
+    for copy in copies:
+        copy.start()
+    return copies
+
+
+def mix_fwd(x_ref, o0, o1, o2, o3, gain_ref, next_ref, out_hbm, up_hbm, down_hbm,
+            mid_ref, c_ref, x_out, a_out, out_s, up_s, down_s, sems):
+    sources, targets = ([out_hbm], [out_s])
+    for r in range(4):
+        sources += [up_hbm.at[r], down_hbm.at[r]]
+        targets += [up_s.at[r], down_s.at[r]]
+    copies = fetches(sources, targets, sems)
+    copies[0].wait()
+    total = x_ref[...]
+    for k, ref in enumerate((o0, o1, o2, o3)):
+        total = total + mm(ref[...], out_s[TILE * k : TILE * k + TILE, :], 0, 0)
+    mid_ref[...] = total
+    low = (normalize(total)[0] * gain_ref[...]).astype(bf16)
+    c_ref[...] = low
+    x_out[...] = total
+    for r in range(4):
+        copies[1 + 2 * r].wait()
+        u = mm(low, up_s[r], 1, 1)
+        copies[2 + 2 * r].wait()
+        x_out[...] += mm(gelu(u).astype(bf16), down_s[r])
+    a_out[...] = (normalize(x_out[...])[0] * next_ref[...]).astype(bf16)
+
+
+def weight_scratch():
+    return [
+        pltpu.VMEM((D, D), bf16),
+        pltpu.VMEM((4, D, D), bf16),
+        pltpu.VMEM((4, D, D), bf16),
+        pltpu.SemaphoreType.DMA((9,)),
+    ]
 
 
 def run_mix_fwd(x, outs, w_out, gain, gain_next, up, down):
     return pl.pallas_call(
         mix_fwd,
-        grid=(4,),
-        in_specs=[whole(OWN, D)] + [whole(TILE, OWN)] * 4 + [whole(D, D), whole(1, D), whole(1, D), part(D, D), part(D, D)],
-        out_specs=[whole(OWN, D), part(OWN, D), whole(OWN, D), whole(OWN, D), whole(OWN, D)],
-        out_shape=[shape((OWN, D)), shape((4, OWN, D)), shape((OWN, D), bf16), shape((OWN, D)), shape((OWN, D), bf16)],
+        in_specs=[VM] * 7 + [ANY] * 3,
+        out_specs=[VM] * 4,
+        out_shape=[shape((OWN, D)), shape((OWN, D), bf16), shape((OWN, D)), shape((OWN, D), bf16)],
+        scratch_shapes=weight_scratch(),
         compiler_params=params(60),
         cost_estimate=cost(6 * 10**9, 17 * 10**6, 10**6),
         name="mix_fwd",
-    )(x, *outs, w_out, gain, gain_next, up, down)
-
-
-def mix_bwd(g_ref, low_ref, mid_ref, u_ref, gain_ref, w_out, up_ref, down_ref,
-            mid_grad, mid_low, dgain_ref, do0, do1, do2, do3, acc):
-    r = pl.program_id(0)
-
-    @pl.when(r == 0)
-    def _():
-        acc[...] = jnp.zeros_like(acc)
-
-    df = mm(low_ref[...], down_ref[0], 1, 1)
-    u = u_ref[0]
-    cdf, bell = gauss_parts(u)
-    du = (df * (cdf + u * bell * 0.3989422804014327)).astype(bf16)
-    acc[...] += mm(du, up_ref[0])
-
-    @pl.when(r == 3)
-    def _():
-        normed, inverse = normalize(mid_ref[...])
-        grad = acc[...]
-        dgain_ref[...] = jnp.sum(grad * normed, 0, keepdims=True)
-        total = g_ref[...] + norm_back(grad, gain_ref[...], normed, inverse)
-        mid_grad[...] = total
-        low = total.astype(bf16)
-        mid_low[...] = low
-        for k, ref in enumerate((do0, do1, do2, do3)):
-            ref[...] = mm(w_out[TILE * k : TILE * k + TILE, :], low, 1, 1).astype(bf16)
-
-
-def run_mix_bwd(grad, grad_low, mid, u, gain, w_out, up, down):
+    )(x, *outs, gain, gain_next, *in_hbm(w_out, up, down))
+
+
+def mix_bwd(g_ref, low_ref, mid_ref, c_ref, gain_ref, out_hbm, up_hbm, down_hbm,
+            mid_grad, mid_low, dgain_ref, do0, do1, do2, do3, out_s, up_s, down_s, sems, acc):
+    sources, targets = ([], [])
+    for r in range(4):
+        sources += [down_hbm.at[r], up_hbm.at[r]]
+        targets += [down_s.at[r], up_s.at[r]]
+    copies = fetches(sources + [out_hbm], targets + [out_s], sems)
+    acc[...] = jnp.zeros_like(acc)
+    for r in range(4):
+        copies[2 * r].wait()
+        df = mm(low_ref[...], down_s[r], 1, 1)
+        copies[2 * r + 1].wait()
+        u = mm(c_ref[...], up_s[r], 1, 1)
+        cdf, bell = gauss_parts(u)
+        du = (df * (cdf + u * bell * 0.3989422804014327)).astype(bf16)
+        acc[...] += mm(du, up_s[r])
+    normed, inverse = normalize(mid_ref[...])
+    grad = acc[...]
+    dgain_ref[...] = jnp.sum(grad * normed, 0, keepdims=True)
+    total = g_ref[...] + norm_back(grad, gain_ref[...], normed, inverse)
+    mid_grad[...] = total
+    low = total.astype(bf16)
+    mid_low[...] = low
+    copies[8].wait()
+    for k, ref in enumerate((do0, do1, do2, do3)):
+        ref[...] = mm(out_s[TILE * k : TILE * k + TILE, :], low, 1, 1).astype(bf16)
+
+
+def run_mix_bwd(grad, grad_low, mid, normed, gain, w_out, up, down):
     return pl.pallas_call(
         mix_bwd,
-        grid=(4,),
-        in_specs=[whole(OWN, D), whole(OWN, D), whole(OWN, D), part(OWN, D), whole(1, D), whole(D, D), part(D, D), part(D, D)],
-        out_specs=[whole(OWN, D), whole(OWN, D), whole(1, D)] + [whole(TILE, OWN)] * 4,
+        in_specs=[VM] * 5 + [ANY] * 3,
+        out_specs=[VM] * 7,
         out_shape=[shape((OWN, D)), shape((OWN, D), bf16), shape((1, D))] + [shape((TILE, OWN), bf16)] * 4,
-        scratch_shapes=[pltpu.VMEM((OWN, D), f32)],
+        scratch_shapes=weight_scratch() + [pltpu.VMEM((OWN, D), f32)],
         compiler_params=params(60),
         cost_estimate=cost(6 * 10**9, 17 * 10**6, 10**6),
         name="mix_bwd",
-    )(grad, grad_low, mid, u, gain, w_out, up, down)
+    )(grad, grad_low, mid, normed, gain, *in_hbm(w_out, up, down))
 
 
 def input_bwd(mid_grad, d0, d1, d2, d3, w_ref, x_ref, gain_ref, grad_ref, low_ref, dgain_ref):
@@ -568,19 +583,32 @@
     return buffers, token
 
 
-def run_mlp_grads(depth, places, act, low, up, down, buffers):
+def run_mlp_grads(depth, places, pair, up, down, buffers):
     first = pl.BlockSpec((1, D, D), lambda i: (0, 0, 0))
+    sides = [pl.BlockSpec((TOKENS, D), lambda i, side=side: (0, side)) for side in range(2)]
+    if isinstance(pair, tuple):
+        sides = [VM] * 2
+    else:
+        pair = (pair, pair)
     return grads_call(
         lambda *refs: mlp_grads(depth, *refs), "mlp_grads", [places],
-        [act, low, up, down], [VM] * 2 + [first] * 2, buffers, 32, 5 * 10**9,
+        in_hbm(*pair, up, down), sides + [first] * 2, buffers, 32, 5 * 10**9,
     )
 
 
 def run_head_grads(depth, places, index, mid_low, outs, grads, acts, buffers):
     return grads_call(
         lambda *refs: head_grads(depth, *refs), "head_grads", [places, index],
-        [mid_low, *outs, *grads, *acts], [VM] * 13, buffers, 16, 2 * 10**9,
-    )
+        [*in_hbm(mid_low), *outs, *grads, *acts], [VM] * 13, buffers, 16, 2 * 10**9,
+    )
+
+
+def whole(*dims):
+    return pl.BlockSpec(dims, lambda r: (0,) * len(dims))
+
+
+def part(*dims):
+    return pl.BlockSpec((1, *dims), lambda r: (r,) + (0,) * len(dims))
 
 
 def add_core(keep, got, own_a, a1, a2, a3, own_b, b1, b2, b3):
@@ -638,7 +666,7 @@
         lambda *refs: None, in_specs=[ANY] * (1 + len(others)), out_specs=ANY,
         out_shape=shape(array.shape, array.dtype), input_output_aliases={0: 0},
         compiler_params=params(16), name="gate",
-    )(array, *others)
+    )(array, *[in_hbm(other)[0] if other.size > 2**17 else other for other in others])
 
 
 def soap_early(first, stat_l, stat_r, left, right, turned_ref, l_ref, r_ref):
@@ -714,7 +742,7 @@
 
 def soap_late(
     f_ref, second, left, right, weight, turned, turned_first, xl, xr, yl, yr,
-    weight_ref, left_ref, right_ref, low_ref, panels, work,
+    weight_ref, left_ref, right_ref, panels, work,
 ):
     factor = f_ref[0, 0]
     bias_one = 1.0 - first_decay**STEP
@@ -743,7 +771,6 @@
         back = mm_split(work[n], right[n], 1, 1)
         weight_new = weight[n] * (1.0 - matrix_rate * weight_decay) - matrix_rate * back
         weight_ref[n] = weight_new
-        low_ref[n] = weight_new.astype(bf16)
 
     def remove(i, basis, k):
         panel = panels[i, k]
@@ -799,8 +826,8 @@
 
 def run_soap_late(*args):
     return pl.pallas_call(
-        soap_late, in_specs=[SM] + [VM] * 10, out_specs=[VM] * 4,
-        out_shape=tiles_of_three(3) + [shape((3, TILE, TILE), bf16)],
+        soap_late, in_specs=[SM] + [VM] * 10, out_specs=[VM] * 3,
+        out_shape=tiles_of_three(3),
         scratch_shapes=[pltpu.VMEM((6, 3, TILE, 64), f32), pltpu.VMEM((3, TILE, TILE), f32)],
         compiler_params=params(56), cost_estimate=cost(10**9, 10**7), name="soap_late",
     )(*args)
@@ -888,6 +915,7 @@
     head_low = lax.all_gather(head_weight.astype(bf16), "mp", axis=0, tiled=True)
 
     split_one = (2 * LAYERS + 1) * D
+    split_two = split_one + 2 * LAYERS * HD
     gain_rows = vectors[:split_one].reshape(2 * LAYERS + 1, 4, TILE)
     gain_rows = widen([gain_rows[:, t] for t in range(4)], 1)[:, None, :]
     head_gains = vectors[split_one : split_one + 2 * LAYERS * HD].reshape(LAYERS, 2, HD)
@@ -932,21 +960,19 @@
             acts[0] = gate(acts[0], turned_first, second_tiles, image_sum)
         else:
             normed = gate(normed, *acts[1:], qkv)
+            gains = gate(gains, head_low)
             saved[-1].append(lax.all_gather(normed, "mp", axis=0, tiled=True))
         pre, v, lse, *o = run_attend_fwd(qkv, acts, gains, query_ids, key_ids)
         outs = trade_mp(o)
-        if depth == 0:
-            outs[0] = gate(outs[0], head_low)
-        mid, u, normed, resid_next, act = run_mix_fwd(
+        mid, normed, resid_next, act = run_mix_fwd(
             resid, outs, out, gain_rows[2 * depth + 1], gain_rows[2 * depth + 2], up, down
         )
-        saved.append([resid, acts, pre, v, lse, o, mid, u])
+        saved.append([resid, acts, pre, v, lse, o, mid, normed])
         resid = resid_next
-    saved[-1].append(lax.all_gather(normed, "mp", axis=0, tiled=True))
-
-    resid = gate(resid, saved[0][-1])
+    saved[-1].append(None)
+
     final, final_inverse = normalize(resid)
-    gain_last = gain_rows[2 * LAYERS]
+    gain_last = gate(gain_rows[2 * LAYERS], saved[0][-1])
     pooled = total_mp(jnp.dot(member.T, final * gain_last, precision=highest)) / divisor[:, None]
     pooled = jnp.concatenate([pooled[:, :512].reshape(IMGS, 4, 128), pooled[:, 512:].reshape(IMGS, 4, 64)], axis=2)
     pooled_low = pooled.reshape(IMGS, D).astype(bf16)
@@ -974,26 +1000,27 @@
     head_gain_grads = []
     for depth in reversed(range(LAYERS)):
         qkv, out, up, down = weights[depth]
-        resid, acts, pre, v, lse, o, mid, u, normed = saved[depth]
+        resid, acts, pre, v, lse, o, mid, own_normed, normed = saved[depth]
         gains = head_gains[depth].T
         out = out.reshape(D, D)
-        lows = lax.all_gather(grad_low, "mp", axis=0, tiled=True)
+        if normed is None:
+            pair = lax.all_gather(jnp.concatenate([own_normed, grad_low], axis=1), "mp", axis=0, tiled=True)
+        else:
+            pair = (normed, lax.all_gather(grad_low, "mp", axis=0, tiled=True))
         mid_grad, mid_low, gain_two, *do = run_mix_bwd(
-            grad, grad_low, mid, u, gain_rows[2 * depth + 1], out, up, down
+            grad, grad_low, mid, own_normed, gain_rows[2 * depth + 1], out, up, down
         )
         dos = trade_mp(do)
         mid_lows = lax.all_gather(gate(mid_low, *dos[1:]), "mp", axis=0, tiled=True)
-        if waiting is None:
-            pre = gate(pre, normed)
-        else:
+        if waiting is not None:
             deeper, given, *rest = waiting
-            buffers, token = run_head_grads(deeper, places, index, gate(given, do[0]), *rest, buffers)
-            pre = gate(pre, token)
+            buffers, token = run_head_grads(deeper, places, gate(index, dos[1]), given, *rest, buffers)
+            gains = gate(gains, token)
         *dp, gain_heads = run_attend_bwd(pre, v, lse, dos, gains, query_ids, key_ids)
         dps = trade_mp(dp)
-        buffers, token = run_mlp_grads(depth, places, normed, lows, up, down, buffers)
-        mid_grad = gate(mid_grad, token)
-        grad, grad_low, gain_one = run_input_bwd(mid_grad, dps, qkv, resid, gain_rows[2 * depth])
+        buffers, token = run_mlp_grads(depth, places, pair, up, down, buffers)
+        gain = gate(gain_rows[2 * depth], token)
+        grad, grad_low, gain_one = run_input_bwd(mid_grad, dps, qkv, resid, gain)
         waiting = (depth, mid_lows, o, dp, acts)
         gain_grads = [wide_back(gain_one[0]), wide_back(gain_two[0])] + gain_grads
         head_gain_grads.insert(0, gain_heads.T)
@@ -1001,14 +1028,18 @@
     deeper, *rest = waiting
     buffers, token = run_head_grads(deeper, places, index, *rest, buffers)
 
-    columns = trade_mp([wide_part(grad_low, mp_index ^ r, 1) for r in range(4)])
-    columns[0] = gate(columns[0], token)
-    columns = jnp.concatenate(columns, axis=0)
+    vector_part = jnp.concatenate([jnp.concatenate(gain_grads), jnp.stack(head_gain_grads).reshape(-1)])
+    vector_part = jnp.pad(vector_part, (0, 32 * TILE - vector_part.shape[0])).reshape(32, TILE).astype(bf16)
+    traded = trade_mp(
+        [jnp.concatenate([wide_part(grad_low, mp_index ^ r, 1), vector_part], axis=0) for r in range(4)]
+    )
+    traded[0] = gate(traded[0], token)
+    columns = jnp.concatenate([piece[:OWN] for piece in traded], axis=0)
     grad_embed = jnp.dot(columns.T, tokens.reshape(TOKENS, D), preferred_element_type=f32)
     embed_rows = grad_embed.reshape(32, EMBED_ROWS, 128)
+    vector_total = sum_four([piece[OWN:].astype(f32) for piece in traded]).reshape(-1)
     head_rows = jnp.pad(grad_head, ((0, 0), (0, 24))).reshape(32, HEAD_ROWS, 128)
-    vector_part = jnp.concatenate([jnp.concatenate(gain_grads), jnp.stack(head_gain_grads).reshape(-1)])
-    vector_sum = jnp.concatenate([total_mp(vector_part), grad_bias, jnp.zeros((24,), f32)])
+    vector_sum = jnp.concatenate([vector_total[:split_two], grad_bias, jnp.zeros((24,), f32)])
     vector_rows = jnp.pad(vector_sum.reshape(32, 160), ((0, 0), (0, 1536 - 160))).reshape(32, 12, 128)
     small = jnp.concatenate([embed_rows, head_rows, vector_rows], axis=1).astype(bf16)
     small = by_partner(small, dp_index).reshape(16, 2, SMALL, 128)
@@ -1054,20 +1085,21 @@
     factor = clip_limit / jnp.maximum(grad_norm, clip_limit)
 
     grad_flat, turned_flat, gram_left, gram_right = flats
-    weight_new, left_basis, right_basis, weight_low = run_soap_late(
+    weight_new, left_basis, right_basis = run_soap_late(
         factor.reshape(1, 1), second_tiles, left, right, master, turned, turned_first,
         left_old, right_old, left_new, right_new,
     )
     turned_flat = turned_flat * factor
+    weight_flat = flat(weight_new)
     soap_new = (
-        flat(weight_new),
+        weight_flat,
         first_decay * soap_first + (1.0 - first_decay) * (grad_flat * factor),
         second_decay * soap_second + (1.0 - second_decay) * turned_flat * turned_flat,
         second_decay * stat_left + (1.0 - second_decay) * (factor * (factor * gram_left)),
         second_decay * stat_right + (1.0 - second_decay) * (factor * (factor * gram_right)),
         flat(left_basis),
         flat(right_basis),
-        flat(weight_low),
+        weight_flat.astype(bf16),
     )
 
     grad_embed = shares[:, :EMBED_ROWS].reshape(TILE, D)

time: 586 us -> 575 us (0.981)
  local copies, waits for them, and re-layouts: 75.5 us -> 54 us
    unnamed x193 -> x202, local copies, waits for them, and re-layouts: 38.4 us -> 21 us
    all_gather x2, waiting for transfers between devices: 8.6 us -> 0.01 us  [the longest x1 0.01 us: shards(): lax.all_gather(jnp.concatenate([own_normed, grad_low], axis=1), 'mp', axi...]
    ppermute x66 -> x63, waiting for transfers between devices: 63.5 us -> 72 us  [swap(): return lax.ppermute(array, axis, [(i, i ^ r) for i in range(size)])]
    all_gather x1, waiting for transfers between devices: 2.89 us -> 9.61 us  [shards(): shares = lax.all_gather(share, 'dp', axis=0)]
    ppermute x66 -> x63, starting transfers between devices: 92.6 us -> 92.1 us  [swap(): return lax.ppermute(array, axis, [(i, i ^ r) for i in range(size)])]
  transfers between devices with their start and end apart: 75 -> 71, of which waited for: 27 -> 26; matrix products, arithmetic and copies ran while one was open for 9% -> 9% of each run, Pallas kernels for 35% -> 38%
where the time goes in v4:
time: 575 us; the launch traced here: 567 us
  Pallas kernels  217 us (38%)
  waiting for transfers between devices  139 us (24%)
  starting transfers between devices  93.6 us (16%)
  local copies, waits for them, and re-layouts  54 us (9%)
  other arithmetic  34.6 us (6%)
  between operations  20.8 us (4%)
  matrix products  7.95 us (1%)
    ppermute x63, starting transfers between devices, swap(): return lax.ppermute(array, axis, [(i, i ^ r) for i in range(size)])  92.1 us
    ppermute x63, waiting for transfers between devices, swap(): return lax.ppermute(array, axis, [(i, i ^ r) for i in range(size)])  72 us
    all_gather x1, waiting for transfers between devices, shards(): slots = lax.all_gather(pack_tile(low), ('dp', 'mp'), axis=0, tiled=True)  54.2 us
    pallas_call x4, Pallas kernels, grads_call(): pl.pallas_call(kernel, grid=(1,), in_specs=[SM] * len(scalars) + specs +...  36.6 us
    pallas_call x2, Pallas kernels, run_attend_bwd(): pl.pallas_call(attend_bwd, in_specs=[VM] * 10, out_specs=[VM] * 5, out_sh...  35.3 us
    pallas_call x2, Pallas kernels, run_attend_fwd(): pl.pallas_call(attend_fwd, grid=(1,), in_specs=[pl.BlockSpec((1, 3 * TILE...  27.6 us
    pallas_call x3, Pallas kernels, assemble(): pl.pallas_call(kernel, in_specs=[SM, ANY], out_specs=[ANY] * len(groups),...  27.5 us
    pallas_call x2, Pallas kernels, run_mix_bwd(): pl.pallas_call(mix_bwd, in_specs=[VM] * 5 + [ANY] * 3, out_specs=[VM] * 7...  25 us
  transfers between devices with their start and end apart: 71, of which 26 were waited for; matrix products, arithmetic and copies ran while one was open for 9% of the time, Pallas kernels for 38%

profile of v4, /device:TPU:1, one launch (start us, length us, event | category | flops | bytes accessed | tf_op | source)
XLA Modules:
  0.0 567.0 jit_solution(2731862897162141507)
XLA Ops:
  27.0 3.7 collective-permute-start.5
  58.7 5.3 collective-permute-done.12.a3.refs_14_
  67.4 54.2 %all-gather.10.cloned.1.call-done.slots_ref = bf16[384,288,128]{2,1,0:T(8,128)(2,1)} async-done(((bf16[3,288,128]{2,1,0:T(8,128)(2,1)}), bf16[384,288,128]{2,1,0:T(8,128)(2,1)}) %all-gather.10.cloned.1.call-update) | async-done | bytes 28311568 | tf_op jit(solution)/shard_map/all_gather | solution.py:913
  121.6 4.3 assemble.3
  125.9 13.8 %attend_fwd.2 = (f32[384,1024]{1,0:T(8,128)}, bf16[192,1024]{1,0:T(8,128)(2,1)}, f32[3,1,1024]{2,1,0:T(1,128)}, bf16[192,256]{1,0:T(8,128)(2,1)}, bf16[192,256]{...) custom-call(bf16[4,576,768]{2,1,0:T(8,128)(2,1)} %bitcast.120, bf16[256,768]{1,0:T(8,128)(2,1)} %copy-done.4, ...), custom_call_target="tpu_custom_call" | custom-call | flops 10000000000 | bytes 6000000 | tf_op jit(solution)/shard_map/attend_fwd/pallas_call | solution.py:275
  144.7 10.2 %assemble.4 = (bf16[4,192,768]{2,1,0:T(8,128)(2,1)}, bf16[16,192,768]{2,1,0:T(8,128)(2,1)}, bf16[16,192,768]{2,1,0:T(8,128)(2,1)}) custom-call(s32[384]{0:T(512)} %add.335.table_ref, bf16[384,288,128]{2,1,0:T(8,128)(2,1)} %all-gather.10.cloned.1.call-done.slots_ref), custom_call_target="tpu_custom_call" | custom-call | bytes 21233664 | tf_op jit(solution)/shard_map/assemble/pallas_call | solution.py:197
  155.6 10.6 %mix_fwd.2 = (f32[256,768]{1,0:T(8,128)}, bf16[256,768]{1,0:T(8,128)(2,1)}, f32[256,768]{1,0:T(8,128)}, bf16[256,768]{1,0:T(8,128)(2,1)}) custom-call(f32[256,768]{1,0:T(8,128)} %convert_element_type.91.x_ref, bf16[192,256]{1,0:T(8,128)(2,1)} %get-tuple-element.143.o0.refs_3_, bf16[192,256]{1,0:T(8,128)(2,1)} %copy-done.89, bf16[192,256]{1,0:T(8,128)(2,1)} %copy-done.90, ...), custom_call_target="tpu_custom_call" | custom-call | flops 6000000000 | bytes 17000000 | tf_op jit(solution)/shard_map/mix_fwd/pallas_call | solution.py:421
  169.5 13.0 %assemble.5 = (bf16[12,192,768]{2,1,0:T(8,128)(2,1)}, bf16[4,192,768]{2,1,0:T(8,128)(2,1)}, bf16[16,192,768]{2,1,0:T(8,128)(2,1)}, bf16[16,192,768]{2,1,0:T(8,128)(2,1)}) custom-call(s32[384]{0:T(512)} %add.335.table_ref, bf16[384,288,128]{2,1,0:T(8,128)(2,1)} %all-gather.10.cloned.1.call-done.slots_ref), custom_call_target="tpu_custom_call" | custom-call | bytes 28311552 | tf_op jit(solution)/shard_map/assemble/pallas_call | solution.py:197
  188.3 13.8 %attend_fwd.3 = (f32[384,1024]{1,0:T(8,128)}, bf16[192,1024]{1,0:T(8,128)(2,1)}, f32[3,1,1024]{2,1,0:T(1,128)}, bf16[192,256]{1,0:T(8,128)(2,1)}, bf16[192,256]{...) custom-call(bf16[4,576,768]{2,1,0:T(8,128)(2,1)} %bitcast.118, ...), custom_call_target="tpu_custom_call" | custom-call | flops 10000000000 | bytes 6000000 | tf_op jit(solution)/shard_map/attend_fwd/pallas_call | solution.py:275
  208.3 7.3 %collective-permute-done.20.o2 = bf16[192,256]{1,0:T(8,128)(2,1)S(1)} collective-permute-done((bf16[192,256]{1,0:T(8,128)(2,1)}, bf16[192,256]{1,0:T(8,128)(2,1)S(1)}, u32[]{:S(2)}, u32[]{:S(2)}) %collective-permute-start.20) | collective-permute-done | bytes 98336 | tf_op jit(solution)/shard_map/ppermute | solution.py:848
  216.3 10.6 %mix_fwd.3 = (f32[256,768]{1,0:T(8,128)}, bf16[256,768]{1,0:T(8,128)(2,1)}, f32[256,768]{1,0:T(8,128)}, bf16[256,768]{1,0:T(8,128)(2,1)}) custom-call(f32[256,768]{1,0:T(8,128)} %get-tuple-element.150.x_ref, bf16[192,256]{1,0:T(8,128)(2,1)} %get-tuple-element.153.o0.refs_3_, bf16[192,256]{1,0:T(8,128)(2,1)} %copy-done.91, bf16[192,256]{1,0:T(8,128)(2,1)} %copy-done.93, ...), custom_call_target="tpu_custom_call" | custom-call | flops 6000000000 | bytes 17000000 | tf_op jit(solution)/shard_map/mix_fwd/pallas_call | solution.py:421
  244.7 12.5 %mix_bwd.2 = (f32[256,768]{1,0:T(8,128)}, bf16[256,768]{1,0:T(8,128)(2,1)}, f32[1,768]{1,0:T(1,128)}, bf16[192,256]{1,0:T(8,128)(2,1)}, bf16[192,256]{1,0:T(8,12...) custom-call(f32[256,768]{1,0:T(8,128)} %get-tuple-element.255.g_ref, bf16[256,768]{1,0:T(8,128)(2,1)} %copy-done.62, ...), custom_call_target="tpu_custom_call" | custom-call | flops 6000000000 | bytes 17000000 | tf_op jit(solution)/shard_map/mix_bwd/pallas_call | solution.py:462
  263.3 4.8 collective-permute-done.26.g2.refs_2_
  269.6 17.6 %attend_bwd.2 = (bf16[576,256]{1,0:T(8,128)(2,1)}, bf16[576,256]{1,0:T(8,128)(2,1)}, bf16[576,256]{1,0:T(8,128)(2,1)}, bf16[576,256]{1,0:T(8,128)(2,1)}, f32[64,2]{1,0:T(8,128)}) custom-call(f32[384,1024]{1,0:T(8,128)} %get-tuple-element.165.pre_ref, bf16[192,1024]{1,0:T(8,128)(2,1)} %get-tuple-element.166.v_ref, f32[3,1,1024]{2,1,0:T(1,128)} %get-tuple-element.167.lse_ref, ...), custom_call_target="tpu_custom_call" | custom-call | flops 20000000000 | bytes 6000000 | tf_op jit(solution)/shard_map/attend_bwd/pallas_call | solution.py:356
  291.3 12.5 %mlp_grads.2 = (bf16[16,960,128]{2,1,0:T(8,128)(2,1)}, bf16[16,960,128]{2,1,0:T(8,128)(2,1)}, f32[8,128]{1,0:T(8,128)}) custom-call(s32[96]{0:T(128)} %get-tuple-element.256.refs_0_, bf16[1024,1536]{1,0:T(8,128)(2,1)} %all-gather.16.cloned.1.call-done.refs_1_.refs_2_, bf16[1024,1536]{1,0:T(8,128)(2,1)} %all-gather.16.cloned.1.call-done.refs_1_.refs_2_, ...), custom_call_target="tpu_custom_call" | custom-call | flops 5000000000 | bytes 10000000 | tf_op jit(solution)/shard_map/mlp_grads/pallas_call | solution.py:571
  304.5 4.4 input_bwd.2
  311.9 12.5 %mix_bwd.3 = (f32[256,768]{1,0:T(8,128)}, bf16[256,768]{1,0:T(8,128)(2,1)}, f32[1,768]{1,0:T(1,128)}, bf16[192,256]{1,0:T(8,128)(2,1)}, bf16[192,256]{1,0:T(8,12...) custom-call(f32[256,768]{1,0:T(8,128)} %copy-done.40, bf16[256,768]{1,0:T(8,128)(2,1)} %get-tuple-element.178.low_ref, ...), custom_call_target="tpu_custom_call" | custom-call | flops 6000000000 | bytes 17000000 | tf_op jit(solution)/shard_map/mix_bwd/pallas_call | solution.py:462
  330.1 6.1 %head_grads.2 = (bf16[16,960,128]{2,1,0:T(8,128)(2,1)}, bf16[16,960,128]{2,1,0:T(8,128)(2,1)}, f32[8,128]{1,0:T(8,128)}) custom-call(s32[96]{0:T(128)} %get-tuple-element.256.refs_0_, s32[1]{0:T(128)} %gate.18.refs_1_, bf16[1024,768]{1,0:T(8,128)(2,1)} %all-gather.20.cloned.1.call-done.refs_2_, ...), custom_call_target="tpu_custom_call", output_to_operand_aliasing={{0}: (15, {}), {1}: (16, {})} | custom-call | flops 2000000000 | bytes 10000000 | tf_op jit(solution)/shard_map/head_grads/pallas_call | solution.py:571
  337.5 17.6 %attend_bwd.3 = (bf16[576,256]{1,0:T(8,128)(2,1)}, bf16[576,256]{1,0:T(8,128)(2,1)}, bf16[576,256]{1,0:T(8,128)(2,1)}, bf16[576,256]{1,0:T(8,128)(2,1)}, f32[64,2]{1,0:T(8,128)}) custom-call(f32[384,1024]{1,0:T(8,128)} %get-tuple-element.184.pre_ref, bf16[192,1024]{1,0:T(8,128)(2,1)} %get-tuple-element.185.v_ref, f32[3,1,1024]{2,1,0:T(1,128)} %get-tuple-element.186.lse_ref, ...), custom_call_target="tpu_custom_call" | custom-call | flops 20000000000 | bytes 6000000 | tf_op jit(solution)/shard_map/attend_bwd/pallas_call | solution.py:356
  360.2 12.5 %mlp_grads.3 = (bf16[16,960,128]{2,1,0:T(8,128)(2,1)}, bf16[16,960,128]{2,1,0:T(8,128)(2,1)}, f32[8,128]{1,0:T(8,128)}) custom-call(s32[96]{0:T(128)} %get-tuple-element.256.refs_0_, bf16[1024,768]{1,0:T(8,128)(2,1)} %all-gather.14.cloned.1.call-done.refs_1_, ...), custom_call_target="tpu_custom_call", output_to_operand_aliasing={{0}: (5, {}), {1}: (6, {})} | custom-call | flops 5000000000 | bytes 10000000 | tf_op jit(solution)/shard_map/mlp_grads/pallas_call | solution.py:571
  374.5 4.6 input_bwd.3
  381.0 4.1 collective-permute-start.38
  388.3 5.6 head_grads.3
  398.8 11.2 %collective-permute-start.40 = (bf16[16,960,128]{2,1,0:T(8,128)(2,1)}, bf16[16,960,128]{2,1,0:T(8,128)(2,1)S(1)}, u32[]{:S(2)}, u32[]{:S(2)}) collective-permute-start(bf16[16,960,128]{2,1,0:T(8,128)(2,1)} %get-tuple-element.264), channel_id=1, source_target_pairs={{0,4},{4,0},{8,12},{12,8},{16,20},{20,16},{24,28},{28,24},{32,36},... | collective-permute-start | bytes 11796488 | tf_op jit(solution)/shard_map/ppermute | solution.py:848
  410.0 6.6 %collective-permute-done.40.got = bf16[16,960,128]{2,1,0:T(8,128)(2,1)S(1)} collective-permute-done((bf16[16,960,128]{2,1,0:T(8,128)(2,1)}, bf16[16,960,128]{2,1,0:T(8,128)(2,1)S(1)}, u32[]{:S(2)}, u32[]{:S(2)}) %collective-permute-start.40) | collective-permute-done | bytes 3932192 | tf_op jit(solution)/shard_map/ppermute | solution.py:848
  425.9 7.6 %collective-permute-done.41.refs_1_ = bf16[4,480,128]{2,1,0:T(8,128)(2,1)S(1)} collective-permute-done((bf16[4,480,128]{2,1,0:T(8,128)(2,1)S(1)}, bf16[4,480,128]{2,1,0:T(8,128)(2,1)S(1)}, u32[]{:S(2)}, u32[]{:S(2)}) %collective-permute-start.41) | collective-permute-done | bytes 491552 | tf_op jit(solution)/shard_map/ppermute | solution.py:848
  433.5 12.3 %collective-permute-done.42.refs_2_ = bf16[4,480,128]{2,1,0:T(8,128)(2,1)S(1)} collective-permute-done((bf16[4,480,128]{2,1,0:T(8,128)(2,1)S(1)}, bf16[4,480,128]{2,1,0:T(8,128)(2,1)S(1)}, u32[]{:S(2)}, u32[]{:S(2)}) %collective-permute-start.42) | collective-permute-done | bytes 491552 | tf_op jit(solution)/shard_map/ppermute | solution.py:848
  447.7 8.8 %collective-permute-done.46.refs_7_ = bf16[4,480,128]{2,1,0:T(8,128)(2,1)S(1)} collective-permute-done((bf16[4,480,128]{2,1,0:T(8,128)(2,1)S(1)}, bf16[4,480,128]{2,1,0:T(8,128)(2,1)S(1)}, u32[]{:S(2)}, u32[]{:S(2)}) %collective-permute-start.46) | collective-permute-done | bytes 491552 | tf_op jit(solution)/shard_map/ppermute | solution.py:848
  475.6 5.7 %collective-permute-start.56 = (f32[8,128]{1,0:T(8,128)S(1)}, f32[8,128]{1,0:T(8,128)S(1)}, u32[]{:S(2)}, u32[]{:S(2)}) collective-permute-start(f32[8,128]{1,0:T(8,128)S(1)} %add_add_fusion.4), channel_id=1, source_target_pairs={{0,4},{4,0},{8,12},{12,8},{16,20},{20,16},{24,28},{28,24},{32,36},... | collective-permute-start | bytes 12296 | tf_op jit(solution)/shard_map/ppermute | solution.py:848
  485.4 6.0 %soap_mid.1 = (f32[3,192,192]{2,1,0:T(8,128)S(1)}, f32[3,192,192]{2,1,0:T(8,128)S(1)}, f32[3,192,192]{2,1,0:T(8,128)S(1)}, f32[3,192,192]{2,1,0:T(8,128)S(1)}, f...) custom-call(s32[3]{0:T(128)S(1)} %get-tuple-element.250.flip_ref, f32[3,288,128]{2,1,0:T(8,128)S(1)} %bitcast.114, ...), custom_call_target="tpu_custom_call" | custom-call | flops 1000000000 | bytes 4000000 | tf_op jit(solution)/shard_map/soap_mid/pallas_call | solution.py:819
  510.7 23.5 %soap_late.1 = (f32[3,192,192]{2,1,0:T(8,128)}, f32[3,192,192]{2,1,0:T(8,128)}, f32[3,192,192]{2,1,0:T(8,128)}) custom-call(f32[1,1]{1,0:T(1,128)} %bitcast.44.f_ref, f32[3,192,192]{2,1,0:T(8,128)} %copy-done.3, f32[3,192,192]{2,1,0:T(8,128)} %copy-done.6, f32[3,192,192]{2,1,0:T(8,128)} %copy-done.8, f32[3,192,192]{2,1,0:T(8,128)} %copy-done.44, ...), custom_call_target="tpu_custom_call" | custom-call | flops 1000000000 | bytes 10000000 | tf_op jit(solution)/shard_map/soap_late/pallas_call | solution.py:828
  539.1 9.6 %all-gather.24.cloned.1.call-done = f32[3072,128]{1,0:T(8,128)} async-done(((f32[96,128]{1,0:T(8,128)}), f32[3072,128]{1,0:T(8,128)}) %all-gather.24.cloned.1.call-update) | async-done | bytes 1572880 | tf_op jit(solution)/shard_map/all_gather | solution.py:1083
  (574 shorter events, 193.3 us)
Async XLA Ops:
  7.2 114.4 %all-gather.10.cloned.1.call-start = ((), (), s32[]{:S(2)}) async-start(), calls=%async_computation | async-start | bytes 28532736 | tf_op jit(solution)/shard_map/all_gather | solution.py:913
  11.3 176.3 %all-gather.12.cloned.1.call-start = ((), (), s32[]{:S(2)}) async-start(), calls=%async_computation.1 | async-start | bytes 1966080 | tf_op jit(solution)/shard_map/all_gather | solution.py:915
  17.3 21.0 %collective-permute-start.2 = (bf16[256,192]{0,1:T(8,128)(2,1)S(1)}, bf16[256,192]{0,1:T(8,128)(2,1)S(1)}, u32[]{:S(2)}, u32[]{:S(2)}) collective-permute-start(bf16[256,192]{0,1:T(8,128)(2,1)S(1)} %get-tuple-element.279), channel_id=1, source_target_pairs={{0,3},{1,2},{2,1},{3,0},{4,7},{5,6},{6,5},{7,4},{8,11},{9,10},{10,... | collective-permute-start | bytes 294920 | tf_op jit(solution)/shard_map/ppermute | solution.py:848
  19.8 18.4 %collective-permute-start.1 = (bf16[256,192]{0,1:T(8,128)(2,1)S(1)}, bf16[256,192]{0,1:T(8,128)(2,1)S(1)}, u32[]{:S(2)}, u32[]{:S(2)}) collective-permute-start(bf16[256,192]{0,1:T(8,128)(2,1)S(1)} %get-tuple-element.280), channel_id=1, source_target_pairs={{0,2},{1,3},{2,0},{3,1},{4,6},{5,7},{6,4},{7,5},{8,10},{9,11},{10,... | collective-permute-start | bytes 294920 | tf_op jit(solution)/shard_map/ppermute | solution.py:848
  21.2 208.5 %all-gather.14.cloned.1.call-start = ((), (), s32[]{:S(2)}) async-start(), calls=%async_computation.2 | async-start | bytes 1966080 | tf_op jit(solution)/shard_map/all_gather | solution.py:964
  40.2 23.8 %collective-permute-start.12 = (bf16[256,768]{1,0:T(8,128)(2,1)S(1)}, bf16[256,768]{1,0:T(8,128)(2,1)}, u32[]{:S(2)}, u32[]{:S(2)}) collective-permute-start(bf16[256,768]{1,0:T(8,128)(2,1)S(1)} %multiply_convert_fusion.refs_0_), channel_id=1, source_target_pairs={{0,3},{1,2},{2,1},{3,0},{4,7},{5,6},{6,5},{7,4},{8,11},{9,10},{10,... | collective-permute-start | bytes 1179656 | tf_op jit(solution)/shard_map/ppermute | solution.py:848
  41.7 22.3 %collective-permute-start.11 = (bf16[256,768]{1,0:T(8,128)(2,1)S(1)}, bf16[256,768]{1,0:T(8,128)(2,1)}, u32[]{:S(2)}, u32[]{:S(2)}) collective-permute-start(bf16[256,768]{1,0:T(8,128)(2,1)S(1)} %multiply_convert_fusion.refs_0_), channel_id=1, source_target_pairs={{0,2},{1,3},{2,0},{3,1},{4,6},{5,7},{6,4},{7,5},{8,10},{9,11},{10,... | collective-permute-start | bytes 1179656 | tf_op jit(solution)/shard_map/ppermute | solution.py:848
  42.4 25.0 %collective-permute-start.10 = (bf16[256,768]{1,0:T(8,128)(2,1)S(1)}, bf16[256,768]{1,0:T(8,128)(2,1)}, u32[]{:S(2)}, u32[]{:S(2)}) collective-permute-start(bf16[256,768]{1,0:T(8,128)(2,1)S(1)} %multiply_convert_fusion.refs_0_), channel_id=1, source_target_pairs={{0,1},{1,0},{2,3},{3,2},{4,5},{5,4},{6,7},{7,6},{8,9},{9,8},{10,11... | collective-permute-start | bytes 1179656 | tf_op jit(solution)/shard_map/ppermute | solution.py:848
  139.7 15.2 %collective-permute-start.13 = (bf16[192,256]{1,0:T(8,128)(2,1)}, bf16[192,256]{1,0:T(8,128)(2,1)S(1)}, u32[]{:S(2)}, u32[]{:S(2)}) collective-permute-start(bf16[192,256]{1,0:T(8,128)(2,1)} %get-tuple-element.144.refs_4_), channel_id=1, source_target_pairs={{0,1},{1,0},{2,3},{3,2},{4,5},{5,4},{6,7},{7,6},{8,9},{9,8},{10,11... | collective-permute-start | bytes 294920 | tf_op jit(solution)/shard_map/ppermute | solution.py:848
  166.2 19.4 %collective-permute-start.18 = (bf16[256,768]{1,0:T(8,128)(2,1)}, bf16[256,768]{1,0:T(8,128)(2,1)S(1)}, u32[]{:S(2)}, u32[]{:S(2)}) collective-permute-start(bf16[256,768]{1,0:T(8,128)(2,1)} %get-tuple-element.152.a0.refs_11_), channel_id=1, source_target_pairs={{0,3},{1,2},{2,1},{3,0},{4,7},{5,6},{6,5},{7,4},{8,11},{9,10},{10,... | collective-permute-start | bytes 1179656 | tf_op jit(solution)/shard_map/ppermute | solution.py:848
  168.7 17.0 %collective-permute-start.17 = (bf16[256,768]{1,0:T(8,128)(2,1)}, bf16[256,768]{1,0:T(8,128)(2,1)S(1)}, u32[]{:S(2)}, u32[]{:S(2)}) collective-permute-start(bf16[256,768]{1,0:T(8,128)(2,1)} %get-tuple-element.152.a0.refs_11_), channel_id=1, source_target_pairs={{0,2},{1,3},{2,0},{3,1},{4,6},{5,7},{6,4},{7,5},{8,10},{9,11},{10,... | collective-permute-start | bytes 1179656 | tf_op jit(solution)/shard_map/ppermute | solution.py:848
  168.7 17.3 %collective-permute-start.16 = (bf16[256,768]{1,0:T(8,128)(2,1)}, bf16[256,768]{1,0:T(8,128)(2,1)S(1)}, u32[]{:S(2)}, u32[]{:S(2)}) collective-permute-start(bf16[256,768]{1,0:T(8,128)(2,1)} %get-tuple-element.152.a0.refs_11_), channel_id=1, source_target_pairs={{0,1},{1,0},{2,3},{3,2},{4,5},{5,4},{6,7},{7,6},{8,9},{9,8},{10,11... | collective-permute-start | bytes 1179656 | tf_op jit(solution)/shard_map/ppermute | solution.py:848
  186.8 104.5 %all-gather.16.cloned.1.call-start = ((), (), s32[]{:S(2)}) async-start(), calls=%async_computation.3 | async-start | bytes 3932160 | tf_op jit(solution)/shard_map/all_gather | solution.py:1007
  243.4 86.6 %all-gather.20.cloned.1.call-start = ((), (), s32[]{:S(2)}) async-start(), calls=%async_computation.5 | async-start | bytes 1966080 | tf_op jit(solution)/shard_map/all_gather | solution.py:1014
  268.9 91.2 %all-gather.22.cloned.1.call-start = ((), (), s32[]{:S(2)}) async-start(), calls=%async_computation.6 | async-start | bytes 1966080 | tf_op jit(solution)/shard_map/all_gather | solution.py:1009
  287.2 17.2 %collective-permute-start.28 = (bf16[576,256]{1,0:T(8,128)(2,1)}, bf16[576,256]{1,0:T(8,128)(2,1)S(1)}, u32[]{:S(2)}, u32[]{:S(2)}) collective-permute-start(bf16[576,256]{1,0:T(8,128)(2,1)} %get-tuple-element.173.refs_8_), channel_id=1, source_target_pairs={{0,1},{1,0},{2,3},{3,2},{4,5},{5,4},{6,7},{7,6},{8,9},{9,8},{10,11... | collective-permute-start | bytes 884744 | tf_op jit(solution)/shard_map/ppermute | solution.py:848
  287.2 17.2 %collective-permute-start.29 = (bf16[576,256]{1,0:T(8,128)(2,1)}, bf16[576,256]{1,0:T(8,128)(2,1)S(1)}, u32[]{:S(2)}, u32[]{:S(2)}) collective-permute-start(bf16[576,256]{1,0:T(8,128)(2,1)} %get-tuple-element.174.refs_9_), channel_id=1, source_target_pairs={{0,2},{1,3},{2,0},{3,1},{4,6},{5,7},{6,4},{7,5},{8,10},{9,11},{10,... | collective-permute-start | bytes 884744 | tf_op jit(solution)/shard_map/ppermute | solution.py:848
  289.1 15.3 %collective-permute-start.30 = (bf16[576,256]{1,0:T(8,128)(2,1)}, bf16[576,256]{1,0:T(8,128)(2,1)S(1)}, u32[]{:S(2)}, u32[]{:S(2)}) collective-permute-start(bf16[576,256]{1,0:T(8,128)(2,1)} %get-tuple-element.175.refs_10_), channel_id=1, source_target_pairs={{0,3},{1,2},{2,1},{3,0},{4,7},{5,6},{6,5},{7,4},{8,11},{9,10},{10,... | collective-permute-start | bytes 884744 | tf_op jit(solution)/shard_map/ppermute | solution.py:848
  309.9 78.4 %all-gather.18.cloned.1.call-start = ((), (), s32[]{:S(2)}) async-start(), calls=%async_computation.4 | async-start | bytes 1966080 | tf_op jit(solution)/shard_map/all_gather | solution.py:1014
  336.9 211.8 %all-gather.24.cloned.1.call-start = ((), (), s32[]{:S(2)}) async-start(), calls=%async_computation.7 | async-start | bytes 1622016 | tf_op jit(solution)/shard_map/all_gather | solution.py:1083
  356.1 17.2 %collective-permute-start.34 = (bf16[576,256]{1,0:T(8,128)(2,1)}, bf16[576,256]{1,0:T(8,128)(2,1)S(1)}, u32[]{:S(2)}, u32[]{:S(2)}) collective-permute-start(bf16[576,256]{1,0:T(8,128)(2,1)} %get-tuple-element.193.refs_8_), channel_id=1, source_target_pairs={{0,1},{1,0},{2,3},{3,2},{4,5},{5,4},{6,7},{7,6},{8,9},{9,8},{10,11... | collective-permute-start | bytes 884744 | tf_op jit(solution)/shard_map/ppermute | solution.py:848
  356.1 17.2 %collective-permute-start.35 = (bf16[576,256]{1,0:T(8,128)(2,1)}, bf16[576,256]{1,0:T(8,128)(2,1)S(1)}, u32[]{:S(2)}, u32[]{:S(2)}) collective-permute-start(bf16[576,256]{1,0:T(8,128)(2,1)} %get-tuple-element.194.refs_9_), channel_id=1, source_target_pairs={{0,2},{1,3},{2,0},{3,1},{4,6},{5,7},{6,4},{7,5},{8,10},{9,11},{10,... | collective-permute-start | bytes 884744 | tf_op jit(solution)/shard_map/ppermute | solution.py:848
  358.3 16.2 %collective-permute-start.36 = (bf16[576,256]{1,0:T(8,128)(2,1)}, bf16[576,256]{1,0:T(8,128)(2,1)S(1)}, u32[]{:S(2)}, u32[]{:S(2)}) collective-permute-start(bf16[576,256]{1,0:T(8,128)(2,1)} %get-tuple-element.195.refs_10_), channel_id=1, source_target_pairs={{0,3},{1,2},{2,1},{3,0},{4,7},{5,6},{6,5},{7,4},{8,11},{9,10},{10,... | collective-permute-start | bytes 884744 | tf_op jit(solution)/shard_map/ppermute | solution.py:848
  398.8 17.8 %collective-permute-start.40 = (bf16[16,960,128]{2,1,0:T(8,128)(2,1)}, bf16[16,960,128]{2,1,0:T(8,128)(2,1)S(1)}, u32[]{:S(2)}, u32[]{:S(2)}) collective-permute-start(bf16[16,960,128]{2,1,0:T(8,128)(2,1)} %get-tuple-element.264), channel_id=1, source_target_pairs={{0,4},{4,0},{8,12},{12,8},{16,20},{20,16},{24,28},{28,24},{32,36},... | collective-permute-start | bytes 11796488 | tf_op jit(solution)/shard_map/ppermute | solution.py:848
  421.8 24.0 %collective-permute-start.42 = (bf16[4,480,128]{2,1,0:T(8,128)(2,1)S(1)}, bf16[4,480,128]{2,1,0:T(8,128)(2,1)S(1)}, u32[]{:S(2)}, u32[]{:S(2)}) collective-permute-start(bf16[4,480,128]{2,1,0:T(8,128)(2,1)S(1)} %get-tuple-element.214), channel_id=1, source_target_pairs={{0,64},{4,68},{8,72},{12,76},{16,80},{20,84},{24,88},{28,92},{32,9... | collective-permute-start | bytes 1474568 | tf_op jit(solution)/shard_map/ppermute | solution.py:848
  424.2 23.5 %collective-permute-start.43 = (bf16[4,480,128]{2,1,0:T(8,128)(2,1)S(1)}, bf16[4,480,128]{2,1,0:T(8,128)(2,1)S(1)}, u32[]{:S(2)}, u32[]{:S(2)}) collective-permute-start(bf16[4,480,128]{2,1,0:T(8,128)(2,1)S(1)} %get-tuple-element.215), channel_id=1, source_target_pairs={{0,96},{4,100},{8,104},{12,108},{16,112},{20,116},{24,120},{28,124... | collective-permute-start | bytes 1474568 | tf_op jit(solution)/shard_map/ppermute | solution.py:848
  424.9 22.8 %collective-permute-start.44 = (bf16[4,480,128]{2,1,0:T(8,128)(2,1)S(1)}, bf16[4,480,128]{2,1,0:T(8,128)(2,1)S(1)}, u32[]{:S(2)}, u32[]{:S(2)}) collective-permute-start(bf16[4,480,128]{2,1,0:T(8,128)(2,1)S(1)} %get-tuple-element.217), channel_id=1, source_target_pairs={{0,8},{4,12},{8,0},{12,4},{16,24},{20,28},{24,16},{28,20},{32,40},... | collective-permute-start | bytes 1474568 | tf_op jit(solution)/shard_map/ppermute | solution.py:848
  424.9 22.8 %collective-permute-start.45 = (bf16[4,480,128]{2,1,0:T(8,128)(2,1)S(1)}, bf16[4,480,128]{2,1,0:T(8,128)(2,1)S(1)}, u32[]{:S(2)}, u32[]{:S(2)}) collective-permute-start(bf16[4,480,128]{2,1,0:T(8,128)(2,1)S(1)} %get-tuple-element.218), channel_id=1, source_target_pairs={{0,16},{4,20},{8,24},{12,28},{16,0},{20,4},{24,8},{28,12},{32,48},... | collective-permute-start | bytes 1474568 | tf_op jit(solution)/shard_map/ppermute | solution.py:848
  433.5 23.1 %collective-permute-start.46 = (bf16[4,480,128]{2,1,0:T(8,128)(2,1)S(1)}, bf16[4,480,128]{2,1,0:T(8,128)(2,1)S(1)}, u32[]{:S(2)}, u32[]{:S(2)}) collective-permute-start(bf16[4,480,128]{2,1,0:T(8,128)(2,1)S(1)} %get-tuple-element.219), channel_id=1, source_target_pairs={{0,24},{4,28},{8,16},{12,20},{16,8},{20,12},{24,0},{28,4},{32,56},... | collective-permute-start | bytes 1474568 | tf_op jit(solution)/shard_map/ppermute | solution.py:848
  482.1 16.8 %collective-permute-start.59 = (f32[8,128]{1,0:T(8,128)S(1)}, f32[8,128]{1,0:T(8,128)S(1)}, u32[]{:S(2)}, u32[]{:S(2)}) collective-permute-start(f32[8,128]{1,0:T(8,128)S(1)} %add.386), channel_id=1, source_target_pairs={{0,24},{4,28},{8,16},{12,20},{16,8},{20,12},{24,0},{28,4},{32,56},... | collective-permute-start | bytes 12296 | tf_op jit(solution)/shard_map/ppermute | solution.py:848
  483.5 15.5 %collective-permute-start.58 = (f32[8,128]{1,0:T(8,128)S(1)}, f32[8,128]{1,0:T(8,128)S(1)}, u32[]{:S(2)}, u32[]{:S(2)}) collective-permute-start(f32[8,128]{1,0:T(8,128)S(1)} %add.386), channel_id=1, source_target_pairs={{0,16},{4,20},{8,24},{12,28},{16,0},{20,4},{24,8},{28,12},{32,48},... | collective-permute-start | bytes 12296 | tf_op jit(solution)/shard_map/ppermute | solution.py:848
  483.5 15.5 %collective-permute-start.57 = (f32[8,128]{1,0:T(8,128)S(1)}, f32[8,128]{1,0:T(8,128)}, u32[]{:S(2)}, u32[]{:S(2)}) collective-permute-start(f32[8,128]{1,0:T(8,128)S(1)} %add.386), channel_id=1, source_target_pairs={{0,8},{4,12},{8,0},{12,4},{16,24},{20,28},{24,16},{28,20},{32,40},... | collective-permute-start | bytes 12296 | tf_op jit(solution)/shard_map/ppermute | solution.py:848
  (136 other events, 1756.9 us)
Sparse Core Ops, SparseCore 0:
  11.6 109.9 all-gather.9
  123.3 28.4 all-gather.11
  186.9 31.2 all-gather.13
  243.5 46.5 all-gather.15
  291.7 27.6 all-gather.19
  320.8 27.4 all-gather.21
  350.0 38.1 all-gather.17
  504.7 43.9 all-gather.23

commit v5 on v4

--- a/solution.py
+++ b/solution.py
@@ -659,6 +659,32 @@
         out_shape=([shape((half, 128))] + [shape((half, 128), bf16)] * 3) * 2,
         compiler_params=params(32), cost_estimate=cost(10**7, 6 * 10**6), name="add_axis",
     )(*a, *b)
+
+
+def add_last(loss_ref, *refs):
+    ins, (slots, share, squares) = (refs[:8], refs[8:])
+    halves = []
+    for side in range(2):
+        own, r1, r2, r3 = ins[4 * side : 4 * side + 4]
+        halves.append((own[...] + r1[...].astype(f32)) + (r2[...].astype(f32) + r3[...].astype(f32)))
+    mine = jnp.concatenate(halves, axis=0)
+    for j in range(3):
+        slots[j] = mine[PACK * j : PACK * j + PACK]
+    small = mine[3 * PACK :]
+    share[...] = small
+    lower = lax.broadcasted_iota(jnp.int32, (SMALL, 128), 0) < EMBED_ROWS + HEAD_ROWS
+    weighted = small * small * jnp.where(lower, 1.0, 0.25)
+    own_part = jnp.sum(mine[: 3 * PACK] * mine[: 3 * PACK], keepdims=True) + jnp.sum(weighted, keepdims=True)
+    row = lax.broadcasted_iota(jnp.int32, (8, 128), 0)
+    squares[...] = jnp.where(row == 0, own_part, loss_ref[...] * 0.25)
+
+
+def run_add_last(loss, a, b):
+    return pl.pallas_call(
+        add_last, in_specs=[VM] * 9, out_specs=[VM] * 3,
+        out_shape=[shape((3, PACK, 128)), shape((SMALL, 128)), shape((8, 128))],
+        compiler_params=params(32), cost_estimate=cost(10**6, 2 * 10**6), name="add_last",
+    )(loss, *a, *b)
 
 
 def gate(array, *others):
@@ -1051,36 +1077,27 @@
         [sums[0]] + [swap_dp(sums[r], 8 * r) for r in (1, 2, 3)],
         [sums[4]] + [swap_dp(sums[4 + r], 2 * r) for r in (1, 2, 3)],
     )
-    mine = jnp.concatenate(
-        [
-            sum_four([sums[0]] + [swap_dp(sums[r], 2 * r).astype(f32) for r in (1, 2, 3)]),
-            sum_four([sums[4]] + [swap_dp(sums[4 + r], 8 * r).astype(f32) for r in (1, 2, 3)]),
-        ],
-        axis=0,
-    )
-    mine_slots = mine[: 3 * PACK]
-    share = mine[3 * PACK :]
+    mine_slots, share, squares = run_add_last(
+        local_loss.reshape(1, 1),
+        [sums[0]] + [swap_dp(sums[r], 2 * r) for r in (1, 2, 3)],
+        [sums[4]] + [swap_dp(sums[4 + r], 8 * r) for r in (1, 2, 3)],
+    )
+    shares = lax.all_gather(share, "dp", axis=0)
     cut_at = EMBED_ROWS + HEAD_ROWS
-    local_squares = (
-        jnp.sum(mine_slots * mine_slots)
-        + jnp.sum(share[:cut_at] * share[:cut_at])
-        + jnp.sum(share[cut_at:] * share[cut_at:]) * 0.25
-    )
+
     def flat(tiles):
         return tiles.reshape(3, TILE * TILE)
 
     grad_tiles, turned, left_new, right_new, gram_left, gram_right = run_soap_mid(
-        flips.astype(jnp.int32), mine_slots.reshape(3, PACK, 128), left, right
-    )
-    rows = jnp.arange(8)[:, None] + jnp.zeros((8, 128), jnp.int32)
-    squares = total_mp(jnp.where(rows == 0, local_squares, local_loss * 0.25))
+        flips.astype(jnp.int32), mine_slots, left, right
+    )
+    squares = total_mp(squares)
     squares = squares + swap_dp(squares, 1)
     squares = sum_four([squares] + [swap_dp(squares, 2 * r) for r in (1, 2, 3)])
     flats = [flat(grad_tiles), flat(turned), flat(gram_left), flat(gram_right)]
     squares = gate(squares, *flats)
     squares = sum_four([squares] + [swap_dp(squares, 8 * r) for r in (1, 2, 3)])
     squares, loss_total = (squares[0, 0], squares[1, 0])
-    shares = lax.all_gather(share, "dp", axis=0)
     grad_norm = jnp.sqrt(squares)
     factor = clip_limit / jnp.maximum(grad_norm, clip_limit)
 

time: 575 us -> 572 us (level)
    unnamed x202 -> x200, local copies, waits for them, and re-layouts: 21 us -> 21.1 us
  transfers between devices with their start and end apart: 71 -> 71, of which waited for: 26 -> 28; matrix products, arithmetic and copies ran while one was open for 9% -> 9% of each run, Pallas kernels for 38% -> 38%
where the time goes in v5:
time: 572 us; the launch traced here: 563 us
  Pallas kernels  219 us (38%)
  waiting for transfers between devices  139 us (24%)
  starting transfers between devices  94 us (16%)
  local copies, waits for them, and re-layouts  52.5 us (9%)
  other arithmetic  32.5 us (6%)
  between operations  18.1 us (3%)
  matrix products  7.95 us (1%)
    ppermute x63, starting transfers between devices, swap(): return lax.ppermute(array, axis, [(i, i ^ r) for i in range(size)])  92.6 us
    ppermute x63, waiting for transfers between devices, swap(): return lax.ppermute(array, axis, [(i, i ^ r) for i in range(size)])  74.1 us
    all_gather x1, waiting for transfers between devices, shards(): slots = lax.all_gather(pack_tile(low), ('dp', 'mp'), axis=0, tiled=True)  55.6 us
    pallas_call x4, Pallas kernels, grads_call(): pl.pallas_call(kernel, grid=(1,), in_specs=[SM] * len(scalars) + specs +...  36.7 us
    pallas_call x2, Pallas kernels, run_attend_bwd(): pl.pallas_call(attend_bwd, in_specs=[VM] * 10, out_specs=[VM] * 5, out_sh...  35.3 us
    pallas_call x2, Pallas kernels, run_attend_fwd(): pl.pallas_call(attend_fwd, grid=(1,), in_specs=[pl.BlockSpec((1, 3 * TILE...  27.6 us
    pallas_call x3, Pallas kernels, assemble(): pl.pallas_call(kernel, in_specs=[SM, ANY], out_specs=[ANY] * len(groups),...  27.5 us
    pallas_call x2, Pallas kernels, run_mix_bwd(): pl.pallas_call(mix_bwd, in_specs=[VM] * 5 + [ANY] * 3, out_specs=[VM] * 7...  25 us
  transfers between devices with their start and end apart: 71, of which 28 were waited for; matrix products, arithmetic and copies ran while one was open for 9% of the time, Pallas kernels for 38%

profile of v5, /device:TPU:1, one launch (start us, length us, event | category | flops | bytes accessed | tf_op | source)
XLA Modules:
  0.0 563.4 jit_solution(13650881033583669806)
XLA Ops:
  27.0 3.7 collective-permute-start.5
  58.5 4.9 collective-permute-done.12.a3.refs_14_
  65.9 55.6 %all-gather.10.cloned.1.call-done.slots_ref = bf16[384,288,128]{2,1,0:T(8,128)(2,1)} async-done(((bf16[3,288,128]{2,1,0:T(8,128)(2,1)}), bf16[384,288,128]{2,1,0:T(8,128)(2,1)}) %all-gather.10.cloned.1.call-update) | async-done | bytes 28311568 | tf_op jit(solution)/shard_map/all_gather | solution.py:939
  121.6 4.3 assemble.3
  125.9 13.8 %attend_fwd.2 = (f32[384,1024]{1,0:T(8,128)}, bf16[192,1024]{1,0:T(8,128)(2,1)}, f32[3,1,1024]{2,1,0:T(1,128)}, bf16[192,256]{1,0:T(8,128)(2,1)}, bf16[192,256]{...) custom-call(bf16[4,576,768]{2,1,0:T(8,128)(2,1)} %bitcast.119, bf16[256,768]{1,0:T(8,128)(2,1)} %copy-done.4, ...), custom_call_target="tpu_custom_call" | custom-call | flops 10000000000 | bytes 6000000 | tf_op jit(solution)/shard_map/attend_fwd/pallas_call | solution.py:275
  144.6 10.2 %assemble.4 = (bf16[4,192,768]{2,1,0:T(8,128)(2,1)}, bf16[16,192,768]{2,1,0:T(8,128)(2,1)}, bf16[16,192,768]{2,1,0:T(8,128)(2,1)}) custom-call(s32[384]{0:T(512)} %add.304.table_ref, bf16[384,288,128]{2,1,0:T(8,128)(2,1)} %all-gather.10.cloned.1.call-done.slots_ref), custom_call_target="tpu_custom_call" | custom-call | bytes 21233664 | tf_op jit(solution)/shard_map/assemble/pallas_call | solution.py:197
  155.6 10.6 %mix_fwd.2 = (f32[256,768]{1,0:T(8,128)}, bf16[256,768]{1,0:T(8,128)(2,1)}, f32[256,768]{1,0:T(8,128)}, bf16[256,768]{1,0:T(8,128)(2,1)}) custom-call(f32[256,768]{1,0:T(8,128)} %convert_element_type.74.x_ref, bf16[192,256]{1,0:T(8,128)(2,1)} %get-tuple-element.146.o0.refs_3_, bf16[192,256]{1,0:T(8,128)(2,1)} %copy-done.88, bf16[192,256]{1,0:T(8,128)(2,1)} %copy-done.89, ...), custom_call_target="tpu_custom_call" | custom-call | flops 6000000000 | bytes 17000000 | tf_op jit(solution)/shard_map/mix_fwd/pallas_call | solution.py:421
  169.5 13.0 %assemble.5 = (bf16[12,192,768]{2,1,0:T(8,128)(2,1)}, bf16[4,192,768]{2,1,0:T(8,128)(2,1)}, bf16[16,192,768]{2,1,0:T(8,128)(2,1)}, bf16[16,192,768]{2,1,0:T(8,128)(2,1)}) custom-call(s32[384]{0:T(512)} %add.304.table_ref, bf16[384,288,128]{2,1,0:T(8,128)(2,1)} %all-gather.10.cloned.1.call-done.slots_ref), custom_call_target="tpu_custom_call" | custom-call | bytes 28311552 | tf_op jit(solution)/shard_map/assemble/pallas_call | solution.py:197
  188.2 13.8 %attend_fwd.3 = (f32[384,1024]{1,0:T(8,128)}, bf16[192,1024]{1,0:T(8,128)(2,1)}, f32[3,1,1024]{2,1,0:T(1,128)}, bf16[192,256]{1,0:T(8,128)(2,1)}, bf16[192,256]{...) custom-call(bf16[4,576,768]{2,1,0:T(8,128)(2,1)} %bitcast.117, ...), custom_call_target="tpu_custom_call" | custom-call | flops 10000000000 | bytes 6000000 | tf_op jit(solution)/shard_map/attend_fwd/pallas_call | solution.py:275
  208.3 7.3 %collective-permute-done.20.o2 = bf16[192,256]{1,0:T(8,128)(2,1)S(1)} collective-permute-done((bf16[192,256]{1,0:T(8,128)(2,1)}, bf16[192,256]{1,0:T(8,128)(2,1)S(1)}, u32[]{:S(2)}, u32[]{:S(2)}) %collective-permute-start.20) | collective-permute-done | bytes 98336 | tf_op jit(solution)/shard_map/ppermute | solution.py:874
  216.3 10.6 %mix_fwd.3 = (f32[256,768]{1,0:T(8,128)}, bf16[256,768]{1,0:T(8,128)(2,1)}, f32[256,768]{1,0:T(8,128)}, bf16[256,768]{1,0:T(8,128)(2,1)}) custom-call(f32[256,768]{1,0:T(8,128)} %get-tuple-element.153.x_ref, bf16[192,256]{1,0:T(8,128)(2,1)} %get-tuple-element.156.o0.refs_3_, bf16[192,256]{1,0:T(8,128)(2,1)} %copy-done.90, bf16[192,256]{1,0:T(8,128)(2,1)} %copy-done.92, ...), custom_call_target="tpu_custom_call" | custom-call | flops 6000000000 | bytes 17000000 | tf_op jit(solution)/shard_map/mix_fwd/pallas_call | solution.py:421
  244.7 12.5 %mix_bwd.2 = (f32[256,768]{1,0:T(8,128)}, bf16[256,768]{1,0:T(8,128)(2,1)}, f32[1,768]{1,0:T(1,128)}, bf16[192,256]{1,0:T(8,128)(2,1)}, bf16[192,256]{1,0:T(8,12...) custom-call(f32[256,768]{1,0:T(8,128)} %get-tuple-element.259.g_ref, bf16[256,768]{1,0:T(8,128)(2,1)} %copy-done.62, ...), custom_call_target="tpu_custom_call" | custom-call | flops 6000000000 | bytes 17000000 | tf_op jit(solution)/shard_map/mix_bwd/pallas_call | solution.py:462
  263.3 4.8 collective-permute-done.26.g2.refs_2_
  269.5 17.6 %attend_bwd.2 = (bf16[576,256]{1,0:T(8,128)(2,1)}, bf16[576,256]{1,0:T(8,128)(2,1)}, bf16[576,256]{1,0:T(8,128)(2,1)}, bf16[576,256]{1,0:T(8,128)(2,1)}, f32[64,2]{1,0:T(8,128)}) custom-call(f32[384,1024]{1,0:T(8,128)} %get-tuple-element.168.pre_ref, bf16[192,1024]{1,0:T(8,128)(2,1)} %get-tuple-element.169.v_ref, f32[3,1,1024]{2,1,0:T(1,128)} %get-tuple-element.170.lse_ref, ...), custom_call_target="tpu_custom_call" | custom-call | flops 20000000000 | bytes 6000000 | tf_op jit(solution)/shard_map/attend_bwd/pallas_call | solution.py:356
  291.2 12.4 %mlp_grads.2 = (bf16[16,960,128]{2,1,0:T(8,128)(2,1)}, bf16[16,960,128]{2,1,0:T(8,128)(2,1)}, f32[8,128]{1,0:T(8,128)}) custom-call(s32[96]{0:T(128)} %get-tuple-element.260.refs_0_, bf16[1024,1536]{1,0:T(8,128)(2,1)} %all-gather.16.cloned.1.call-done.refs_1_.refs_2_, bf16[1024,1536]{1,0:T(8,128)(2,1)} %all-gather.16.cloned.1.call-done.refs_1_.refs_2_, ...), custom_call_target="tpu_custom_call" | custom-call | flops 5000000000 | bytes 10000000 | tf_op jit(solution)/shard_map/mlp_grads/pallas_call | solution.py:571
  304.4 4.4 input_bwd.2
  311.9 12.5 %mix_bwd.3 = (f32[256,768]{1,0:T(8,128)}, bf16[256,768]{1,0:T(8,128)(2,1)}, f32[1,768]{1,0:T(1,128)}, bf16[192,256]{1,0:T(8,128)(2,1)}, bf16[192,256]{1,0:T(8,12...) custom-call(f32[256,768]{1,0:T(8,128)} %copy-done.40, bf16[256,768]{1,0:T(8,128)(2,1)} %get-tuple-element.181.low_ref, ...), custom_call_target="tpu_custom_call" | custom-call | flops 6000000000 | bytes 17000000 | tf_op jit(solution)/shard_map/mix_bwd/pallas_call | solution.py:462
  330.0 6.1 %head_grads.2 = (bf16[16,960,128]{2,1,0:T(8,128)(2,1)}, bf16[16,960,128]{2,1,0:T(8,128)(2,1)}, f32[8,128]{1,0:T(8,128)}) custom-call(s32[96]{0:T(128)} %get-tuple-element.260.refs_0_, s32[1]{0:T(128)} %gate.18.refs_1_, bf16[1024,768]{1,0:T(8,128)(2,1)} %all-gather.20.cloned.1.call-done.refs_2_, ...), custom_call_target="tpu_custom_call", output_to_operand_aliasing={{0}: (15, {}), {1}: (16, {})} | custom-call | flops 2000000000 | bytes 10000000 | tf_op jit(solution)/shard_map/head_grads/pallas_call | solution.py:571
  337.5 17.6 %attend_bwd.3 = (bf16[576,256]{1,0:T(8,128)(2,1)}, bf16[576,256]{1,0:T(8,128)(2,1)}, bf16[576,256]{1,0:T(8,128)(2,1)}, bf16[576,256]{1,0:T(8,128)(2,1)}, f32[64,2]{1,0:T(8,128)}) custom-call(f32[384,1024]{1,0:T(8,128)} %get-tuple-element.187.pre_ref, bf16[192,1024]{1,0:T(8,128)(2,1)} %get-tuple-element.188.v_ref, f32[3,1,1024]{2,1,0:T(1,128)} %get-tuple-element.189.lse_ref, ...), custom_call_target="tpu_custom_call" | custom-call | flops 20000000000 | bytes 6000000 | tf_op jit(solution)/shard_map/attend_bwd/pallas_call | solution.py:356
  360.1 12.5 %mlp_grads.3 = (bf16[16,960,128]{2,1,0:T(8,128)(2,1)}, bf16[16,960,128]{2,1,0:T(8,128)(2,1)}, f32[8,128]{1,0:T(8,128)}) custom-call(s32[96]{0:T(128)} %get-tuple-element.260.refs_0_, bf16[1024,768]{1,0:T(8,128)(2,1)} %all-gather.14.cloned.1.call-done.refs_1_, ...), custom_call_target="tpu_custom_call", output_to_operand_aliasing={{0}: (5, {}), {1}: (6, {})} | custom-call | flops 5000000000 | bytes 10000000 | tf_op jit(solution)/shard_map/mlp_grads/pallas_call | solution.py:571
  374.4 4.6 input_bwd.3
  380.9 4.2 collective-permute-start.38
  388.2 5.6 head_grads.3
  398.8 10.9 %collective-permute-start.40 = (bf16[16,960,128]{2,1,0:T(8,128)(2,1)}, bf16[16,960,128]{2,1,0:T(8,128)(2,1)S(1)}, u32[]{:S(2)}, u32[]{:S(2)}) collective-permute-start(bf16[16,960,128]{2,1,0:T(8,128)(2,1)} %get-tuple-element.268), channel_id=1, source_target_pairs={{0,4},{4,0},{8,12},{12,8},{16,20},{20,16},{24,28},{28,24},{32,36},... | collective-permute-start | bytes 11796488 | tf_op jit(solution)/shard_map/ppermute | solution.py:874
  409.7 6.6 %collective-permute-done.40.got = bf16[16,960,128]{2,1,0:T(8,128)(2,1)S(1)} collective-permute-done((bf16[16,960,128]{2,1,0:T(8,128)(2,1)}, bf16[16,960,128]{2,1,0:T(8,128)(2,1)S(1)}, u32[]{:S(2)}, u32[]{:S(2)}) %collective-permute-start.40) | collective-permute-done | bytes 3932192 | tf_op jit(solution)/shard_map/ppermute | solution.py:874
  425.8 7.3 %collective-permute-done.41.refs_1_ = bf16[4,480,128]{2,1,0:T(8,128)(2,1)S(1)} collective-permute-done((bf16[4,480,128]{2,1,0:T(8,128)(2,1)S(1)}, bf16[4,480,128]{2,1,0:T(8,128)(2,1)S(1)}, u32[]{:S(2)}, u32[]{:S(2)}) %collective-permute-start.41) | collective-permute-done | bytes 491552 | tf_op jit(solution)/shard_map/ppermute | solution.py:874
  433.2 12.4 %collective-permute-done.42.refs_2_ = bf16[4,480,128]{2,1,0:T(8,128)(2,1)S(1)} collective-permute-done((bf16[4,480,128]{2,1,0:T(8,128)(2,1)S(1)}, bf16[4,480,128]{2,1,0:T(8,128)(2,1)S(1)}, u32[]{:S(2)}, u32[]{:S(2)}) %collective-permute-start.42) | collective-permute-done | bytes 491552 | tf_op jit(solution)/shard_map/ppermute | solution.py:874
  447.6 8.6 %collective-permute-done.46.refs_7_ = bf16[4,480,128]{2,1,0:T(8,128)(2,1)S(1)} collective-permute-done((bf16[4,480,128]{2,1,0:T(8,128)(2,1)S(1)}, bf16[4,480,128]{2,1,0:T(8,128)(2,1)S(1)}, u32[]{:S(2)}, u32[]{:S(2)}) %collective-permute-start.46) | collective-permute-done | bytes 491552 | tf_op jit(solution)/shard_map/ppermute | solution.py:874
  475.5 5.8 %collective-permute-start.56 = (f32[8,128]{1,0:T(8,128)S(1)}, f32[8,128]{1,0:T(8,128)S(1)}, u32[]{:S(2)}, u32[]{:S(2)}) collective-permute-start(f32[8,128]{1,0:T(8,128)S(1)} %add_add_fusion.2), channel_id=1, source_target_pairs={{0,4},{4,0},{8,12},{12,8},{16,20},{20,16},{24,28},{28,24},{32,36},... | collective-permute-start | bytes 12296 | tf_op jit(solution)/shard_map/ppermute | solution.py:874
  485.3 6.0 %soap_mid.1 = (f32[3,192,192]{2,1,0:T(8,128)S(1)}, f32[3,192,192]{2,1,0:T(8,128)S(1)}, f32[3,192,192]{2,1,0:T(8,128)S(1)}, f32[3,192,192]{2,1,0:T(8,128)S(1)}, f...) custom-call(s32[3]{0:T(128)S(1)} %get-tuple-element.256.flip_ref, f32[3,288,128]{2,1,0:T(8,128)S(1)} %get-tuple-element.232.packed, ...), custom_call_target="tpu_custom_call" | custom-call | flops 1000000000 | bytes 4000000 | tf_op jit(solution)/shard_map/soap_mid/pallas_call | solution.py:845
  509.8 23.6 %soap_late.1 = (f32[3,192,192]{2,1,0:T(8,128)}, f32[3,192,192]{2,1,0:T(8,128)}, f32[3,192,192]{2,1,0:T(8,128)}) custom-call(f32[1,1]{1,0:T(1,128)} %bitcast.44.f_ref, f32[3,192,192]{2,1,0:T(8,128)} %copy-done.3, f32[3,192,192]{2,1,0:T(8,128)} %copy-done.6, f32[3,192,192]{2,1,0:T(8,128)} %copy-done.8, f32[3,192,192]{2,1,0:T(8,128)} %copy-done.44, ...), custom_call_target="tpu_custom_call" | custom-call | flops 1000000000 | bytes 10000000 | tf_op jit(solution)/shard_map/soap_late/pallas_call | solution.py:854
  538.2 6.9 %all-gather.24.cloned.1.call-done = f32[3072,128]{1,0:T(8,128)} async-done(((f32[96,128]{1,0:T(8,128)}), f32[3072,128]{1,0:T(8,128)}) %all-gather.24.cloned.1.call-update) | async-done | bytes 1572880 | tf_op jit(solution)/shard_map/all_gather | solution.py:1085
  (565 shorter events, 194.4 us)
Async XLA Ops:
  7.2 114.4 %all-gather.10.cloned.1.call-start = ((), (), s32[]{:S(2)}) async-start(), calls=%async_computation | async-start | bytes 28532736 | tf_op jit(solution)/shard_map/all_gather | solution.py:939
  11.3 176.3 %all-gather.12.cloned.1.call-start = ((), (), s32[]{:S(2)}) async-start(), calls=%async_computation.1 | async-start | bytes 1966080 | tf_op jit(solution)/shard_map/all_gather | solution.py:941
  17.3 20.6 %collective-permute-start.2 = (bf16[256,192]{0,1:T(8,128)(2,1)S(1)}, bf16[256,192]{0,1:T(8,128)(2,1)S(1)}, u32[]{:S(2)}, u32[]{:S(2)}) collective-permute-start(bf16[256,192]{0,1:T(8,128)(2,1)S(1)} %get-tuple-element.283), channel_id=1, source_target_pairs={{0,3},{1,2},{2,1},{3,0},{4,7},{5,6},{6,5},{7,4},{8,11},{9,10},{10,... | collective-permute-start | bytes 294920 | tf_op jit(solution)/shard_map/ppermute | solution.py:874
  19.8 18.0 %collective-permute-start.1 = (bf16[256,192]{0,1:T(8,128)(2,1)S(1)}, bf16[256,192]{0,1:T(8,128)(2,1)S(1)}, u32[]{:S(2)}, u32[]{:S(2)}) collective-permute-start(bf16[256,192]{0,1:T(8,128)(2,1)S(1)} %get-tuple-element.284), channel_id=1, source_target_pairs={{0,2},{1,3},{2,0},{3,1},{4,6},{5,7},{6,4},{7,5},{8,10},{9,11},{10,... | collective-permute-start | bytes 294920 | tf_op jit(solution)/shard_map/ppermute | solution.py:874
  21.2 208.5 %all-gather.14.cloned.1.call-start = ((), (), s32[]{:S(2)}) async-start(), calls=%async_computation.2 | async-start | bytes 1966080 | tf_op jit(solution)/shard_map/all_gather | solution.py:990
  39.8 23.6 %collective-permute-start.12 = (bf16[256,768]{1,0:T(8,128)(2,1)S(1)}, bf16[256,768]{1,0:T(8,128)(2,1)}, u32[]{:S(2)}, u32[]{:S(2)}) collective-permute-start(bf16[256,768]{1,0:T(8,128)(2,1)S(1)} %multiply_convert_fusion.refs_0_), channel_id=1, source_target_pairs={{0,3},{1,2},{2,1},{3,0},{4,7},{5,6},{6,5},{7,4},{8,11},{9,10},{10,... | collective-permute-start | bytes 1179656 | tf_op jit(solution)/shard_map/ppermute | solution.py:874
  41.7 21.7 %collective-permute-start.11 = (bf16[256,768]{1,0:T(8,128)(2,1)S(1)}, bf16[256,768]{1,0:T(8,128)(2,1)}, u32[]{:S(2)}, u32[]{:S(2)}) collective-permute-start(bf16[256,768]{1,0:T(8,128)(2,1)S(1)} %multiply_convert_fusion.refs_0_), channel_id=1, source_target_pairs={{0,2},{1,3},{2,0},{3,1},{4,6},{5,7},{6,4},{7,5},{8,10},{9,11},{10,... | collective-permute-start | bytes 1179656 | tf_op jit(solution)/shard_map/ppermute | solution.py:874
  42.4 23.5 %collective-permute-start.10 = (bf16[256,768]{1,0:T(8,128)(2,1)S(1)}, bf16[256,768]{1,0:T(8,128)(2,1)}, u32[]{:S(2)}, u32[]{:S(2)}) collective-permute-start(bf16[256,768]{1,0:T(8,128)(2,1)S(1)} %multiply_convert_fusion.refs_0_), channel_id=1, source_target_pairs={{0,1},{1,0},{2,3},{3,2},{4,5},{5,4},{6,7},{7,6},{8,9},{9,8},{10,11... | collective-permute-start | bytes 1179656 | tf_op jit(solution)/shard_map/ppermute | solution.py:874
  139.7 15.2 %collective-permute-start.13 = (bf16[192,256]{1,0:T(8,128)(2,1)}, bf16[192,256]{1,0:T(8,128)(2,1)S(1)}, u32[]{:S(2)}, u32[]{:S(2)}) collective-permute-start(bf16[192,256]{1,0:T(8,128)(2,1)} %get-tuple-element.147.refs_4_), channel_id=1, source_target_pairs={{0,1},{1,0},{2,3},{3,2},{4,5},{5,4},{6,7},{7,6},{8,9},{9,8},{10,11... | collective-permute-start | bytes 294920 | tf_op jit(solution)/shard_map/ppermute | solution.py:874
  166.2 19.4 %collective-permute-start.18 = (bf16[256,768]{1,0:T(8,128)(2,1)}, bf16[256,768]{1,0:T(8,128)(2,1)S(1)}, u32[]{:S(2)}, u32[]{:S(2)}) collective-permute-start(bf16[256,768]{1,0:T(8,128)(2,1)} %get-tuple-element.155.a0.refs_11_), channel_id=1, source_target_pairs={{0,3},{1,2},{2,1},{3,0},{4,7},{5,6},{6,5},{7,4},{8,11},{9,10},{10,... | collective-permute-start | bytes 1179656 | tf_op jit(solution)/shard_map/ppermute | solution.py:874
  168.6 17.0 %collective-permute-start.17 = (bf16[256,768]{1,0:T(8,128)(2,1)}, bf16[256,768]{1,0:T(8,128)(2,1)S(1)}, u32[]{:S(2)}, u32[]{:S(2)}) collective-permute-start(bf16[256,768]{1,0:T(8,128)(2,1)} %get-tuple-element.155.a0.refs_11_), channel_id=1, source_target_pairs={{0,2},{1,3},{2,0},{3,1},{4,6},{5,7},{6,4},{7,5},{8,10},{9,11},{10,... | collective-permute-start | bytes 1179656 | tf_op jit(solution)/shard_map/ppermute | solution.py:874
  168.6 17.4 %collective-permute-start.16 = (bf16[256,768]{1,0:T(8,128)(2,1)}, bf16[256,768]{1,0:T(8,128)(2,1)S(1)}, u32[]{:S(2)}, u32[]{:S(2)}) collective-permute-start(bf16[256,768]{1,0:T(8,128)(2,1)} %get-tuple-element.155.a0.refs_11_), channel_id=1, source_target_pairs={{0,1},{1,0},{2,3},{3,2},{4,5},{5,4},{6,7},{7,6},{8,9},{9,8},{10,11... | collective-permute-start | bytes 1179656 | tf_op jit(solution)/shard_map/ppermute | solution.py:874
  186.8 104.4 %all-gather.16.cloned.1.call-start = ((), (), s32[]{:S(2)}) async-start(), calls=%async_computation.3 | async-start | bytes 3932160 | tf_op jit(solution)/shard_map/all_gather | solution.py:1033
  243.4 86.6 %all-gather.20.cloned.1.call-start = ((), (), s32[]{:S(2)}) async-start(), calls=%async_computation.5 | async-start | bytes 1966080 | tf_op jit(solution)/shard_map/all_gather | solution.py:1040
  268.9 91.2 %all-gather.22.cloned.1.call-start = ((), (), s32[]{:S(2)}) async-start(), calls=%async_computation.6 | async-start | bytes 1966080 | tf_op jit(solution)/shard_map/all_gather | solution.py:1035
  287.2 17.2 %collective-permute-start.28 = (bf16[576,256]{1,0:T(8,128)(2,1)}, bf16[576,256]{1,0:T(8,128)(2,1)S(1)}, u32[]{:S(2)}, u32[]{:S(2)}) collective-permute-start(bf16[576,256]{1,0:T(8,128)(2,1)} %get-tuple-element.176.refs_8_), channel_id=1, source_target_pairs={{0,1},{1,0},{2,3},{3,2},{4,5},{5,4},{6,7},{7,6},{8,9},{9,8},{10,11... | collective-permute-start | bytes 884744 | tf_op jit(solution)/shard_map/ppermute | solution.py:874
  287.2 17.2 %collective-permute-start.29 = (bf16[576,256]{1,0:T(8,128)(2,1)}, bf16[576,256]{1,0:T(8,128)(2,1)S(1)}, u32[]{:S(2)}, u32[]{:S(2)}) collective-permute-start(bf16[576,256]{1,0:T(8,128)(2,1)} %get-tuple-element.177.refs_9_), channel_id=1, source_target_pairs={{0,2},{1,3},{2,0},{3,1},{4,6},{5,7},{6,4},{7,5},{8,10},{9,11},{10,... | collective-permute-start | bytes 884744 | tf_op jit(solution)/shard_map/ppermute | solution.py:874
  289.1 15.3 %collective-permute-start.30 = (bf16[576,256]{1,0:T(8,128)(2,1)}, bf16[576,256]{1,0:T(8,128)(2,1)S(1)}, u32[]{:S(2)}, u32[]{:S(2)}) collective-permute-start(bf16[576,256]{1,0:T(8,128)(2,1)} %get-tuple-element.178.refs_10_), channel_id=1, source_target_pairs={{0,3},{1,2},{2,1},{3,0},{4,7},{5,6},{6,5},{7,4},{8,11},{9,10},{10,... | collective-permute-start | bytes 884744 | tf_op jit(solution)/shard_map/ppermute | solution.py:874
  309.8 78.4 %all-gather.18.cloned.1.call-start = ((), (), s32[]{:S(2)}) async-start(), calls=%async_computation.4 | async-start | bytes 1966080 | tf_op jit(solution)/shard_map/all_gather | solution.py:1040
  336.9 208.2 %all-gather.24.cloned.1.call-start = ((), (), s32[]{:S(2)}) async-start(), calls=%async_computation.7 | async-start | bytes 1622016 | tf_op jit(solution)/shard_map/all_gather | solution.py:1085
  356.1 17.3 %collective-permute-start.34 = (bf16[576,256]{1,0:T(8,128)(2,1)}, bf16[576,256]{1,0:T(8,128)(2,1)S(1)}, u32[]{:S(2)}, u32[]{:S(2)}) collective-permute-start(bf16[576,256]{1,0:T(8,128)(2,1)} %get-tuple-element.196.refs_8_), channel_id=1, source_target_pairs={{0,1},{1,0},{2,3},{3,2},{4,5},{5,4},{6,7},{7,6},{8,9},{9,8},{10,11... | collective-permute-start | bytes 884744 | tf_op jit(solution)/shard_map/ppermute | solution.py:874
  356.1 17.2 %collective-permute-start.35 = (bf16[576,256]{1,0:T(8,128)(2,1)}, bf16[576,256]{1,0:T(8,128)(2,1)S(1)}, u32[]{:S(2)}, u32[]{:S(2)}) collective-permute-start(bf16[576,256]{1,0:T(8,128)(2,1)} %get-tuple-element.197.refs_9_), channel_id=1, source_target_pairs={{0,2},{1,3},{2,0},{3,1},{4,6},{5,7},{6,4},{7,5},{8,10},{9,11},{10,... | collective-permute-start | bytes 884744 | tf_op jit(solution)/shard_map/ppermute | solution.py:874
  358.3 16.1 %collective-permute-start.36 = (bf16[576,256]{1,0:T(8,128)(2,1)}, bf16[576,256]{1,0:T(8,128)(2,1)S(1)}, u32[]{:S(2)}, u32[]{:S(2)}) collective-permute-start(bf16[576,256]{1,0:T(8,128)(2,1)} %get-tuple-element.198.refs_10_), channel_id=1, source_target_pairs={{0,3},{1,2},{2,1},{3,0},{4,7},{5,6},{6,5},{7,4},{8,11},{9,10},{10,... | collective-permute-start | bytes 884744 | tf_op jit(solution)/shard_map/ppermute | solution.py:874
  398.8 17.5 %collective-permute-start.40 = (bf16[16,960,128]{2,1,0:T(8,128)(2,1)}, bf16[16,960,128]{2,1,0:T(8,128)(2,1)S(1)}, u32[]{:S(2)}, u32[]{:S(2)}) collective-permute-start(bf16[16,960,128]{2,1,0:T(8,128)(2,1)} %get-tuple-element.268), channel_id=1, source_target_pairs={{0,4},{4,0},{8,12},{12,8},{16,20},{20,16},{24,28},{28,24},{32,36},... | collective-permute-start | bytes 11796488 | tf_op jit(solution)/shard_map/ppermute | solution.py:874
  421.6 24.0 %collective-permute-start.42 = (bf16[4,480,128]{2,1,0:T(8,128)(2,1)S(1)}, bf16[4,480,128]{2,1,0:T(8,128)(2,1)S(1)}, u32[]{:S(2)}, u32[]{:S(2)}) collective-permute-start(bf16[4,480,128]{2,1,0:T(8,128)(2,1)S(1)} %get-tuple-element.217), channel_id=1, source_target_pairs={{0,64},{4,68},{8,72},{12,76},{16,80},{20,84},{24,88},{28,92},{32,9... | collective-permute-start | bytes 1474568 | tf_op jit(solution)/shard_map/ppermute | solution.py:874
  424.1 23.5 %collective-permute-start.43 = (bf16[4,480,128]{2,1,0:T(8,128)(2,1)S(1)}, bf16[4,480,128]{2,1,0:T(8,128)(2,1)S(1)}, u32[]{:S(2)}, u32[]{:S(2)}) collective-permute-start(bf16[4,480,128]{2,1,0:T(8,128)(2,1)S(1)} %get-tuple-element.218), channel_id=1, source_target_pairs={{0,96},{4,100},{8,104},{12,108},{16,112},{20,116},{24,120},{28,124... | collective-permute-start | bytes 1474568 | tf_op jit(solution)/shard_map/ppermute | solution.py:874
  424.6 23.0 %collective-permute-start.44 = (bf16[4,480,128]{2,1,0:T(8,128)(2,1)S(1)}, bf16[4,480,128]{2,1,0:T(8,128)(2,1)S(1)}, u32[]{:S(2)}, u32[]{:S(2)}) collective-permute-start(bf16[4,480,128]{2,1,0:T(8,128)(2,1)S(1)} %get-tuple-element.220), channel_id=1, source_target_pairs={{0,8},{4,12},{8,0},{12,4},{16,24},{20,28},{24,16},{28,20},{32,40},... | collective-permute-start | bytes 1474568 | tf_op jit(solution)/shard_map/ppermute | solution.py:874
  424.6 23.0 %collective-permute-start.45 = (bf16[4,480,128]{2,1,0:T(8,128)(2,1)S(1)}, bf16[4,480,128]{2,1,0:T(8,128)(2,1)S(1)}, u32[]{:S(2)}, u32[]{:S(2)}) collective-permute-start(bf16[4,480,128]{2,1,0:T(8,128)(2,1)S(1)} %get-tuple-element.221), channel_id=1, source_target_pairs={{0,16},{4,20},{8,24},{12,28},{16,0},{20,4},{24,8},{28,12},{32,48},... | collective-permute-start | bytes 1474568 | tf_op jit(solution)/shard_map/ppermute | solution.py:874
  433.2 23.1 %collective-permute-start.46 = (bf16[4,480,128]{2,1,0:T(8,128)(2,1)S(1)}, bf16[4,480,128]{2,1,0:T(8,128)(2,1)S(1)}, u32[]{:S(2)}, u32[]{:S(2)}) collective-permute-start(bf16[4,480,128]{2,1,0:T(8,128)(2,1)S(1)} %get-tuple-element.222), channel_id=1, source_target_pairs={{0,24},{4,28},{8,16},{12,20},{16,8},{20,12},{24,0},{28,4},{32,56},... | collective-permute-start | bytes 1474568 | tf_op jit(solution)/shard_map/ppermute | solution.py:874
  482.1 16.8 %collective-permute-start.59 = (f32[8,128]{1,0:T(8,128)S(1)}, f32[8,128]{1,0:T(8,128)S(1)}, u32[]{:S(2)}, u32[]{:S(2)}) collective-permute-start(f32[8,128]{1,0:T(8,128)S(1)} %add.348), channel_id=1, source_target_pairs={{0,24},{4,28},{8,16},{12,20},{16,8},{20,12},{24,0},{28,4},{32,56},... | collective-permute-start | bytes 12296 | tf_op jit(solution)/shard_map/ppermute | solution.py:874
  482.9 16.0 %collective-permute-start.58 = (f32[8,128]{1,0:T(8,128)S(1)}, f32[8,128]{1,0:T(8,128)S(1)}, u32[]{:S(2)}, u32[]{:S(2)}) collective-permute-start(f32[8,128]{1,0:T(8,128)S(1)} %add.348), channel_id=1, source_target_pairs={{0,16},{4,20},{8,24},{12,28},{16,0},{20,4},{24,8},{28,12},{32,48},... | collective-permute-start | bytes 12296 | tf_op jit(solution)/shard_map/ppermute | solution.py:874
  482.9 16.0 %collective-permute-start.57 = (f32[8,128]{1,0:T(8,128)S(1)}, f32[8,128]{1,0:T(8,128)}, u32[]{:S(2)}, u32[]{:S(2)}) collective-permute-start(f32[8,128]{1,0:T(8,128)S(1)} %add.348), channel_id=1, source_target_pairs={{0,8},{4,12},{8,0},{12,4},{16,24},{20,28},{24,16},{28,20},{32,40},... | collective-permute-start | bytes 12296 | tf_op jit(solution)/shard_map/ppermute | solution.py:874
  (135 other events, 1737.0 us)
Sparse Core Ops, SparseCore 0:
  11.6 109.9 all-gather.9
  123.2 28.4 all-gather.11
  186.9 31.2 all-gather.13
  243.5 46.5 all-gather.15
  291.7 27.5 all-gather.19
  320.8 27.5 all-gather.21
  350.0 38.1 all-gather.17
  503.2 41.8 all-gather.23
